TPU v7x, 256 devices: a whole 4x4x8 slice. The times are simulated.
256 devices in a mesh: seq: 32 (over y, z), mp: 8 (over x, core).
Axes of the slice: x: 4, y: 4, z: 8, core: 2. Of those that a mesh axis runs over, the one named last changes fastest.
Arguments:
- queries: bfloat16 [512, 8192], P('seq', 'mp'), may hold values from -64 to 64
- prefix_keys: bfloat16 [131072, 1024], P('seq', 'mp'), may hold values from -24 to 24
- prefix_values: bfloat16 [131072, 1024], P('seq', 'mp'), may hold values from -6 to 6
- resp_keys: bfloat16 [512, 1024], P('seq', 'mp'), may hold values from -28 to 28
- resp_values: bfloat16 [512, 1024], P('seq', 'mp'), may hold values from -6 to 6
- segment_ids: int32 [512], replicated, may hold values from 0 to 3, never falling along the last dimension, each value on 1 to 256 neighbouring positions
- out_weight: bfloat16 [8192, 8192], P('mp', 'seq'), may hold values from -0.0625 to 0.0625
Outputs:
- scored: bfloat16 [512, 8192], P('mp', 'seq')
Inputs may be any that keep to these rules, and one draw needn't show every extreme that they name: `segment_ids`: never falling; each of the 4 responses holds 1 to 256 tokens, one exactly 256.
All inputs are finite; a program needn't handle non-finite values.
Results may differ from a plain program's by a relative error of at most 0.013.
Values may be sent and summed in bfloat16 or wider, within the bound.
No kernel may reach another device: no remote copies, remote signals or barrier semaphores. Data moves between devices by JAX's collectives and lax.ppermute only.
A program may use at most 64 MiB of HBM per device.

v0:
```python
import jax
import jax.numpy as jnp
from jax import lax
from jax.experimental import pallas as pl
from jax.experimental.pallas import tpu as pltpu
from jax.sharding import PartitionSpec as P

HD = 128
SCALE2 = HD**-0.5 * 1.4426950408889634
LOWEST = 2.0**-60
HIGHEST = 2.0**100
SMALL = 2.0**-20
ONES = 16
DEPTH = 4
f32 = jnp.float32
bf16 = jnp.bfloat16


def split3(x):
    high = x.astype(bf16).astype(f32)
    rest = x - high
    middle = rest.astype(bf16).astype(f32)
    return high, middle, rest - middle


def prepare_kernel(v_ref, rv_ref, vt_ref, rvt_ref, fact_ref):
    v = v_ref[...]
    vt_ref[:HD, :] = v.T
    vt_ref[HD:, :] = jnp.ones((ONES, v.shape[0]), bf16)
    rvt_ref[:HD, :] = rv_ref[...].T
    rvt_ref[HD:, :] = jnp.ones((ONES, rv_ref.shape[0]), bf16)
    fact_ref[0, 0] = jnp.maximum(
        jnp.max(jnp.abs(v.astype(f32))), jnp.max(jnp.abs(rv_ref[...].astype(f32)))
    )


def prepare(values, own_values):
    vmem = pl.BlockSpec(memory_space=pltpu.VMEM)
    return pl.pallas_call(
        prepare_kernel,
        out_shape=(
            jax.ShapeDtypeStruct((HD + ONES, values.shape[0]), bf16),
            jax.ShapeDtypeStruct((HD + ONES, own_values.shape[0]), bf16),
            jax.ShapeDtypeStruct((1, 1), f32),
        ),
        out_specs=(vmem, vmem, pl.BlockSpec(memory_space=pltpu.SMEM)),
        name="prepare",
    )(values, own_values)


def attend_kernel(
    group, stack, key_block, q_ref, k_ref, vt_ref, rk_ref, rvt_ref, bias_ref, fact_ref, out_ref,
    logs_ref,
):
    tokens = q_ref.shape[0]
    keys = k_ref.shape[0]

    def scores(keys_block, q):
        return (
            lax.dot_general(
                keys_block, q, (((1,), (1,)), ((), ())), preferred_element_type=f32
            )
            * SCALE2
        )

    def product(columns, weights):
        return jnp.dot(columns, weights.astype(bf16), preferred_element_type=f32)

    def result_of(total):
        return (total[:HD] / total[HD : HD + 1]).T.astype(bf16)

    def logs_rows(rows):
        pieces = split3(jnp.concatenate(rows, axis=0))
        out_ref[group * tokens :, :] = jnp.concatenate(
            pieces + (jnp.zeros((group, tokens), f32),), axis=0
        ).astype(bf16)

    lowest, highest = [], []
    logs = []
    bias = jnp.concatenate([bias_ref[...]] * stack, axis=1)
    for first in range(0, group, stack):
        q = jnp.concatenate(
            [q_ref[:, head * HD : (head + 1) * HD] for head in range(first, first + stack)], axis=0
        )
        total = product(rvt_ref[...], jnp.exp2(scores(rk_ref[...], q) + bias))
        now = scores(k_ref[:key_block, :], q)
        for start in range(0, keys, key_block):
            later = start + key_block
            if later < keys:
                following = scores(k_ref[later : later + key_block, :], q)
            total += product(vt_ref[:, start:later], jnp.exp2(now))
            if later < keys:
                now = following
        sums = total[HD : HD + 1]
        lowest.append(jnp.min(sums))
        highest.append(jnp.max(sums))
        log = jnp.log2(sums)
        for at in range(stack):
            lanes = slice(at * tokens, (at + 1) * tokens)
            logs.append(log[:, lanes])
            head = first + at
            out_ref[head * tokens : (head + 1) * tokens, :] = result_of(total[:, lanes])
    logs_rows(logs)
    inside = fact_ref[0, 0] >= SMALL
    for low, high in zip(lowest, highest):
        inside = inside & (low >= LOWEST) & (high <= HIGHEST)

    @pl.when(jnp.logical_not(inside))
    def _():
        @pl.loop(0, group)
        def _(head):
            q = q_ref[:, pl.ds(pl.multiple_of(head * HD, HD), HD)]
            mine = scores(rk_ref[...], q) + bias_ref[...]
            rest = scores(k_ref[...], q)
            top = jnp.maximum(
                jnp.max(mine, axis=0, keepdims=True), jnp.max(rest, axis=0, keepdims=True)
            )
            total = product(rvt_ref[...], jnp.exp2(mine - top))
            total += product(vt_ref[...], jnp.exp2(rest - top))
            logs_ref[pl.ds(head, 1), :] = jnp.log2(total[HD : HD + 1]) + top
            out_ref[pl.ds(pl.multiple_of(head * tokens, tokens), tokens), :] = result_of(total)

        logs_rows([logs_ref[...]])


def attend(queries, keys, columns, own_keys, own_columns, bias, fact):
    tokens, width = queries.shape
    group = width // HD
    vmem = pl.BlockSpec(memory_space=pltpu.VMEM)
    return pl.pallas_call(
        lambda *refs: attend_kernel(group, min(4, group), 512, *refs),
        out_shape=jax.ShapeDtypeStruct((group * (tokens + DEPTH), HD), bf16),
        in_specs=[vmem] * 6 + [pl.BlockSpec(memory_space=pltpu.SMEM)],
        out_specs=vmem,
        scratch_shapes=[pltpu.VMEM((group, tokens), f32)],
        compiler_params=pltpu.CompilerParams(vmem_limit_bytes=20 << 20),
        name="attend",
    )(queries, keys, columns, own_keys, own_columns, bias, fact)


def join_kernel(group, halves, *refs):
    own_refs, part_refs, out_ref = refs[:halves], refs[halves:-1], refs[-1]
    owners = out_ref.shape[0]
    tokens = part_refs[0].shape[0] // group - DEPTH
    few = group // halves

    def log_of(ref, heads):
        pieces = ref[heads * tokens :, :].astype(f32)
        return sum(pieces[at * heads : (at + 1) * heads] for at in range(3))

    def part_of(at, head):
        ref = part_refs[at - 1] if at else own_refs[head // few]
        row = head * tokens if at else head % few * tokens
        return ref[row : row + tokens, :].astype(f32)

    logs = [jnp.concatenate([log_of(ref, few) for ref in own_refs], axis=0)]
    logs += [log_of(ref, group) for ref in part_refs]
    top = logs[0]
    for log in logs[1:]:
        top = jnp.maximum(top, log)
    shares = [jnp.exp2(log - top) for log in logs]
    whole = sum(shares)
    shares = [share / whole for share in shares]
    rows = list(split3(top + jnp.log2(whole))) + shares
    rows.append(jnp.zeros((HD - group * len(rows), tokens), f32))
    turned = jnp.concatenate(rows, axis=0).T
    split = tokens // owners
    for head in range(group):
        total = None
        for at in range(len(shares)):
            lane = (3 + at) * group + head
            term = part_of(at, head) * turned[:, lane : lane + 1]
            total = term if total is None else total + term
        out_ref[:, head * split : (head + 1) * split, :] = total.astype(bf16).reshape(
            owners, split, HD
        )
    out_ref[:, group * split :, :] = turned.astype(bf16).reshape(owners, split, HD)


def join(own, parts, group, owners):
    tokens = parts[0].shape[0] // group - DEPTH
    return pl.pallas_call(
        lambda *refs: join_kernel(group, len(own), *refs),
        out_shape=jax.ShapeDtypeStruct((owners, (group + 1) * (tokens // owners), HD), bf16),
        compiler_params=pltpu.CompilerParams(vmem_limit_bytes=20 << 20),
        name="join",
    )(*own, *parts)


def combine_kernel(group, parts_ref, out_ref):
    copies, tokens, _ = out_ref.shape
    pieces = parts_ref[:, group * tokens :, :].astype(f32)
    logs = sum(pieces[:, :, piece * group : (piece + 1) * group] for piece in range(3))
    share = jnp.exp2(logs - jnp.max(logs, axis=0, keepdims=True))
    share = share / jnp.sum(share, axis=0, keepdims=True)
    for head in range(group):
        part = parts_ref[:, head * tokens : (head + 1) * tokens, :].astype(f32)
        result = jnp.sum(part * share[:, :, head : head + 1], axis=0).astype(bf16)
        out_ref[:, :, head * HD : (head + 1) * HD] = jnp.broadcast_to(
            result[None], (copies, tokens, HD)
        )


def combine(parts, group):
    owners, height, _ = parts.shape
    return pl.pallas_call(
        lambda *refs: combine_kernel(group, *refs),
        out_shape=jax.ShapeDtypeStruct((owners, height // (group + 1), group * HD), bf16),
        compiler_params=pltpu.CompilerParams(vmem_limit_bytes=20 << 20),
        name="combine",
    )(parts)


Y, Z = 4, 8


def on_device(queries, prefix_keys, prefix_values, resp_keys, resp_values, segment_ids, out_weight):
    ways = lax.axis_size("mp")
    tokens, width = queries.shape
    group = width // HD
    rows = segment_ids.shape[0]
    quarter = rows // Y
    along_z = [[y * Z + z for z in range(Z)] for y in range(Y)]
    place = lax.axis_index("seq")

    def across_z(array):
        return lax.all_to_all(array, "seq", 0, 0, axis_index_groups=along_z, tiled=True)

    def along_y(array, step):
        pairs = [(y * Z + z, (y + step) % Y * Z + z) for y in range(Y) for z in range(Z)]
        return lax.ppermute(array, "seq", pairs)

    mine = across_z(jnp.broadcast_to(queries[None], (Z,) + queries.shape)).reshape(quarter, width)

    columns, own_columns, fact = prepare(prefix_values, resp_values)
    first = place * tokens
    own_segments = lax.dynamic_slice_in_dim(segment_ids, first, tokens)
    own_rows = first + jnp.arange(tokens, dtype=jnp.int32)
    allowed = (own_segments[:, None] == segment_ids[None, :]) & (
        own_rows[:, None] <= jnp.arange(rows, dtype=jnp.int32)[None, :]
    )
    bias = jnp.where(allowed, f32(0), f32(-1e30))

    def bias_for(step):
        owner = (place // Z + Y - step) % Y
        return lax.dynamic_slice_in_dim(bias, owner * quarter, quarter, 1)

    def part_for(array, block):
        return attend(array, prefix_keys, columns, resp_keys, own_columns, block, fact)

    blocks = [bias_for(step) for step in range(Y)]
    mine, columns, own_columns, fact, *blocks = lax.optimization_barrier(
        (mine, columns, own_columns, fact, *blocks)
    )
    arrivals = {step: along_y(mine, step) for step in (1, 3, 2)}
    own = [part_for(mine[:, : width // 2], blocks[0])]
    *blocks, own[0] = lax.optimization_barrier((*blocks, own[0]))
    parts = [along_y(part_for(arrivals[step], blocks[step]), -step) for step in (1, 2, 3)]
    own.append(part_for(mine[:, width // 2 :], blocks[0]))

    joined = across_z(join(own, parts, group, Z))
    heads = across_z(combine(joined, group)).reshape(quarter, width)
    pieces = [heads] + [along_y(heads, step) for step in (1, 3, 2)]
    scored = [
        jnp.dot(piece, out_weight, preferred_element_type=f32).astype(bf16) for piece in pieces
    ]
    order = (0, 1, 3, 2)
    whole = jnp.zeros((rows, out_weight.shape[1]), bf16)
    for step, piece in zip(order, scored):
        owner = (place // Z + Y - step) % Y
        whole = lax.dynamic_update_slice_in_dim(whole, piece, owner * quarter, 0)
    scored = whole.reshape(ways, rows // ways, -1)
    scored = lax.all_to_all(scored, "mp", 0, 0, tiled=True)
    return jnp.sum(scored.astype(f32), axis=0).astype(bf16)


def solution(mesh):
    in_specs = (
        P("seq", "mp"),
        P("seq", "mp"),
        P("seq", "mp"),
        P("seq", "mp"),
        P("seq", "mp"),
        P(),
        P("mp", "seq"),
    )
    return jax.shard_map(
        on_device, mesh=mesh, in_specs=in_specs, out_specs=P("mp", "seq"), check_vma=False
    )
```

profile of v0, /device:TPU:1, one launch (start us, length us, event | category | flops | bytes accessed | tf_op | source)
XLA Modules:
  0.0 158.2 jit_solution(7764786227177640212)
XLA Ops:
  0.0 0.0 copy-start
  0.0 1.5 broadcast_in_dim.22
  1.6 0.0 copy-start.2
  1.6 9.1 %all-to-all-start = ((bf16[8,16,1024]{2,1,0:T(8,128)(2,1)}), bf16[8,16,1024]{2,1,0:T(8,128)(2,1)S(1)}, u32[]{:S(2)}, u32[]{:S(2)}) async-start(bf16[8,16,1024]{2,1,0:T(8,128)(2,1)} %broadcast_in_dim.22), calls=%async_computation | async-start | bytes 524288 | tf_op jit(solution)/shard_map/all_to_all | solution.py:227
  10.7 0.8 dynamic_slice.15
  11.5 2.7 %prepare.1 = (bf16[144,4096]{1,0:T(8,128)(2,1)}, bf16[144,16]{1,0:T(8,128)(2,1)}, f32[1,1]{1,0:T(1,128)}) custom-call(bf16[4096,128]{1,0:T(8,128)(2,1)} %v_ref.1, bf16[16,128]{1,0:T(8,128)(2,1)} %rv_ref.1), custom_call_target="tpu_custom_call" | custom-call | tf_op jit(solution)/shard_map/prepare/pallas_call | solution.py:39
  14.1 0.0 copy-done.5
  14.1 0.1 fusion.5
  14.2 6.8 %all-to-all-done = bf16[8,16,1024]{2,1,0:T(8,128)(2,1)S(1)} async-done(((bf16[8,16,1024]{2,1,0:T(8,128)(2,1)}), bf16[8,16,1024]{2,1,0:T(8,128)(2,1)S(1)}, u32[]{:S(2)}, u32[]{:S(2)}) %all-to-all-start) | async-done | bytes 262176 | tf_op jit(solution)/shard_map/all_to_all | solution.py:227
  21.1 2.7 %collective-permute-start.4 = (bf16[128,1024]{1,0:T(8,128)(2,1)S(1)}, bf16[128,1024]{1,0:T(8,128)(2,1)S(1)}, u32[]{:S(2)}, u32[]{:S(2)}) collective-permute-start(bf16[128,1024]{1,0:T(8,128)(2,1)S(1)} %bitcast.15), channel_id=1, source_target_pairs={{0,192},{8,200},{16,208},{24,216},{32,224},{40,232},{48,240},{56,2... | collective-permute-start | bytes 786440 | tf_op jit(solution)/shard_map/ppermute | solution.py:231
  23.8 0.3 collective-permute-start.2
  24.2 0.7 collective-permute-start
  24.9 0.0 copy-done.2
  24.9 0.0 copy-done.4
  24.9 0.0 copy-start.1
  24.9 1.3 copy-done.1
  26.2 0.8 copy-done.3
  26.9 2.7 %attend.5.refs_0_ = bf16[528,128]{1,0:T(8,128)(2,1)S(1)} custom-call(bf16[128,512]{1,0:T(8,128)(2,1)S(1)} %get-tuple-element.38.refs_0_, bf16[4096,128]{1,0:T(8,128)(2,1)S(1)} %copy-done.2, bf16[144,4096]{1,0:T(8,128)(2,1)S(1)} %copy-done.1, bf16[16,128]{1,0:T(8,128)(2,1)S(1)} %copy-done.4, bf16[144,16]{1,0:T(8,128)(2,1)S(1)} %copy-done.3, ...), custom_call_target="tpu_custom_call" | custom-call | tf_op jit(solution)/shard_map/attend/pallas_call | solution.py:130
  29.7 0.2 collective-permute-done.4.refs_0_
  29.8 18.0 %attend.9 = bf16[1056,128]{1,0:T(8,128)(2,1)S(1)} custom-call(bf16[128,1024]{1,0:T(8,128)(2,1)S(1)} %collective-permute-done.4.refs_0_, bf16[4096,128]{1,0:T(8,128)(2,1)S(1)} %copy-done.2, bf16[144,4096]{1,0:T(8,128)(2,1)S(1)} %copy-done.1, bf16[16,128]{1,0:T(8,128)(2,1)S(1)} %copy-done.4, bf16[144,16]{1,0:T(8,128)(2,1)S(1)} %copy-done.3, ...), custom_call_target="tpu_custom_call" | custom-call | tf_op jit(solution)/shard_map/attend/pallas_call | solution.py:130
  47.8 8.4 %collective-permute-start.5 = (bf16[1056,128]{1,0:T(8,128)(2,1)S(1)}, bf16[1056,128]{1,0:T(8,128)(2,1)S(1)}, u32[]{:S(2)}, u32[]{:S(2)}) collective-permute-start(bf16[1056,128]{1,0:T(8,128)(2,1)S(1)} %attend.9), channel_id=1, source_target_pairs={{0,64},{8,72},{16,80},{24,88},{32,96},{40,104},{48,112},{56,120},{... | collective-permute-start | bytes 811016 | tf_op jit(solution)/shard_map/ppermute | solution.py:231
  56.2 0.0 collective-permute-done.2.refs_0_
  56.2 18.0 %attend.8 = bf16[1056,128]{1,0:T(8,128)(2,1)S(1)} custom-call(bf16[128,1024]{1,0:T(8,128)(2,1)S(1)} %collective-permute-done.2.refs_0_, bf16[4096,128]{1,0:T(8,128)(2,1)S(1)} %copy-done.2, bf16[144,4096]{1,0:T(8,128)(2,1)S(1)} %copy-done.1, bf16[16,128]{1,0:T(8,128)(2,1)S(1)} %copy-done.4, bf16[144,16]{1,0:T(8,128)(2,1)S(1)} %copy-done.3, ...), custom_call_target="tpu_custom_call" | custom-call | tf_op jit(solution)/shard_map/attend/pallas_call | solution.py:130
  74.2 0.1 collective-permute-start.3
  74.3 0.0 collective-permute-done.refs_0_
  74.3 18.0 %attend.7 = bf16[1056,128]{1,0:T(8,128)(2,1)S(1)} custom-call(bf16[128,1024]{1,0:T(8,128)(2,1)S(1)} %collective-permute-done.refs_0_, bf16[4096,128]{1,0:T(8,128)(2,1)S(1)} %copy-done.2, bf16[144,4096]{1,0:T(8,128)(2,1)S(1)} %copy-done.1, bf16[16,128]{1,0:T(8,128)(2,1)S(1)} %copy-done.4, bf16[144,16]{1,0:T(8,128)(2,1)S(1)} %copy-done.3, ...), custom_call_target="tpu_custom_call" | custom-call | tf_op jit(solution)/shard_map/attend/pallas_call | solution.py:130
  92.3 2.7 %collective-permute-start.1 = (bf16[1056,128]{1,0:T(8,128)(2,1)S(1)}, bf16[1056,128]{1,0:T(8,128)(2,1)S(1)}, u32[]{:S(2)}, u32[]{:S(2)}) collective-permute-start(bf16[1056,128]{1,0:T(8,128)(2,1)S(1)} %attend.7), channel_id=1, source_target_pairs={{0,192},{8,200},{16,208},{24,216},{32,224},{40,232},{48,240},{56,2... | collective-permute-start | bytes 811016 | tf_op jit(solution)/shard_map/ppermute | solution.py:231
  95.0 2.7 %attend.6.refs_1_ = bf16[528,128]{1,0:T(8,128)(2,1)S(1)} custom-call(bf16[128,512]{1,0:T(8,128)(2,1)S(1)} %get-tuple-element.37.refs_0_, bf16[4096,128]{1,0:T(8,128)(2,1)S(1)} %copy-done.2, bf16[144,4096]{1,0:T(8,128)(2,1)S(1)} %copy-done.1, bf16[16,128]{1,0:T(8,128)(2,1)S(1)} %copy-done.4, bf16[144,16]{1,0:T(8,128)(2,1)S(1)} %copy-done.3, ...), custom_call_target="tpu_custom_call" | custom-call | tf_op jit(solution)/shard_map/attend/pallas_call | solution.py:130
  97.7 0.0 collective-permute-done.5.refs_4_
  97.7 0.0 collective-permute-done.3.refs_3_
  97.7 1.5 collective-permute-done.1.refs_2_
  99.2 0.8 join.1
  100.1 17.3 %all_to_all.20.refs_0_ = bf16[8,144,128]{2,1,0:T(8,128)(2,1)S(1)} all-to-all(bf16[8,144,128]{2,1,0:T(8,128)(2,1)S(1)} %join.1), channel_id=1, replica_groups={{0,8,16,24,32,40,48,56},{64,72,80,88,96,104,112,120},{128,136,144,152,1..., dimensions={0} | all-to-all | bytes 589824 | tf_op jit(solution)/shard_map/all_to_all | solution.py:227
  117.4 0.3 combine.1
  117.7 11.8 %all_to_all.21 = bf16[8,16,1024]{2,1,0:T(8,128)(2,1)S(1)} all-to-all(bf16[8,16,1024]{2,1,0:T(8,128)(2,1)S(1)} %combine.1), channel_id=1, replica_groups={{0,8,16,24,32,40,48,56},{64,72,80,88,96,104,112,120},{128,136,144,152,1..., dimensions={0} | all-to-all | bytes 524288 | tf_op jit(solution)/shard_map/all_to_all | solution.py:227
  129.5 0.0 collective-permute-start.6
  129.5 2.7 %collective-permute-start.7 = (bf16[128,1024]{1,0:T(8,128)(2,1)S(1)}, bf16[128,1024]{1,0:T(8,128)(2,1)S(1)}, u32[]{:S(2)}, u32[]{:S(2)}) collective-permute-start(bf16[128,1024]{1,0:T(8,128)(2,1)S(1)} %bitcast.12), channel_id=1, source_target_pairs={{0,192},{8,200},{16,208},{24,216},{32,224},{40,232},{48,240},{56,2... | collective-permute-start | bytes 786440 | tf_op jit(solution)/shard_map/ppermute | solution.py:231
  132.2 0.0 collective-permute-start.8
  132.2 0.0 copy-done
  132.2 0.2 fusion.3
  132.5 3.5 %collective-permute-done.6 = bf16[128,1024]{1,0:T(8,128)(2,1)S(1)} collective-permute-done((bf16[128,1024]{1,0:T(8,128)(2,1)S(1)}, bf16[128,1024]{1,0:T(8,128)(2,1)S(1)}, u32[]{:S(2)}, u32[]{:S(2)}) %collective-permute-start.6) | collective-permute-done | bytes 262176 | tf_op jit(solution)/shard_map/ppermute | solution.py:231
  135.9 0.2 fusion.2
  136.2 2.1 %collective-permute-done.7 = bf16[128,1024]{1,0:T(8,128)(2,1)S(1)} collective-permute-done((bf16[128,1024]{1,0:T(8,128)(2,1)S(1)}, bf16[128,1024]{1,0:T(8,128)(2,1)S(1)}, u32[]{:S(2)}, u32[]{:S(2)}) %collective-permute-start.7) | collective-permute-done | bytes 262176 | tf_op jit(solution)/shard_map/ppermute | solution.py:231
  138.3 0.2 fusion.1
  138.5 0.7 collective-permute-done.8
  139.2 0.2 fusion
  139.5 18.0 %all_to_all.22 = bf16[8,64,256]{2,1,0:T(8,128)(2,1)S(1)} all-to-all(bf16[8,64,256]{2,1,0:T(8,128)(2,1)S(1)} %bitcast.19), channel_id=1, replica_groups=mesh['seq'=32,'mp'=8] {'mp'}, dimensions={0} | all-to-all | bytes 524288 | tf_op jit(solution)/shard_map/all_to_all | solution.py:273
  157.5 0.7 reduce_sum.12
  (7 shorter events, 0.1 us)
Async XLA Ops:
  0.0 132.2 %copy-start = (bf16[1024,256]{1,0:T(8,128)(2,1)S(1)}, bf16[1024,256]{1,0:T(8,128)(2,1)}, u32[]{:S(2)}) copy-start(bf16[1024,256]{1,0:T(8,128)(2,1)} %param.13) | copy-start | bytes 1572868
  0.0 14.1 %copy-start.5 = (s32[512]{0:T(512)S(1)}, s32[512]{0:T(512)}, u32[]{:S(2)}) copy-start(s32[512]{0:T(512)} %param.12) | copy-start | bytes 6148
  1.6 23.3 %copy-start.2 = (bf16[4096,128]{1,0:T(8,128)(2,1)S(1)}, bf16[4096,128]{1,0:T(8,128)(2,1)}, u32[]{:S(2)}) copy-start(bf16[4096,128]{1,0:T(8,128)(2,1)} %refs_1_.9) | copy-start | bytes 3145732
  1.6 23.3 %copy-start.4 = (bf16[16,128]{1,0:T(8,128)(2,1)S(1)}, bf16[16,128]{1,0:T(8,128)(2,1)}, u32[]{:S(2)}) copy-start(bf16[16,128]{1,0:T(8,128)(2,1)} %refs_3_.9) | copy-start | bytes 12292
  1.6 19.5 %all-to-all-start = ((bf16[8,16,1024]{2,1,0:T(8,128)(2,1)}), bf16[8,16,1024]{2,1,0:T(8,128)(2,1)S(1)}, u32[]{:S(2)}, u32[]{:S(2)}) async-start(bf16[8,16,1024]{2,1,0:T(8,128)(2,1)} %broadcast_in_dim.22), calls=%async_computation | async-start | bytes 524288 | tf_op jit(solution)/shard_map/all_to_all | solution.py:227
  21.1 8.8 %collective-permute-start.4 = (bf16[128,1024]{1,0:T(8,128)(2,1)S(1)}, bf16[128,1024]{1,0:T(8,128)(2,1)S(1)}, u32[]{:S(2)}, u32[]{:S(2)}) collective-permute-start(bf16[128,1024]{1,0:T(8,128)(2,1)S(1)} %bitcast.15), channel_id=1, source_target_pairs={{0,192},{8,200},{16,208},{24,216},{32,224},{40,232},{48,240},{56,2... | collective-permute-start | bytes 786440 | tf_op jit(solution)/shard_map/ppermute | solution.py:231
  23.8 32.4 %collective-permute-start.2 = (bf16[128,1024]{1,0:T(8,128)(2,1)S(1)}, bf16[128,1024]{1,0:T(8,128)(2,1)S(1)}, u32[]{:S(2)}, u32[]{:S(2)}) collective-permute-start(bf16[128,1024]{1,0:T(8,128)(2,1)S(1)} %bitcast.16), channel_id=1, source_target_pairs={{0,128},{8,136},{16,144},{24,152},{32,160},{40,168},{48,176},{56,1... | collective-permute-start | bytes 786440 | tf_op jit(solution)/shard_map/ppermute | solution.py:231
  24.2 50.1 %collective-permute-start = (bf16[128,1024]{1,0:T(8,128)(2,1)S(1)}, bf16[128,1024]{1,0:T(8,128)(2,1)S(1)}, u32[]{:S(2)}, u32[]{:S(2)}) collective-permute-start(bf16[128,1024]{1,0:T(8,128)(2,1)S(1)} %bitcast.17), channel_id=1, source_target_pairs={{0,64},{8,72},{16,80},{24,88},{32,96},{40,104},{48,112},{56,120},{... | collective-permute-start | bytes 786440 | tf_op jit(solution)/shard_map/ppermute | solution.py:231
  24.9 1.3 copy-start.1
  26.2 0.8 copy-start.3
  47.8 49.9 %collective-permute-start.5 = (bf16[1056,128]{1,0:T(8,128)(2,1)S(1)}, bf16[1056,128]{1,0:T(8,128)(2,1)S(1)}, u32[]{:S(2)}, u32[]{:S(2)}) collective-permute-start(bf16[1056,128]{1,0:T(8,128)(2,1)S(1)} %attend.9), channel_id=1, source_target_pairs={{0,64},{8,72},{16,80},{24,88},{32,96},{40,104},{48,112},{56,120},{... | collective-permute-start | bytes 811016 | tf_op jit(solution)/shard_map/ppermute | solution.py:231
  74.2 23.5 %collective-permute-start.3 = (bf16[1056,128]{1,0:T(8,128)(2,1)S(1)}, bf16[1056,128]{1,0:T(8,128)(2,1)S(1)}, u32[]{:S(2)}, u32[]{:S(2)}) collective-permute-start(bf16[1056,128]{1,0:T(8,128)(2,1)S(1)} %attend.8), channel_id=1, source_target_pairs={{0,128},{8,136},{16,144},{24,152},{32,160},{40,168},{48,176},{56,1... | collective-permute-start | bytes 811016 | tf_op jit(solution)/shard_map/ppermute | solution.py:231
  92.3 7.0 %collective-permute-start.1 = (bf16[1056,128]{1,0:T(8,128)(2,1)S(1)}, bf16[1056,128]{1,0:T(8,128)(2,1)S(1)}, u32[]{:S(2)}, u32[]{:S(2)}) collective-permute-start(bf16[1056,128]{1,0:T(8,128)(2,1)S(1)} %attend.7), channel_id=1, source_target_pairs={{0,192},{8,200},{16,208},{24,216},{32,224},{40,232},{48,240},{56,2... | collective-permute-start | bytes 811016 | tf_op jit(solution)/shard_map/ppermute | solution.py:231
  129.5 6.4 %collective-permute-start.6 = (bf16[128,1024]{1,0:T(8,128)(2,1)S(1)}, bf16[128,1024]{1,0:T(8,128)(2,1)S(1)}, u32[]{:S(2)}, u32[]{:S(2)}) collective-permute-start(bf16[128,1024]{1,0:T(8,128)(2,1)S(1)} %bitcast.11), channel_id=1, source_target_pairs={{0,64},{8,72},{16,80},{24,88},{32,96},{40,104},{48,112},{56,120},{... | collective-permute-start | bytes 786440 | tf_op jit(solution)/shard_map/ppermute | solution.py:231
  129.5 8.8 %collective-permute-start.7 = (bf16[128,1024]{1,0:T(8,128)(2,1)S(1)}, bf16[128,1024]{1,0:T(8,128)(2,1)S(1)}, u32[]{:S(2)}, u32[]{:S(2)}) collective-permute-start(bf16[128,1024]{1,0:T(8,128)(2,1)S(1)} %bitcast.12), channel_id=1, source_target_pairs={{0,192},{8,200},{16,208},{24,216},{32,224},{40,232},{48,240},{56,2... | collective-permute-start | bytes 786440 | tf_op jit(solution)/shard_map/ppermute | solution.py:231
  132.2 7.0 %collective-permute-start.8 = (bf16[128,1024]{1,0:T(8,128)(2,1)S(1)}, bf16[128,1024]{1,0:T(8,128)(2,1)S(1)}, u32[]{:S(2)}, u32[]{:S(2)}) collective-permute-start(bf16[128,1024]{1,0:T(8,128)(2,1)S(1)} %bitcast.13), channel_id=1, source_target_pairs={{0,128},{8,136},{16,144},{24,152},{32,160},{40,168},{48,176},{56,1... | collective-permute-start | bytes 786440 | tf_op jit(solution)/shard_map/ppermute | solution.py:231
where the time goes:
time: 159 us; the launch traced here: 158 us
  Pallas kernels  63.2 us (40%)
  blocking collectives  47.1 us (30%)
  starting transfers between devices  26.8 us (17%)
  waiting for transfers between devices  14.8 us (9%)
  local copies, waits for them, and re-layouts  4.39 us (3%)
    pallas_call x5, Pallas kernels, attend(): pl.pallas_call(lambda *refs: attend_kernel(group, min(4, group), 512, *re...  59.4 us
    all_to_all x2, blocking collectives, across_z(): lax.all_to_all(array, 'seq', 0, 0, axis_index_groups=along_z, tiled=True)  29.1 us
    all_to_all x1, blocking collectives, on_device(): scored = lax.all_to_all(scored, 'mp', 0, 0, tiled=True)  18 us
    ppermute x9, starting transfers between devices, along_y(): return lax.ppermute(array, 'seq', pairs)  17.6 us
    all_to_all x1, starting transfers between devices, across_z(): lax.all_to_all(array, 'seq', 0, 0, axis_index_groups=along_z, tiled=True)  9.15 us
    ppermute x9, waiting for transfers between devices, along_y(): return lax.ppermute(array, 'seq', pairs)  7.95 us
    all_to_all x1, waiting for transfers between devices, across_z(): lax.all_to_all(array, 'seq', 0, 0, axis_index_groups=along_z, tiled=True)  6.84 us
  transfers between devices with their start and end apart: 10, of which 6 were waited for; matrix products, arithmetic and copies ran while one was open for 1% of the time, Pallas kernels for 39%

commit v1 on v0

--- a/solution.py
+++ b/solution.py
@@ -23,12 +23,10 @@
     return high, middle, rest - middle
 
 
-def prepare_kernel(v_ref, rv_ref, vt_ref, rvt_ref, fact_ref):
+def prepare_kernel(v_ref, rv_ref, vt_ref, fact_ref):
     v = v_ref[...]
     vt_ref[:HD, :] = v.T
     vt_ref[HD:, :] = jnp.ones((ONES, v.shape[0]), bf16)
-    rvt_ref[:HD, :] = rv_ref[...].T
-    rvt_ref[HD:, :] = jnp.ones((ONES, rv_ref.shape[0]), bf16)
     fact_ref[0, 0] = jnp.maximum(
         jnp.max(jnp.abs(v.astype(f32))), jnp.max(jnp.abs(rv_ref[...].astype(f32)))
     )
@@ -40,16 +38,15 @@
         prepare_kernel,
         out_shape=(
             jax.ShapeDtypeStruct((HD + ONES, values.shape[0]), bf16),
-            jax.ShapeDtypeStruct((HD + ONES, own_values.shape[0]), bf16),
             jax.ShapeDtypeStruct((1, 1), f32),
         ),
-        out_specs=(vmem, vmem, pl.BlockSpec(memory_space=pltpu.SMEM)),
+        out_specs=(vmem, pl.BlockSpec(memory_space=pltpu.SMEM)),
         name="prepare",
     )(values, own_values)
 
 
 def attend_kernel(
-    group, stack, key_block, q_ref, k_ref, vt_ref, rk_ref, rvt_ref, bias_ref, fact_ref, out_ref,
+    group, stack, key_block, q_ref, k_ref, vt_ref, rk_ref, rv_ref, bias_ref, fact_ref, out_ref,
     logs_ref,
 ):
     tokens = q_ref.shape[0]
@@ -75,6 +72,9 @@
             pieces + (jnp.zeros((group, tokens), f32),), axis=0
         ).astype(bf16)
 
+    own_columns = jnp.concatenate(
+        [rv_ref[...].T, jnp.ones((ONES, rv_ref.shape[0]), bf16)], axis=0
+    )
     lowest, highest = [], []
     logs = []
     bias = jnp.concatenate([bias_ref[...]] * stack, axis=1)
@@ -82,7 +82,7 @@
         q = jnp.concatenate(
             [q_ref[:, head * HD : (head + 1) * HD] for head in range(first, first + stack)], axis=0
         )
-        total = product(rvt_ref[...], jnp.exp2(scores(rk_ref[...], q) + bias))
+        total = product(own_columns, jnp.exp2(scores(rk_ref[...], q) + bias))
         now = scores(k_ref[:key_block, :], q)
         for start in range(0, keys, key_block):
             later = start + key_block
@@ -115,7 +115,7 @@
             top = jnp.maximum(
                 jnp.max(mine, axis=0, keepdims=True), jnp.max(rest, axis=0, keepdims=True)
             )
-            total = product(rvt_ref[...], jnp.exp2(mine - top))
+            total = product(own_columns, jnp.exp2(mine - top))
             total += product(vt_ref[...], jnp.exp2(rest - top))
             logs_ref[pl.ds(head, 1), :] = jnp.log2(total[HD : HD + 1]) + top
             out_ref[pl.ds(pl.multiple_of(head * tokens, tokens), tokens), :] = result_of(total)
@@ -123,7 +123,7 @@
         logs_rows([logs_ref[...]])
 
 
-def attend(queries, keys, columns, own_keys, own_columns, bias, fact):
+def attend(queries, keys, columns, own_keys, own_values, bias, fact):
     tokens, width = queries.shape
     group = width // HD
     vmem = pl.BlockSpec(memory_space=pltpu.VMEM)
@@ -135,7 +135,7 @@
         scratch_shapes=[pltpu.VMEM((group, tokens), f32)],
         compiler_params=pltpu.CompilerParams(vmem_limit_bytes=20 << 20),
         name="attend",
-    )(queries, keys, columns, own_keys, own_columns, bias, fact)
+    )(queries, keys, columns, own_keys, own_values, bias, fact)
 
 
 def join_kernel(group, halves, *refs):
@@ -211,6 +211,31 @@
     )(parts)
 
 
+def project_kernel(side_ref, heads_ref, *refs):
+    weight_refs, out_ref = refs[:-1], refs[-1]
+    heads = heads_ref[...]
+    sides = len(weight_refs)
+    rows = out_ref.shape[1]
+    for step, ref in enumerate(weight_refs):
+        column = lax.rem(side_ref[0] + sides - step, sides)
+        block = jnp.dot(heads, ref[...], preferred_element_type=f32).astype(bf16)
+        for half in range(out_ref.shape[0] // sides):
+            out_ref[half * sides + column] = block[half * rows : (half + 1) * rows]
+
+
+def project(side, heads, weights, ways):
+    rows = heads.shape[0] * len(weights) // ways
+    vmem = pl.BlockSpec(memory_space=pltpu.VMEM)
+    return pl.pallas_call(
+        project_kernel,
+        out_shape=jax.ShapeDtypeStruct((ways, rows, weights[0].shape[1]), bf16),
+        in_specs=[pl.BlockSpec(memory_space=pltpu.SMEM)] + [vmem] * (1 + len(weights)),
+        out_specs=vmem,
+        compiler_params=pltpu.CompilerParams(vmem_limit_bytes=20 << 20),
+        name="project",
+    )(side, heads, *weights)
+
+
 Y, Z = 4, 8
 
 
@@ -232,7 +257,7 @@
 
     mine = across_z(jnp.broadcast_to(queries[None], (Z,) + queries.shape)).reshape(quarter, width)
 
-    columns, own_columns, fact = prepare(prefix_values, resp_values)
+    columns, fact = prepare(prefix_values, resp_values)
     first = place * tokens
     own_segments = lax.dynamic_slice_in_dim(segment_ids, first, tokens)
     own_rows = first + jnp.arange(tokens, dtype=jnp.int32)
@@ -246,32 +271,31 @@
         return lax.dynamic_slice_in_dim(bias, owner * quarter, quarter, 1)
 
     def part_for(array, block):
-        return attend(array, prefix_keys, columns, resp_keys, own_columns, block, fact)
+        return attend(array, prefix_keys, columns, resp_keys, resp_values, block, fact)
 
     blocks = [bias_for(step) for step in range(Y)]
-    mine, columns, own_columns, fact, *blocks = lax.optimization_barrier(
-        (mine, columns, own_columns, fact, *blocks)
-    )
+    mine, columns, fact, *blocks = lax.optimization_barrier((mine, columns, fact, *blocks))
     arrivals = {step: along_y(mine, step) for step in (1, 3, 2)}
     own = [part_for(mine[:, : width // 2], blocks[0])]
     *blocks, own[0] = lax.optimization_barrier((*blocks, own[0]))
     parts = [along_y(part_for(arrivals[step], blocks[step]), -step) for step in (1, 2, 3)]
     own.append(part_for(mine[:, width // 2 :], blocks[0]))
 
+    out_weight, own[1] = lax.optimization_barrier((out_weight, own[1]))
+    weights = [out_weight] + [along_y(out_weight, step) for step in (1, 2, 3)]
     joined = across_z(join(own, parts, group, Z))
     heads = across_z(combine(joined, group)).reshape(quarter, width)
-    pieces = [heads] + [along_y(heads, step) for step in (1, 3, 2)]
-    scored = [
-        jnp.dot(piece, out_weight, preferred_element_type=f32).astype(bf16) for piece in pieces
-    ]
-    order = (0, 1, 3, 2)
-    whole = jnp.zeros((rows, out_weight.shape[1]), bf16)
-    for step, piece in zip(order, scored):
-        owner = (place // Z + Y - step) % Y
-        whole = lax.dynamic_update_slice_in_dim(whole, piece, owner * quarter, 0)
-    scored = whole.reshape(ways, rows // ways, -1)
-    scored = lax.all_to_all(scored, "mp", 0, 0, tiled=True)
-    return jnp.sum(scored.astype(f32), axis=0).astype(bf16)
+    side = (place // Z).astype(jnp.int32).reshape(1)
+    scored = lax.all_to_all(project(side, heads, weights, ways), "mp", 0, 0, tiled=True)
+    scored = jnp.sum(scored.astype(f32), axis=0).astype(bf16)
+    pairs = []
+    for y in range(Y):
+        for z in range(Z):
+            for block in range(ways):
+                half, column = block // Y, block % Y
+                source = (y * Z + z) * ways + block
+                pairs.append((source, (column * Z + z) * ways + y * (ways // Y) + half))
+    return lax.ppermute(scored, ("seq", "mp"), pairs)
 
 
 def solution(mesh):

time: 159 us -> 157 us (0.987)
  blocking collectives: 47.1 us -> 11.7 us
  starting transfers between devices: 26.8 us -> 52.8 us
  waiting for transfers between devices: 14.8 us -> 35.1 us
  Pallas kernels: 63.2 us -> 51.6 us
    all_to_all x3 -> x1, blocking collectives: 47.1 us -> 11.7 us  [on_device(): lax.all_to_all(project(side, heads, weights, ways), 'mp', 0, 0, tiled=True)]
    all_to_all x1 -> x3, starting transfers between devices: 9.15 us -> 24.5 us  [across_z(): lax.all_to_all(array, 'seq', 0, 0, axis_index_groups=along_z, tiled=True)]
    pallas_call x5, Pallas kernels: 59.4 us -> 45.9 us  [attend(): pl.pallas_call(lambda *refs: attend_kernel(group, min(4, group), 512, *re...]
    ppermute x9, waiting for transfers between devices: 7.95 us -> 19.6 us  [along_y(): return lax.ppermute(array, 'seq', pairs)]
    ppermute x9, starting transfers between devices: 17.6 us -> 24.7 us  [along_y(): return lax.ppermute(array, 'seq', pairs)]
    all_to_all x1 -> x3, waiting for transfers between devices: 6.84 us -> 12.2 us  [across_z(): lax.all_to_all(array, 'seq', 0, 0, axis_index_groups=along_z, tiled=True)]
    ppermute x0 -> x1, starting transfers between devices: none -> 3.53 us  [on_device(): return lax.ppermute(scored, ('seq', 'mp'), pairs)]
    ppermute x0 -> x1, waiting for transfers between devices: none -> 3.39 us  [on_device(): return lax.ppermute(scored, ('seq', 'mp'), pairs)]
  transfers between devices with their start and end apart: 10 -> 13, of which waited for: 6 -> 6; matrix products, arithmetic and copies ran while one was open for 1% -> 1% of each run, Pallas kernels for 39% -> 32%
where the time goes in v1:
time: 157 us; the launch traced here: 156 us
  starting transfers between devices  52.8 us (34%)
  Pallas kernels  51.6 us (33%)
  waiting for transfers between devices  35.1 us (22%)
  blocking collectives  11.7 us (7%)
  local copies, waits for them, and re-layouts  4.19 us (3%)
    pallas_call x5, Pallas kernels, attend(): pl.pallas_call(lambda *refs: attend_kernel(group, min(4, group), 512, *re...  45.9 us
    ppermute x9, starting transfers between devices, along_y(): return lax.ppermute(array, 'seq', pairs)  24.7 us
    all_to_all x3, starting transfers between devices, across_z(): lax.all_to_all(array, 'seq', 0, 0, axis_index_groups=along_z, tiled=True)  24.5 us
    ppermute x9, waiting for transfers between devices, along_y(): return lax.ppermute(array, 'seq', pairs)  19.6 us
    all_to_all x3, waiting for transfers between devices, across_z(): lax.all_to_all(array, 'seq', 0, 0, axis_index_groups=along_z, tiled=True)  12.2 us
    all_to_all x1, blocking collectives, on_device(): lax.all_to_all(project(side, heads, weights, ways), 'mp', 0, 0, tiled=True)  11.7 us
    ppermute x1, starting transfers between devices, on_device(): return lax.ppermute(scored, ('seq', 'mp'), pairs)  3.53 us
    ppermute x1, waiting for transfers between devices, on_device(): return lax.ppermute(scored, ('seq', 'mp'), pairs)  3.39 us
  transfers between devices with their start and end apart: 13, of which 6 were waited for; matrix products, arithmetic and copies ran while one was open for 1% of the time, Pallas kernels for 32%

profile of v1, /device:TPU:1, one launch (start us, length us, event | category | flops | bytes accessed | tf_op | source)
XLA Modules:
  0.0 155.7 jit_solution(17348641907603338412)
XLA Ops:
  0.0 1.5 broadcast_in_dim.8
  1.5 9.1 %all-to-all-start = ((bf16[8,16,1024]{2,1,0:T(8,128)(2,1)}), bf16[8,16,1024]{2,1,0:T(8,128)(2,1)S(1)}, u32[]{:S(2)}, u32[]{:S(2)}) async-start(bf16[8,16,1024]{2,1,0:T(8,128)(2,1)} %broadcast_in_dim.8), calls=%async_computation | async-start | bytes 524288 | tf_op jit(solution)/shard_map/all_to_all | solution.py:252
  10.7 0.8 dynamic_slice.15
  11.4 2.6 %prepare.1 = (bf16[144,4096]{1,0:T(8,128)(2,1)}, f32[1,1]{1,0:T(1,128)}) custom-call(bf16[4096,128]{1,0:T(8,128)(2,1)} %v_ref.1, bf16[16,128]{1,0:T(8,128)(2,1)} %refs_4_.9), custom_call_target="tpu_custom_call" | custom-call | tf_op jit(solution)/shard_map/prepare/pallas_call | solution.py:37
  14.1 0.0 copy-done.5
  14.1 0.1 fusion.1
  14.2 6.9 %all-to-all-done = bf16[8,16,1024]{2,1,0:T(8,128)(2,1)S(1)} async-done(((bf16[8,16,1024]{2,1,0:T(8,128)(2,1)}), bf16[8,16,1024]{2,1,0:T(8,128)(2,1)S(1)}, u32[]{:S(2)}, u32[]{:S(2)}) %all-to-all-start) | async-done | bytes 262176 | tf_op jit(solution)/shard_map/all_to_all | solution.py:252
  21.0 2.7 %collective-permute-start.4 = (bf16[128,1024]{1,0:T(8,128)(2,1)S(1)}, bf16[128,1024]{1,0:T(8,128)(2,1)S(1)}, u32[]{:S(2)}, u32[]{:S(2)}) collective-permute-start(bf16[128,1024]{1,0:T(8,128)(2,1)S(1)} %bitcast.4), channel_id=1, source_target_pairs={{0,192},{8,200},{16,208},{24,216},{32,224},{40,232},{48,240},{56,2... | collective-permute-start | bytes 786440 | tf_op jit(solution)/shard_map/ppermute | solution.py:256
  23.8 0.0 collective-permute-start
  23.8 1.6 %collective-permute-start.2 = (bf16[128,1024]{1,0:T(8,128)(2,1)S(1)}, bf16[128,1024]{1,0:T(8,128)(2,1)S(1)}, u32[]{:S(2)}, u32[]{:S(2)}) collective-permute-start(bf16[128,1024]{1,0:T(8,128)(2,1)S(1)} %bitcast.6), channel_id=1, source_target_pairs={{0,128},{8,136},{16,144},{24,152},{32,160},{40,168},{48,176},{56,1... | collective-permute-start | bytes 786440 | tf_op jit(solution)/shard_map/ppermute | solution.py:256
  25.4 0.0 copy-done.1
  25.4 0.0 copy-done.3
  25.5 0.0 copy-done.4
  25.5 0.0 copy-start
  25.5 1.3 copy-done
  26.7 2.7 %attend.5.refs_0_ = bf16[528,128]{1,0:T(8,128)(2,1)S(1)} custom-call(bf16[128,512]{1,0:T(8,128)(2,1)S(1)} %get-tuple-element.38.refs_0_, bf16[4096,128]{1,0:T(8,128)(2,1)S(1)} %copy-done.1, bf16[144,4096]{1,0:T(8,128)(2,1)S(1)} %copy-done, bf16[16,128]{1,0:T(8,128)(2,1)S(1)} %copy-done.4, bf16[16,128]{1,0:T(8,128)(2,1)S(1)} %copy-done.3, ...), custom_call_target="tpu_custom_call" | custom-call | tf_op jit(solution)/shard_map/attend/pallas_call | solution.py:130
  29.4 0.0 collective-permute-done.4.refs_0_
  29.5 4.5 %attend.9 = bf16[1056,128]{1,0:T(8,128)(2,1)S(1)} custom-call(bf16[128,1024]{1,0:T(8,128)(2,1)S(1)} %collective-permute-done.4.refs_0_, bf16[4096,128]{1,0:T(8,128)(2,1)S(1)} %copy-done.1, bf16[144,4096]{1,0:T(8,128)(2,1)S(1)} %copy-done, bf16[16,128]{1,0:T(8,128)(2,1)S(1)} %copy-done.4, bf16[16,128]{1,0:T(8,128)(2,1)S(1)} %copy-done.3, ...), custom_call_target="tpu_custom_call" | custom-call | tf_op jit(solution)/shard_map/attend/pallas_call | solution.py:130
  34.0 15.3 %collective-permute-start.5 = (bf16[1056,128]{1,0:T(8,128)(2,1)S(1)}, bf16[1056,128]{1,0:T(8,128)(2,1)S(1)}, u32[]{:S(2)}, u32[]{:S(2)}) collective-permute-start(bf16[1056,128]{1,0:T(8,128)(2,1)S(1)} %attend.9), channel_id=1, source_target_pairs={{0,64},{8,72},{16,80},{24,88},{32,96},{40,104},{48,112},{56,120},{... | collective-permute-start | bytes 811016 | tf_op jit(solution)/shard_map/ppermute | solution.py:256
  49.3 0.0 collective-permute-done.refs_0_
  49.3 18.0 %attend.7 = bf16[1056,128]{1,0:T(8,128)(2,1)S(1)} custom-call(bf16[128,1024]{1,0:T(8,128)(2,1)S(1)} %collective-permute-done.refs_0_, bf16[4096,128]{1,0:T(8,128)(2,1)S(1)} %copy-done.1, bf16[144,4096]{1,0:T(8,128)(2,1)S(1)} %copy-done, bf16[16,128]{1,0:T(8,128)(2,1)S(1)} %copy-done.4, bf16[16,128]{1,0:T(8,128)(2,1)S(1)} %copy-done.3, ...), custom_call_target="tpu_custom_call" | custom-call | tf_op jit(solution)/shard_map/attend/pallas_call | solution.py:130
  67.3 0.1 collective-permute-start.1
  67.4 0.0 collective-permute-done.2.refs_0_
  67.4 18.0 %attend.8 = bf16[1056,128]{1,0:T(8,128)(2,1)S(1)} custom-call(bf16[128,1024]{1,0:T(8,128)(2,1)S(1)} %collective-permute-done.2.refs_0_, bf16[4096,128]{1,0:T(8,128)(2,1)S(1)} %copy-done.1, bf16[144,4096]{1,0:T(8,128)(2,1)S(1)} %copy-done, bf16[16,128]{1,0:T(8,128)(2,1)S(1)} %copy-done.4, bf16[16,128]{1,0:T(8,128)(2,1)S(1)} %copy-done.3, ...), custom_call_target="tpu_custom_call" | custom-call | tf_op jit(solution)/shard_map/attend/pallas_call | solution.py:130
  85.4 0.3 collective-permute-start.3
  85.7 2.7 %attend.6.refs_1_ = bf16[528,128]{1,0:T(8,128)(2,1)S(1)} custom-call(bf16[128,512]{1,0:T(8,128)(2,1)S(1)} %get-tuple-element.37.refs_0_, bf16[4096,128]{1,0:T(8,128)(2,1)S(1)} %copy-done.1, bf16[144,4096]{1,0:T(8,128)(2,1)S(1)} %copy-done, bf16[16,128]{1,0:T(8,128)(2,1)S(1)} %copy-done.4, bf16[16,128]{1,0:T(8,128)(2,1)S(1)} %copy-done.3, ...), custom_call_target="tpu_custom_call" | custom-call | tf_op jit(solution)/shard_map/attend/pallas_call | solution.py:130
  88.4 0.0 copy-start.2
  88.4 0.0 collective-permute-done.5.refs_4_
  88.5 0.0 collective-permute-done.1.refs_2_
  88.5 4.1 %collective-permute-done.3.refs_3_ = bf16[1056,128]{1,0:T(8,128)(2,1)S(1)} collective-permute-done((bf16[1056,128]{1,0:T(8,128)(2,1)S(1)}, bf16[1056,128]{1,0:T(8,128)(2,1)S(1)}, u32[]{:S(2)}, u32[]{:S(2)}) %collective-permute-start.3) | collective-permute-done | bytes 270368 | tf_op jit(solution)/shard_map/ppermute | solution.py:256
  92.5 1.5 join.1
  94.1 12.0 %all-to-all-start.1 = ((bf16[8,144,128]{2,1,0:T(8,128)(2,1)}), bf16[8,144,128]{2,1,0:T(8,128)(2,1)S(1)}, u32[]{:S(2)}, u32[]{:S(2)}) async-start(bf16[8,144,128]{2,1,0:T(8,128)(2,1)} %join.1), calls=%async_computation.1 | async-start | bytes 589824 | tf_op jit(solution)/shard_map/all_to_all | solution.py:252
  106.1 0.0 copy-done.2
  106.1 3.9 %collective-permute-start.8 = (bf16[1024,256]{1,0:T(8,128)(2,1)S(1)}, bf16[1024,256]{1,0:T(8,128)(2,1)S(1)}, u32[]{:S(2)}, u32[]{:S(2)}) collective-permute-start(bf16[1024,256]{1,0:T(8,128)(2,1)S(1)} %copy-done.2), channel_id=1, source_target_pairs={{0,192},{8,200},{16,208},{24,216},{32,224},{40,232},{48,240},{56,2... | collective-permute-start | bytes 1572872 | tf_op jit(solution)/shard_map/ppermute | solution.py:256
  110.0 0.0 collective-permute-start.7
  110.0 0.7 collective-permute-start.6
  110.7 5.3 %all-to-all-done.1.refs_0_ = bf16[8,144,128]{2,1,0:T(8,128)(2,1)S(1)} async-done(((bf16[8,144,128]{2,1,0:T(8,128)(2,1)}), bf16[8,144,128]{2,1,0:T(8,128)(2,1)S(1)}, u32[]{:S(2)}, u32[]{:S(2)}) %all-to-all-start.1) | async-done | bytes 294944 | tf_op jit(solution)/shard_map/all_to_all | solution.py:252
  116.0 1.0 combine.1
  117.0 3.4 %all-to-all-start.2 = ((bf16[8,16,1024]{2,1,0:T(8,128)(2,1)}), bf16[8,16,1024]{2,1,0:T(8,128)(2,1)S(1)}, u32[]{:S(2)}, u32[]{:S(2)}) async-start(bf16[8,16,1024]{2,1,0:T(8,128)(2,1)} %combine.1), calls=%async_computation.2 | async-start | bytes 524288 | tf_op jit(solution)/shard_map/all_to_all | solution.py:252
  120.4 0.0 collective-permute-done.8.refs_3_
  120.5 1.2 collective-permute-done.7.refs_2_
  121.6 14.3 %collective-permute-done.6.refs_1_ = bf16[1024,256]{1,0:T(8,128)(2,1)S(1)} collective-permute-done((bf16[1024,256]{1,0:T(8,128)(2,1)S(1)}, bf16[1024,256]{1,0:T(8,128)(2,1)S(1)}, u32[]{:S(2)}, u32[]{:S(2)}) %collective-permute-start.6) | collective-permute-done | bytes 524320 | tf_op jit(solution)/shard_map/ppermute | solution.py:256
  135.9 0.0 all-to-all-done.2
  135.9 0.4 project.1
  136.4 11.7 %all_to_all.20 = bf16[8,64,256]{2,1,0:T(8,128)(2,1)S(1)} all-to-all(bf16[8,64,256]{2,1,0:T(8,128)(2,1)S(1)} %project.1), channel_id=1, replica_groups=mesh['seq'=32,'mp'=8] {'mp'}, dimensions={0} | all-to-all | bytes 524288 | tf_op jit(solution)/shard_map/all_to_all | solution.py:289
  148.1 3.5 %collective-permute-start.9 = (bf16[64,256]{1,0:T(8,128)(2,1)S(1)}, bf16[64,256]{1,0:T(8,128)(2,1)S(1)}, u32[]{:S(2)}, u32[]{:S(2)}) collective-permute-start(bf16[64,256]{1,0:T(8,128)(2,1)S(1)} %reduce_sum.12), channel_id=1, source_target_pairs={{0,0},{1,64},{2,128},{3,192},{4,1},{5,65},{6,129},{7,193},{8,8},{9... | collective-permute-start | bytes 98312 | tf_op jit(solution)/shard_map/ppermute | solution.py:298
  151.7 3.4 %collective-permute-done.9 = bf16[64,256]{1,0:T(8,128)(2,1)S(1)} collective-permute-done((bf16[64,256]{1,0:T(8,128)(2,1)S(1)}, bf16[64,256]{1,0:T(8,128)(2,1)S(1)}, u32[]{:S(2)}, u32[]{:S(2)}) %collective-permute-start.9) | collective-permute-done | bytes 32800 | tf_op jit(solution)/shard_map/ppermute | solution.py:298
  155.1 0.6 copy.9
  (8 shorter events, 0.1 us)
Async XLA Ops:
  0.0 14.1 %copy-start.5 = (s32[512]{0:T(512)S(1)}, s32[512]{0:T(512)}, u32[]{:S(2)}) copy-start(s32[512]{0:T(512)} %param.12) | copy-start | bytes 6148
  1.5 23.9 %copy-start.1 = (bf16[4096,128]{1,0:T(8,128)(2,1)S(1)}, bf16[4096,128]{1,0:T(8,128)(2,1)}, u32[]{:S(2)}) copy-start(bf16[4096,128]{1,0:T(8,128)(2,1)} %refs_1_.9) | copy-start | bytes 3145732
  1.5 23.9 %copy-start.3 = (bf16[16,128]{1,0:T(8,128)(2,1)S(1)}, bf16[16,128]{1,0:T(8,128)(2,1)}, u32[]{:S(2)}) copy-start(bf16[16,128]{1,0:T(8,128)(2,1)} %refs_4_.9) | copy-start | bytes 12292
  1.5 23.9 %copy-start.4 = (bf16[16,128]{1,0:T(8,128)(2,1)S(1)}, bf16[16,128]{1,0:T(8,128)(2,1)}, u32[]{:S(2)}) copy-start(bf16[16,128]{1,0:T(8,128)(2,1)} %refs_3_.9) | copy-start | bytes 12292
  1.5 19.5 %all-to-all-start = ((bf16[8,16,1024]{2,1,0:T(8,128)(2,1)}), bf16[8,16,1024]{2,1,0:T(8,128)(2,1)S(1)}, u32[]{:S(2)}, u32[]{:S(2)}) async-start(bf16[8,16,1024]{2,1,0:T(8,128)(2,1)} %broadcast_in_dim.8), calls=%async_computation | async-start | bytes 524288 | tf_op jit(solution)/shard_map/all_to_all | solution.py:252
  21.0 8.4 %collective-permute-start.4 = (bf16[128,1024]{1,0:T(8,128)(2,1)S(1)}, bf16[128,1024]{1,0:T(8,128)(2,1)S(1)}, u32[]{:S(2)}, u32[]{:S(2)}) collective-permute-start(bf16[128,1024]{1,0:T(8,128)(2,1)S(1)} %bitcast.4), channel_id=1, source_target_pairs={{0,192},{8,200},{16,208},{24,216},{32,224},{40,232},{48,240},{56,2... | collective-permute-start | bytes 786440 | tf_op jit(solution)/shard_map/ppermute | solution.py:256
  23.8 25.6 %collective-permute-start = (bf16[128,1024]{1,0:T(8,128)(2,1)S(1)}, bf16[128,1024]{1,0:T(8,128)(2,1)S(1)}, u32[]{:S(2)}, u32[]{:S(2)}) collective-permute-start(bf16[128,1024]{1,0:T(8,128)(2,1)S(1)} %bitcast.5), channel_id=1, source_target_pairs={{0,64},{8,72},{16,80},{24,88},{32,96},{40,104},{48,112},{56,120},{... | collective-permute-start | bytes 786440 | tf_op jit(solution)/shard_map/ppermute | solution.py:256
  23.8 43.6 %collective-permute-start.2 = (bf16[128,1024]{1,0:T(8,128)(2,1)S(1)}, bf16[128,1024]{1,0:T(8,128)(2,1)S(1)}, u32[]{:S(2)}, u32[]{:S(2)}) collective-permute-start(bf16[128,1024]{1,0:T(8,128)(2,1)S(1)} %bitcast.6), channel_id=1, source_target_pairs={{0,128},{8,136},{16,144},{24,152},{32,160},{40,168},{48,176},{56,1... | collective-permute-start | bytes 786440 | tf_op jit(solution)/shard_map/ppermute | solution.py:256
  25.5 1.3 copy-start
  34.0 54.4 %collective-permute-start.5 = (bf16[1056,128]{1,0:T(8,128)(2,1)S(1)}, bf16[1056,128]{1,0:T(8,128)(2,1)S(1)}, u32[]{:S(2)}, u32[]{:S(2)}) collective-permute-start(bf16[1056,128]{1,0:T(8,128)(2,1)S(1)} %attend.9), channel_id=1, source_target_pairs={{0,64},{8,72},{16,80},{24,88},{32,96},{40,104},{48,112},{56,120},{... | collective-permute-start | bytes 811016 | tf_op jit(solution)/shard_map/ppermute | solution.py:256
  67.3 21.1 %collective-permute-start.1 = (bf16[1056,128]{1,0:T(8,128)(2,1)S(1)}, bf16[1056,128]{1,0:T(8,128)(2,1)S(1)}, u32[]{:S(2)}, u32[]{:S(2)}) collective-permute-start(bf16[1056,128]{1,0:T(8,128)(2,1)S(1)} %attend.7), channel_id=1, source_target_pairs={{0,192},{8,200},{16,208},{24,216},{32,224},{40,232},{48,240},{56,2... | collective-permute-start | bytes 811016 | tf_op jit(solution)/shard_map/ppermute | solution.py:256
  85.4 7.1 %collective-permute-start.3 = (bf16[1056,128]{1,0:T(8,128)(2,1)S(1)}, bf16[1056,128]{1,0:T(8,128)(2,1)S(1)}, u32[]{:S(2)}, u32[]{:S(2)}) collective-permute-start(bf16[1056,128]{1,0:T(8,128)(2,1)S(1)} %attend.8), channel_id=1, source_target_pairs={{0,128},{8,136},{16,144},{24,152},{32,160},{40,168},{48,176},{56,1... | collective-permute-start | bytes 811016 | tf_op jit(solution)/shard_map/ppermute | solution.py:256
  88.4 17.6 %copy-start.2 = (bf16[1024,256]{1,0:T(8,128)(2,1)S(1)}, bf16[1024,256]{1,0:T(8,128)(2,1)}, u32[]{:S(2)}) copy-start(bf16[1024,256]{1,0:T(8,128)(2,1)} %refs_0_) | copy-start | bytes 1572868
  94.1 21.9 %all-to-all-start.1 = ((bf16[8,144,128]{2,1,0:T(8,128)(2,1)}), bf16[8,144,128]{2,1,0:T(8,128)(2,1)S(1)}, u32[]{:S(2)}, u32[]{:S(2)}) async-start(bf16[8,144,128]{2,1,0:T(8,128)(2,1)} %join.1), calls=%async_computation.1 | async-start | bytes 589824 | tf_op jit(solution)/shard_map/all_to_all | solution.py:252
  106.1 14.4 %collective-permute-start.8 = (bf16[1024,256]{1,0:T(8,128)(2,1)S(1)}, bf16[1024,256]{1,0:T(8,128)(2,1)S(1)}, u32[]{:S(2)}, u32[]{:S(2)}) collective-permute-start(bf16[1024,256]{1,0:T(8,128)(2,1)S(1)} %copy-done.2), channel_id=1, source_target_pairs={{0,192},{8,200},{16,208},{24,216},{32,224},{40,232},{48,240},{56,2... | collective-permute-start | bytes 1572872 | tf_op jit(solution)/shard_map/ppermute | solution.py:256
  110.0 11.6 %collective-permute-start.7 = (bf16[1024,256]{1,0:T(8,128)(2,1)S(1)}, bf16[1024,256]{1,0:T(8,128)(2,1)S(1)}, u32[]{:S(2)}, u32[]{:S(2)}) collective-permute-start(bf16[1024,256]{1,0:T(8,128)(2,1)S(1)} %copy-done.2), channel_id=1, source_target_pairs={{0,128},{8,136},{16,144},{24,152},{32,160},{40,168},{48,176},{56,1... | collective-permute-start | bytes 1572872 | tf_op jit(solution)/shard_map/ppermute | solution.py:256
  110.0 25.9 %collective-permute-start.6 = (bf16[1024,256]{1,0:T(8,128)(2,1)S(1)}, bf16[1024,256]{1,0:T(8,128)(2,1)S(1)}, u32[]{:S(2)}, u32[]{:S(2)}) collective-permute-start(bf16[1024,256]{1,0:T(8,128)(2,1)S(1)} %copy-done.2), channel_id=1, source_target_pairs={{0,64},{8,72},{16,80},{24,88},{32,96},{40,104},{48,112},{56,120},{... | collective-permute-start | bytes 1572872 | tf_op jit(solution)/shard_map/ppermute | solution.py:256
  117.0 18.9 %all-to-all-start.2 = ((bf16[8,16,1024]{2,1,0:T(8,128)(2,1)}), bf16[8,16,1024]{2,1,0:T(8,128)(2,1)S(1)}, u32[]{:S(2)}, u32[]{:S(2)}) async-start(bf16[8,16,1024]{2,1,0:T(8,128)(2,1)} %combine.1), calls=%async_computation.2 | async-start | bytes 524288 | tf_op jit(solution)/shard_map/all_to_all | solution.py:252
  148.1 6.9 %collective-permute-start.9 = (bf16[64,256]{1,0:T(8,128)(2,1)S(1)}, bf16[64,256]{1,0:T(8,128)(2,1)S(1)}, u32[]{:S(2)}, u32[]{:S(2)}) collective-permute-start(bf16[64,256]{1,0:T(8,128)(2,1)S(1)} %reduce_sum.12), channel_id=1, source_target_pairs={{0,0},{1,64},{2,128},{3,192},{4,1},{5,65},{6,129},{7,193},{8,8},{9... | collective-permute-start | bytes 98312 | tf_op jit(solution)/shard_map/ppermute | solution.py:298

commit v2 on v1

--- a/solution.py
+++ b/solution.py
@@ -10,7 +10,6 @@
 LOWEST = 2.0**-60
 HIGHEST = 2.0**100
 SMALL = 2.0**-20
-ONES = 16
 DEPTH = 4
 f32 = jnp.float32
 bf16 = jnp.bfloat16
@@ -25,8 +24,7 @@
 
 def prepare_kernel(v_ref, rv_ref, vt_ref, fact_ref):
     v = v_ref[...]
-    vt_ref[:HD, :] = v.T
-    vt_ref[HD:, :] = jnp.ones((ONES, v.shape[0]), bf16)
+    vt_ref[...] = v.T
     fact_ref[0, 0] = jnp.maximum(
         jnp.max(jnp.abs(v.astype(f32))), jnp.max(jnp.abs(rv_ref[...].astype(f32)))
     )
@@ -37,12 +35,35 @@
     return pl.pallas_call(
         prepare_kernel,
         out_shape=(
-            jax.ShapeDtypeStruct((HD + ONES, values.shape[0]), bf16),
+            pltpu.VMEM((HD, values.shape[0]), bf16),
             jax.ShapeDtypeStruct((1, 1), f32),
         ),
         out_specs=(vmem, pl.BlockSpec(memory_space=pltpu.SMEM)),
+        compiler_params=pltpu.CompilerParams(vmem_limit_bytes=20 << 20),
         name="prepare",
     )(values, own_values)
+
+
+def replicate_kernel(x_ref, out_ref, sems):
+    moves = [
+        pltpu.make_async_copy(x_ref, out_ref.at[at], sems.at[at]) for at in range(out_ref.shape[0])
+    ]
+    for move in moves:
+        move.start()
+    for move in moves:
+        move.wait()
+
+
+def replicate(array, count):
+    return pl.pallas_call(
+        replicate_kernel,
+        out_shape=jax.ShapeDtypeStruct((count,) + array.shape, array.dtype),
+        in_specs=[pl.BlockSpec(memory_space=pltpu.VMEM)],
+        out_specs=pl.BlockSpec(memory_space=pl.ANY),
+        scratch_shapes=[pltpu.SemaphoreType.DMA((count,))],
+        compiler_params=pltpu.CompilerParams(vmem_limit_bytes=20 << 20),
+        name="replicate",
+    )(array)
 
 
 def attend_kernel(
@@ -63,8 +84,8 @@
     def product(columns, weights):
         return jnp.dot(columns, weights.astype(bf16), preferred_element_type=f32)
 
-    def result_of(total):
-        return (total[:HD] / total[HD : HD + 1]).T.astype(bf16)
+    def result_of(total, sums):
+        return (total / sums).T.astype(bf16)
 
     def logs_rows(rows):
         pieces = split3(jnp.concatenate(rows, axis=0))
@@ -72,38 +93,45 @@
             pieces + (jnp.zeros((group, tokens), f32),), axis=0
         ).astype(bf16)
 
-    own_columns = jnp.concatenate(
-        [rv_ref[...].T, jnp.ones((ONES, rv_ref.shape[0]), bf16)], axis=0
-    )
-    lowest, highest = [], []
-    logs = []
+    def fold(weights):
+        return jnp.sum(weights.reshape(-1, 8, weights.shape[1]), axis=0)
+
+    own_columns = rv_ref[...].T
+    everything, logs = [], []
     bias = jnp.concatenate([bias_ref[...]] * stack, axis=1)
     for first in range(0, group, stack):
         q = jnp.concatenate(
             [q_ref[:, head * HD : (head + 1) * HD] for head in range(first, first + stack)], axis=0
         )
-        total = product(own_columns, jnp.exp2(scores(rk_ref[...], q) + bias))
+        total, sums = None, None
         now = scores(k_ref[:key_block, :], q)
         for start in range(0, keys, key_block):
             later = start + key_block
             if later < keys:
                 following = scores(k_ref[later : later + key_block, :], q)
-            total += product(vt_ref[:, start:later], jnp.exp2(now))
-            if later < keys:
-                now = following
-        sums = total[HD : HD + 1]
-        lowest.append(jnp.min(sums))
-        highest.append(jnp.max(sums))
+            else:
+                following = scores(rk_ref[...], q) + bias
+            weights = jnp.exp2(now)
+            term = product(vt_ref[:, start:later], weights)
+            total = term if total is None else total + term
+            sums = fold(weights) if sums is None else sums + fold(weights)
+            now = following
+        weights = jnp.exp2(now)
+        total += product(own_columns, weights)
+        sums = jnp.sum(sums + fold(weights), axis=0, keepdims=True)
+        everything.append(sums)
         log = jnp.log2(sums)
         for at in range(stack):
             lanes = slice(at * tokens, (at + 1) * tokens)
             logs.append(log[:, lanes])
             head = first + at
-            out_ref[head * tokens : (head + 1) * tokens, :] = result_of(total[:, lanes])
+            out_ref[head * tokens : (head + 1) * tokens, :] = result_of(
+                total[:, lanes], sums[:, lanes]
+            )
     logs_rows(logs)
-    inside = fact_ref[0, 0] >= SMALL
-    for low, high in zip(lowest, highest):
-        inside = inside & (low >= LOWEST) & (high <= HIGHEST)
+    sums = jnp.concatenate(everything, axis=1)
+    outside = jnp.where((sums >= LOWEST) & (sums <= HIGHEST), f32(0), f32(1))
+    inside = (jnp.max(outside) < 0.5) & (fact_ref[0, 0] >= SMALL)
 
     @pl.when(jnp.logical_not(inside))
     def _():
@@ -115,10 +143,13 @@
             top = jnp.maximum(
                 jnp.max(mine, axis=0, keepdims=True), jnp.max(rest, axis=0, keepdims=True)
             )
-            total = product(own_columns, jnp.exp2(mine - top))
-            total += product(vt_ref[...], jnp.exp2(rest - top))
-            logs_ref[pl.ds(head, 1), :] = jnp.log2(total[HD : HD + 1]) + top
-            out_ref[pl.ds(pl.multiple_of(head * tokens, tokens), tokens), :] = result_of(total)
+            mine, rest = jnp.exp2(mine - top), jnp.exp2(rest - top)
+            total = product(own_columns, mine) + product(vt_ref[...], rest)
+            sums = jnp.sum(mine, axis=0, keepdims=True) + jnp.sum(rest, axis=0, keepdims=True)
+            logs_ref[pl.ds(head, 1), :] = jnp.log2(sums) + top
+            out_ref[pl.ds(pl.multiple_of(head * tokens, tokens), tokens), :] = result_of(
+                total, sums
+            )
 
         logs_rows([logs_ref[...]])
 
@@ -211,29 +242,47 @@
     )(parts)
 
 
-def project_kernel(side_ref, heads_ref, *refs):
-    weight_refs, out_ref = refs[:-1], refs[-1]
+def project_kernel(heads_ref, *refs):
+    sides = len(refs) // 2
     heads = heads_ref[...]
-    sides = len(weight_refs)
+    for weight_ref, out_ref in zip(refs[:sides], refs[sides:]):
+        out_ref[...] = jnp.dot(heads, weight_ref[...], preferred_element_type=f32).astype(bf16)
+
+
+def project(heads, weights):
+    vmem = pl.BlockSpec(memory_space=pltpu.VMEM)
+    shape = jax.ShapeDtypeStruct((heads.shape[0], weights[0].shape[1]), bf16)
+    return pl.pallas_call(
+        project_kernel,
+        out_shape=(shape,) * len(weights),
+        out_specs=(vmem,) * len(weights),
+        compiler_params=pltpu.CompilerParams(vmem_limit_bytes=20 << 20),
+        name="project",
+    )(heads, *weights)
+
+
+def place_rows_kernel(side_ref, *refs):
+    block_refs, out_ref = refs[:-1], refs[-1]
+    sides = len(block_refs)
     rows = out_ref.shape[1]
-    for step, ref in enumerate(weight_refs):
-        column = lax.rem(side_ref[0] + sides - step, sides)
-        block = jnp.dot(heads, ref[...], preferred_element_type=f32).astype(bf16)
-        for half in range(out_ref.shape[0] // sides):
-            out_ref[half * sides + column] = block[half * rows : (half + 1) * rows]
-
-
-def project(side, heads, weights, ways):
-    rows = heads.shape[0] * len(weights) // ways
+    per = out_ref.shape[0] // sides
+    for step, ref in enumerate(block_refs):
+        owner = lax.rem(side_ref[0] + step, sides)
+        for half in range(per):
+            out_ref[owner * per + half] = ref[half * rows : (half + 1) * rows, :]
+
+
+def place_rows(side, blocks, ways):
     vmem = pl.BlockSpec(memory_space=pltpu.VMEM)
-    return pl.pallas_call(
-        project_kernel,
-        out_shape=jax.ShapeDtypeStruct((ways, rows, weights[0].shape[1]), bf16),
-        in_specs=[pl.BlockSpec(memory_space=pltpu.SMEM)] + [vmem] * (1 + len(weights)),
+    rows = len(blocks) * blocks[0].shape[0] // ways
+    return pl.pallas_call(
+        place_rows_kernel,
+        out_shape=jax.ShapeDtypeStruct((ways, rows, blocks[0].shape[1]), bf16),
+        in_specs=[pl.BlockSpec(memory_space=pltpu.SMEM)] + [vmem] * len(blocks),
         out_specs=vmem,
         compiler_params=pltpu.CompilerParams(vmem_limit_bytes=20 << 20),
-        name="project",
-    )(side, heads, *weights)
+        name="place_rows",
+    )(side, *blocks)
 
 
 Y, Z = 4, 8
@@ -255,7 +304,7 @@
         pairs = [(y * Z + z, (y + step) % Y * Z + z) for y in range(Y) for z in range(Z)]
         return lax.ppermute(array, "seq", pairs)
 
-    mine = across_z(jnp.broadcast_to(queries[None], (Z,) + queries.shape)).reshape(quarter, width)
+    mine = across_z(replicate(queries, Z)).reshape(quarter, width)
 
     columns, fact = prepare(prefix_values, resp_values)
     first = place * tokens
@@ -285,17 +334,11 @@
     weights = [out_weight] + [along_y(out_weight, step) for step in (1, 2, 3)]
     joined = across_z(join(own, parts, group, Z))
     heads = across_z(combine(joined, group)).reshape(quarter, width)
+    blocks = project(heads, weights)
     side = (place // Z).astype(jnp.int32).reshape(1)
-    scored = lax.all_to_all(project(side, heads, weights, ways), "mp", 0, 0, tiled=True)
-    scored = jnp.sum(scored.astype(f32), axis=0).astype(bf16)
-    pairs = []
-    for y in range(Y):
-        for z in range(Z):
-            for block in range(ways):
-                half, column = block // Y, block % Y
-                source = (y * Z + z) * ways + block
-                pairs.append((source, (column * Z + z) * ways + y * (ways // Y) + half))
-    return lax.ppermute(scored, ("seq", "mp"), pairs)
+    blocks = [blocks[0]] + [along_y(blocks[step], -step) for step in (1, 2, 3)]
+    scored = lax.all_to_all(place_rows(side, blocks, ways), "mp", 0, 0, tiled=True)
+    return jnp.sum(scored.astype(f32), axis=0).astype(bf16)
 
 
 def solution(mesh):

time: 157 us -> 155 us (0.987); the launches traced: 156 us -> 155 us
  blocking collectives: 11.7 us -> 15.4 us
  starting transfers between devices: 52.8 us -> 49.9 us
  Pallas kernels: 51.6 us -> 49 us
  waiting for transfers between devices: 35.1 us -> 37.2 us
    ppermute x9 -> x12, waiting for transfers between devices: 19.6 us -> 23.5 us  [along_y(): return lax.ppermute(array, 'seq', pairs)]
    all_to_all x1, blocking collectives: 11.7 us -> 15.4 us  [on_device(): lax.all_to_all(place_rows(side, blocks, ways), 'mp', 0, 0, tiled=True)]
    ppermute x1 -> x0, starting transfers between devices: 3.53 us -> none  [on_device(): return lax.ppermute(scored, ('seq', 'mp'), pairs)]
    ppermute x1 -> x0, waiting for transfers between devices: 3.39 us -> none  [on_device(): return lax.ppermute(scored, ('seq', 'mp'), pairs)]
    ppermute x9 -> x12, starting transfers between devices: 24.7 us -> 25 us  [along_y(): return lax.ppermute(array, 'seq', pairs)]
  transfers between devices with their start and end apart: 13 -> 15, of which waited for: 6 -> 7; matrix products, arithmetic and copies ran while one was open for 1% -> 0% of each run, Pallas kernels for 32% -> 30%
where the time goes in v2:
time: 155 us
  starting transfers between devices  49.9 us (32%)
  Pallas kernels  49 us (32%)
  waiting for transfers between devices  37.2 us (24%)
  blocking collectives  15.4 us (10%)
  local copies, waits for them, and re-layouts  2.87 us (2%)
    pallas_call x5, Pallas kernels, attend(): pl.pallas_call(lambda *refs: attend_kernel(group, min(4, group), 512, *re...  44.4 us
    all_to_all x3, starting transfers between devices, across_z(): lax.all_to_all(array, 'seq', 0, 0, axis_index_groups=along_z, tiled=True)  25 us
    ppermute x12, starting transfers between devices, along_y(): return lax.ppermute(array, 'seq', pairs)  25 us
    ppermute x12, waiting for transfers between devices, along_y(): return lax.ppermute(array, 'seq', pairs)  23.5 us
    all_to_all x1, blocking collectives, on_device(): lax.all_to_all(place_rows(side, blocks, ways), 'mp', 0, 0, tiled=True)  15.4 us
    all_to_all x3, waiting for transfers between devices, across_z(): lax.all_to_all(array, 'seq', 0, 0, axis_index_groups=along_z, tiled=True)  13.7 us
  transfers between devices with their start and end apart: 15, of which 7 were waited for; matrix products, arithmetic and copies ran while one was open for 0% of the time, Pallas kernels for 30%

profile of v2, /device:TPU:1, one launch (start us, length us, event | category | flops | bytes accessed | tf_op | source)
XLA Modules:
  0.0 155.5 jit_solution(5435083107600733944)
XLA Ops:
  0.0 0.8 copy-done.5
  0.8 0.8 replicate.1
  1.5 0.0 copy-start.6
  1.6 0.0 copy-start.3
  1.6 9.0 %all-to-all-start = ((bf16[8,16,1024]{2,1,0:T(8,128)(2,1)}), bf16[8,16,1024]{2,1,0:T(8,128)(2,1)S(1)}, u32[]{:S(2)}, u32[]{:S(2)}) async-start(bf16[8,16,1024]{2,1,0:T(8,128)(2,1)} %replicate.1), calls=%async_computation | async-start | bytes 524288 | tf_op jit(solution)/shard_map/all_to_all | solution.py:301
  10.7 0.1 dynamic_slice.15
  10.8 1.3 copy-done.1
  12.1 0.8 prepare.1
  12.9 0.1 fusion.1
  13.0 8.0 %all-to-all-done = bf16[8,16,1024]{2,1,0:T(8,128)(2,1)S(1)} async-done(((bf16[8,16,1024]{2,1,0:T(8,128)(2,1)}), bf16[8,16,1024]{2,1,0:T(8,128)(2,1)S(1)}, u32[]{:S(2)}, u32[]{:S(2)}) %all-to-all-start) | async-done | bytes 262176 | tf_op jit(solution)/shard_map/all_to_all | solution.py:301
  21.0 2.7 %collective-permute-start.4 = (bf16[128,1024]{1,0:T(8,128)(2,1)S(1)}, bf16[128,1024]{1,0:T(8,128)(2,1)S(1)}, u32[]{:S(2)}, u32[]{:S(2)}) collective-permute-start(bf16[128,1024]{1,0:T(8,128)(2,1)S(1)} %bitcast.4), channel_id=1, source_target_pairs={{0,192},{8,200},{16,208},{24,216},{32,224},{40,232},{48,240},{56,2... | collective-permute-start | bytes 786440 | tf_op jit(solution)/shard_map/ppermute | solution.py:305
  23.7 0.0 collective-permute-start
  23.7 1.6 %collective-permute-start.2 = (bf16[128,1024]{1,0:T(8,128)(2,1)S(1)}, bf16[128,1024]{1,0:T(8,128)(2,1)S(1)}, u32[]{:S(2)}, u32[]{:S(2)}) collective-permute-start(bf16[128,1024]{1,0:T(8,128)(2,1)S(1)} %bitcast.6), channel_id=1, source_target_pairs={{0,128},{8,136},{16,144},{24,152},{32,160},{40,168},{48,176},{56,1... | collective-permute-start | bytes 786440 | tf_op jit(solution)/shard_map/ppermute | solution.py:305
  25.4 0.7 copy-done.4
  26.0 2.6 %attend.5.refs_0_ = bf16[528,128]{1,0:T(8,128)(2,1)S(1)} custom-call(bf16[128,512]{1,0:T(8,128)(2,1)S(1)} %get-tuple-element.46.refs_0_, bf16[4096,128]{1,0:T(8,128)(2,1)S(1)} %copy-done, bf16[128,4096]{1,0:T(8,128)(2,1)S(1)} %get-tuple-element.32.refs_2_, bf16[16,128]{1,0:T(8,128)(2,1)S(1)} %copy-done.4, bf16[16,128]{1,0:T(8,128)(2,1)S(1)} %copy-done.3, ...), custom_call_target="tpu_custom_call" | custom-call | tf_op jit(solution)/shard_map/attend/pallas_call | solution.py:161
  28.7 0.0 collective-permute-done.4.refs_0_
  28.7 4.5 %attend.9 = bf16[1056,128]{1,0:T(8,128)(2,1)S(1)} custom-call(bf16[128,1024]{1,0:T(8,128)(2,1)S(1)} %collective-permute-done.4.refs_0_, bf16[4096,128]{1,0:T(8,128)(2,1)S(1)} %copy-done, bf16[128,4096]{1,0:T(8,128)(2,1)S(1)} %get-tuple-element.32.refs_2_, bf16[16,128]{1,0:T(8,128)(2,1)S(1)} %copy-done.4, bf16[16,128]{1,0:T(8,128)(2,1)S(1)} %copy-done.3, ...), custom_call_target="tpu_custom_call" | custom-call | tf_op jit(solution)/shard_map/attend/pallas_call | solution.py:161
  33.1 14.7 %collective-permute-start.5 = (bf16[1056,128]{1,0:T(8,128)(2,1)S(1)}, bf16[1056,128]{1,0:T(8,128)(2,1)S(1)}, u32[]{:S(2)}, u32[]{:S(2)}) collective-permute-start(bf16[1056,128]{1,0:T(8,128)(2,1)S(1)} %attend.9), channel_id=1, source_target_pairs={{0,64},{8,72},{16,80},{24,88},{32,96},{40,104},{48,112},{56,120},{... | collective-permute-start | bytes 811016 | tf_op jit(solution)/shard_map/ppermute | solution.py:305
  47.9 0.0 collective-permute-done.refs_0_
  47.9 17.4 %attend.7 = bf16[1056,128]{1,0:T(8,128)(2,1)S(1)} custom-call(bf16[128,1024]{1,0:T(8,128)(2,1)S(1)} %collective-permute-done.refs_0_, bf16[4096,128]{1,0:T(8,128)(2,1)S(1)} %copy-done, bf16[128,4096]{1,0:T(8,128)(2,1)S(1)} %get-tuple-element.32.refs_2_, bf16[16,128]{1,0:T(8,128)(2,1)S(1)} %copy-done.4, bf16[16,128]{1,0:T(8,128)(2,1)S(1)} %copy-done.3, ...), custom_call_target="tpu_custom_call" | custom-call | tf_op jit(solution)/shard_map/attend/pallas_call | solution.py:161
  65.2 0.1 collective-permute-start.1
  65.3 0.0 collective-permute-done.2.refs_0_
  65.3 17.4 %attend.8 = bf16[1056,128]{1,0:T(8,128)(2,1)S(1)} custom-call(bf16[128,1024]{1,0:T(8,128)(2,1)S(1)} %collective-permute-done.2.refs_0_, bf16[4096,128]{1,0:T(8,128)(2,1)S(1)} %copy-done, bf16[128,4096]{1,0:T(8,128)(2,1)S(1)} %get-tuple-element.32.refs_2_, bf16[16,128]{1,0:T(8,128)(2,1)S(1)} %copy-done.4, bf16[16,128]{1,0:T(8,128)(2,1)S(1)} %copy-done.3, ...), custom_call_target="tpu_custom_call" | custom-call | tf_op jit(solution)/shard_map/attend/pallas_call | solution.py:161
  82.7 0.3 collective-permute-start.3
  83.0 2.6 %attend.6.refs_1_ = bf16[528,128]{1,0:T(8,128)(2,1)S(1)} custom-call(bf16[128,512]{1,0:T(8,128)(2,1)S(1)} %get-tuple-element.45.refs_0_, bf16[4096,128]{1,0:T(8,128)(2,1)S(1)} %copy-done, bf16[128,4096]{1,0:T(8,128)(2,1)S(1)} %get-tuple-element.32.refs_2_, bf16[16,128]{1,0:T(8,128)(2,1)S(1)} %copy-done.4, bf16[16,128]{1,0:T(8,128)(2,1)S(1)} %copy-done.3, ...), custom_call_target="tpu_custom_call" | custom-call | tf_op jit(solution)/shard_map/attend/pallas_call | solution.py:161
  85.7 0.0 collective-permute-done.5.refs_4_
  85.7 0.0 collective-permute-done.1.refs_2_
  85.7 4.2 %collective-permute-done.3.refs_3_ = bf16[1056,128]{1,0:T(8,128)(2,1)S(1)} collective-permute-done((bf16[1056,128]{1,0:T(8,128)(2,1)S(1)}, bf16[1056,128]{1,0:T(8,128)(2,1)S(1)}, u32[]{:S(2)}, u32[]{:S(2)}) %collective-permute-start.3) | collective-permute-done | bytes 270368 | tf_op jit(solution)/shard_map/ppermute | solution.py:305
  89.8 1.5 join.1
  91.4 12.5 %all-to-all-start.1 = ((bf16[8,144,128]{2,1,0:T(8,128)(2,1)}), bf16[8,144,128]{2,1,0:T(8,128)(2,1)S(1)}, u32[]{:S(2)}, u32[]{:S(2)}) async-start(bf16[8,144,128]{2,1,0:T(8,128)(2,1)} %join.1), calls=%async_computation.1 | async-start | bytes 589824 | tf_op jit(solution)/shard_map/all_to_all | solution.py:301
  103.9 2.9 %collective-permute-start.8 = (bf16[1024,256]{1,0:T(8,128)(2,1)S(1)}, bf16[1024,256]{1,0:T(8,128)(2,1)S(1)}, u32[]{:S(2)}, u32[]{:S(2)}) collective-permute-start(bf16[1024,256]{1,0:T(8,128)(2,1)S(1)} %copy-done.2), channel_id=1, source_target_pairs={{0,192},{8,200},{16,208},{24,216},{32,224},{40,232},{48,240},{56,2... | collective-permute-start | bytes 1572872 | tf_op jit(solution)/shard_map/ppermute | solution.py:305
  106.8 0.3 collective-permute-start.7
  107.0 0.8 collective-permute-start.6
  107.8 5.8 %all-to-all-done.1.refs_0_ = bf16[8,144,128]{2,1,0:T(8,128)(2,1)S(1)} async-done(((bf16[8,144,128]{2,1,0:T(8,128)(2,1)}), bf16[8,144,128]{2,1,0:T(8,128)(2,1)S(1)}, u32[]{:S(2)}, u32[]{:S(2)}) %all-to-all-start.1) | async-done | bytes 294944 | tf_op jit(solution)/shard_map/all_to_all | solution.py:301
  113.6 1.0 combine.1
  114.6 3.4 %all-to-all-start.2 = ((bf16[8,16,1024]{2,1,0:T(8,128)(2,1)}), bf16[8,16,1024]{2,1,0:T(8,128)(2,1)S(1)}, u32[]{:S(2)}, u32[]{:S(2)}) async-start(bf16[8,16,1024]{2,1,0:T(8,128)(2,1)} %combine.1), calls=%async_computation.2 | async-start | bytes 524288 | tf_op jit(solution)/shard_map/all_to_all | solution.py:301
  118.1 0.0 collective-permute-done.7.refs_2_
  118.1 15.2 %collective-permute-done.6.refs_1_ = bf16[1024,256]{1,0:T(8,128)(2,1)S(1)} collective-permute-done((bf16[1024,256]{1,0:T(8,128)(2,1)S(1)}, bf16[1024,256]{1,0:T(8,128)(2,1)S(1)}, u32[]{:S(2)}, u32[]{:S(2)}) %collective-permute-start.6) | collective-permute-done | bytes 524320 | tf_op jit(solution)/shard_map/ppermute | solution.py:305
  133.3 0.0 all-to-all-done.2
  133.3 0.4 project.1
  133.8 0.1 collective-permute-start.9
  133.9 0.1 collective-permute-start.10
  134.0 1.4 collective-permute-start.11
  135.3 1.6 %collective-permute-done.9.refs_1_ = bf16[128,256]{1,0:T(8,128)(2,1)S(1)} collective-permute-done((bf16[128,256]{1,0:T(8,128)(2,1)S(1)}, bf16[128,256]{1,0:T(8,128)(2,1)S(1)}, u32[]{:S(2)}, u32[]{:S(2)}) %collective-permute-start.9) | collective-permute-done | bytes 65568 | tf_op jit(solution)/shard_map/ppermute | solution.py:305
  137.0 1.6 %collective-permute-done.10.refs_2_ = bf16[128,256]{1,0:T(8,128)(2,1)S(1)} collective-permute-done((bf16[128,256]{1,0:T(8,128)(2,1)S(1)}, bf16[128,256]{1,0:T(8,128)(2,1)S(1)}, u32[]{:S(2)}, u32[]{:S(2)}) %collective-permute-start.10) | collective-permute-done | bytes 65568 | tf_op jit(solution)/shard_map/ppermute | solution.py:305
  138.6 0.8 collective-permute-done.11.refs_3_
  139.4 15.4 %all_to_all.20 = bf16[8,64,256]{2,1,0:T(8,128)(2,1)S(1)} all-to-all(bf16[8,64,256]{2,1,0:T(8,128)(2,1)S(1)} %place_rows.1), channel_id=1, replica_groups=mesh['seq'=32,'mp'=8] {'mp'}, dimensions={0} | all-to-all | bytes 524288 | tf_op jit(solution)/shard_map/all_to_all | solution.py:340
  154.8 0.7 reduce_sum.12
  (14 shorter events, 0.1 us)
Async XLA Ops:
  0.0 0.8 copy-start.5
  1.5 9.2 %copy-start.6 = (s32[512]{0:T(512)S(1)}, s32[512]{0:T(512)}, u32[]{:S(2)}) copy-start(s32[512]{0:T(512)} %param.12) | copy-start | bytes 6148
  1.6 9.2 %copy-start.3 = (bf16[16,128]{1,0:T(8,128)(2,1)S(1)}, bf16[16,128]{1,0:T(8,128)(2,1)}, u32[]{:S(2)}) copy-start(bf16[16,128]{1,0:T(8,128)(2,1)} %refs_4_.9) | copy-start | bytes 12292
  1.6 19.4 %all-to-all-start = ((bf16[8,16,1024]{2,1,0:T(8,128)(2,1)}), bf16[8,16,1024]{2,1,0:T(8,128)(2,1)S(1)}, u32[]{:S(2)}, u32[]{:S(2)}) async-start(bf16[8,16,1024]{2,1,0:T(8,128)(2,1)} %replicate.1), calls=%async_computation | async-start | bytes 524288 | tf_op jit(solution)/shard_map/all_to_all | solution.py:301
  10.6 14.8 %copy-start = (bf16[4096,128]{1,0:T(8,128)(2,1)S(1)}, bf16[4096,128]{1,0:T(8,128)(2,1)}, u32[]{:S(2)}) copy-start(bf16[4096,128]{1,0:T(8,128)(2,1)} %refs_1_.9) | copy-start | bytes 3145732
  10.8 1.3 copy-start.1
  21.0 7.7 %collective-permute-start.4 = (bf16[128,1024]{1,0:T(8,128)(2,1)S(1)}, bf16[128,1024]{1,0:T(8,128)(2,1)S(1)}, u32[]{:S(2)}, u32[]{:S(2)}) collective-permute-start(bf16[128,1024]{1,0:T(8,128)(2,1)S(1)} %bitcast.4), channel_id=1, source_target_pairs={{0,192},{8,200},{16,208},{24,216},{32,224},{40,232},{48,240},{56,2... | collective-permute-start | bytes 786440 | tf_op jit(solution)/shard_map/ppermute | solution.py:305
  23.7 24.2 %collective-permute-start = (bf16[128,1024]{1,0:T(8,128)(2,1)S(1)}, bf16[128,1024]{1,0:T(8,128)(2,1)S(1)}, u32[]{:S(2)}, u32[]{:S(2)}) collective-permute-start(bf16[128,1024]{1,0:T(8,128)(2,1)S(1)} %bitcast.5), channel_id=1, source_target_pairs={{0,64},{8,72},{16,80},{24,88},{32,96},{40,104},{48,112},{56,120},{... | collective-permute-start | bytes 786440 | tf_op jit(solution)/shard_map/ppermute | solution.py:305
  23.7 41.6 %collective-permute-start.2 = (bf16[128,1024]{1,0:T(8,128)(2,1)S(1)}, bf16[128,1024]{1,0:T(8,128)(2,1)S(1)}, u32[]{:S(2)}, u32[]{:S(2)}) collective-permute-start(bf16[128,1024]{1,0:T(8,128)(2,1)S(1)} %bitcast.6), channel_id=1, source_target_pairs={{0,128},{8,136},{16,144},{24,152},{32,160},{40,168},{48,176},{56,1... | collective-permute-start | bytes 786440 | tf_op jit(solution)/shard_map/ppermute | solution.py:305
  25.3 0.7 copy-start.4
  33.1 52.5 %collective-permute-start.5 = (bf16[1056,128]{1,0:T(8,128)(2,1)S(1)}, bf16[1056,128]{1,0:T(8,128)(2,1)S(1)}, u32[]{:S(2)}, u32[]{:S(2)}) collective-permute-start(bf16[1056,128]{1,0:T(8,128)(2,1)S(1)} %attend.9), channel_id=1, source_target_pairs={{0,64},{8,72},{16,80},{24,88},{32,96},{40,104},{48,112},{56,120},{... | collective-permute-start | bytes 811016 | tf_op jit(solution)/shard_map/ppermute | solution.py:305
  65.2 20.4 %collective-permute-start.1 = (bf16[1056,128]{1,0:T(8,128)(2,1)S(1)}, bf16[1056,128]{1,0:T(8,128)(2,1)S(1)}, u32[]{:S(2)}, u32[]{:S(2)}) collective-permute-start(bf16[1056,128]{1,0:T(8,128)(2,1)S(1)} %attend.7), channel_id=1, source_target_pairs={{0,192},{8,200},{16,208},{24,216},{32,224},{40,232},{48,240},{56,2... | collective-permute-start | bytes 811016 | tf_op jit(solution)/shard_map/ppermute | solution.py:305
  82.7 7.1 %collective-permute-start.3 = (bf16[1056,128]{1,0:T(8,128)(2,1)S(1)}, bf16[1056,128]{1,0:T(8,128)(2,1)S(1)}, u32[]{:S(2)}, u32[]{:S(2)}) collective-permute-start(bf16[1056,128]{1,0:T(8,128)(2,1)S(1)} %attend.8), channel_id=1, source_target_pairs={{0,128},{8,136},{16,144},{24,152},{32,160},{40,168},{48,176},{56,1... | collective-permute-start | bytes 811016 | tf_op jit(solution)/shard_map/ppermute | solution.py:305
  91.4 12.5 %copy-start.2 = (bf16[1024,256]{1,0:T(8,128)(2,1)S(1)}, bf16[1024,256]{1,0:T(8,128)(2,1)}, u32[]{:S(2)}) copy-start(bf16[1024,256]{1,0:T(8,128)(2,1)} %refs_0_) | copy-start | bytes 1572868
  91.4 22.2 %all-to-all-start.1 = ((bf16[8,144,128]{2,1,0:T(8,128)(2,1)}), bf16[8,144,128]{2,1,0:T(8,128)(2,1)S(1)}, u32[]{:S(2)}, u32[]{:S(2)}) async-start(bf16[8,144,128]{2,1,0:T(8,128)(2,1)} %join.1), calls=%async_computation.1 | async-start | bytes 589824 | tf_op jit(solution)/shard_map/all_to_all | solution.py:301
  103.9 14.1 %collective-permute-start.8 = (bf16[1024,256]{1,0:T(8,128)(2,1)S(1)}, bf16[1024,256]{1,0:T(8,128)(2,1)S(1)}, u32[]{:S(2)}, u32[]{:S(2)}) collective-permute-start(bf16[1024,256]{1,0:T(8,128)(2,1)S(1)} %copy-done.2), channel_id=1, source_target_pairs={{0,192},{8,200},{16,208},{24,216},{32,224},{40,232},{48,240},{56,2... | collective-permute-start | bytes 1572872 | tf_op jit(solution)/shard_map/ppermute | solution.py:305
  106.8 11.3 %collective-permute-start.7 = (bf16[1024,256]{1,0:T(8,128)(2,1)S(1)}, bf16[1024,256]{1,0:T(8,128)(2,1)S(1)}, u32[]{:S(2)}, u32[]{:S(2)}) collective-permute-start(bf16[1024,256]{1,0:T(8,128)(2,1)S(1)} %copy-done.2), channel_id=1, source_target_pairs={{0,128},{8,136},{16,144},{24,152},{32,160},{40,168},{48,176},{56,1... | collective-permute-start | bytes 1572872 | tf_op jit(solution)/shard_map/ppermute | solution.py:305
  107.0 26.3 %collective-permute-start.6 = (bf16[1024,256]{1,0:T(8,128)(2,1)S(1)}, bf16[1024,256]{1,0:T(8,128)(2,1)S(1)}, u32[]{:S(2)}, u32[]{:S(2)}) collective-permute-start(bf16[1024,256]{1,0:T(8,128)(2,1)S(1)} %copy-done.2), channel_id=1, source_target_pairs={{0,64},{8,72},{16,80},{24,88},{32,96},{40,104},{48,112},{56,120},{... | collective-permute-start | bytes 1572872 | tf_op jit(solution)/shard_map/ppermute | solution.py:305
  114.6 18.7 %all-to-all-start.2 = ((bf16[8,16,1024]{2,1,0:T(8,128)(2,1)}), bf16[8,16,1024]{2,1,0:T(8,128)(2,1)S(1)}, u32[]{:S(2)}, u32[]{:S(2)}) async-start(bf16[8,16,1024]{2,1,0:T(8,128)(2,1)} %combine.1), calls=%async_computation.2 | async-start | bytes 524288 | tf_op jit(solution)/shard_map/all_to_all | solution.py:301
  133.8 3.2 %collective-permute-start.9 = (bf16[128,256]{1,0:T(8,128)(2,1)S(1)}, bf16[128,256]{1,0:T(8,128)(2,1)S(1)}, u32[]{:S(2)}, u32[]{:S(2)}) collective-permute-start(bf16[128,256]{1,0:T(8,128)(2,1)S(1)} %get-tuple-element.42), channel_id=1, source_target_pairs={{0,192},{8,200},{16,208},{24,216},{32,224},{40,232},{48,240},{56,2... | collective-permute-start | bytes 196616 | tf_op jit(solution)/shard_map/ppermute | solution.py:305
  133.9 4.7 %collective-permute-start.10 = (bf16[128,256]{1,0:T(8,128)(2,1)S(1)}, bf16[128,256]{1,0:T(8,128)(2,1)S(1)}, u32[]{:S(2)}, u32[]{:S(2)}) collective-permute-start(bf16[128,256]{1,0:T(8,128)(2,1)S(1)} %get-tuple-element.43), channel_id=1, source_target_pairs={{0,128},{8,136},{16,144},{24,152},{32,160},{40,168},{48,176},{56,1... | collective-permute-start | bytes 196616 | tf_op jit(solution)/shard_map/ppermute | solution.py:305
  134.0 5.4 %collective-permute-start.11 = (bf16[128,256]{1,0:T(8,128)(2,1)S(1)}, bf16[128,256]{1,0:T(8,128)(2,1)S(1)}, u32[]{:S(2)}, u32[]{:S(2)}) collective-permute-start(bf16[128,256]{1,0:T(8,128)(2,1)S(1)} %get-tuple-element.44), channel_id=1, source_target_pairs={{0,64},{8,72},{16,80},{24,88},{32,96},{40,104},{48,112},{56,120},{... | collective-permute-start | bytes 196616 | tf_op jit(solution)/shard_map/ppermute | solution.py:305

commit v3 on v2

--- a/solution.py
+++ b/solution.py
@@ -242,47 +242,49 @@
     )(parts)
 
 
-def project_kernel(heads_ref, *refs):
-    sides = len(refs) // 2
+def project_kernel(at_ref, heads_ref, *refs):
+    held = refs[-1]
+    ways, rows, _ = held.shape
+    weight_refs, out_refs = refs[: -1 - ways], refs[-1 - ways : -1]
     heads = heads_ref[...]
-    for weight_ref, out_ref in zip(refs[:sides], refs[sides:]):
-        out_ref[...] = jnp.dot(heads, weight_ref[...], preferred_element_type=f32).astype(bf16)
-
-
-def project(heads, weights):
+    sides = len(weight_refs)
+    for step, ref in enumerate(weight_refs):
+        column = lax.rem(at_ref[0] + sides - step, sides)
+        block = jnp.dot(heads, ref[...], preferred_element_type=f32).astype(bf16)
+        for half in range(ways // sides):
+            held[half * sides + column] = block[half * rows : (half + 1) * rows]
+    for step, ref in enumerate(out_refs):
+        ref[...] = held[lax.rem(at_ref[1] + step, ways)]
+
+
+def project(at, heads, weights, ways):
     vmem = pl.BlockSpec(memory_space=pltpu.VMEM)
-    shape = jax.ShapeDtypeStruct((heads.shape[0], weights[0].shape[1]), bf16)
+    shape = (heads.shape[0] * len(weights) // ways, weights[0].shape[1])
     return pl.pallas_call(
         project_kernel,
-        out_shape=(shape,) * len(weights),
-        out_specs=(vmem,) * len(weights),
+        out_shape=(jax.ShapeDtypeStruct(shape, bf16),) * ways,
+        in_specs=[pl.BlockSpec(memory_space=pltpu.SMEM)] + [vmem] * (1 + len(weights)),
+        out_specs=(vmem,) * ways,
+        scratch_shapes=[pltpu.VMEM((ways,) + shape, bf16)],
         compiler_params=pltpu.CompilerParams(vmem_limit_bytes=20 << 20),
         name="project",
-    )(heads, *weights)
-
-
-def place_rows_kernel(side_ref, *refs):
-    block_refs, out_ref = refs[:-1], refs[-1]
-    sides = len(block_refs)
-    rows = out_ref.shape[1]
-    per = out_ref.shape[0] // sides
-    for step, ref in enumerate(block_refs):
-        owner = lax.rem(side_ref[0] + step, sides)
-        for half in range(per):
-            out_ref[owner * per + half] = ref[half * rows : (half + 1) * rows, :]
-
-
-def place_rows(side, blocks, ways):
-    vmem = pl.BlockSpec(memory_space=pltpu.VMEM)
-    rows = len(blocks) * blocks[0].shape[0] // ways
-    return pl.pallas_call(
-        place_rows_kernel,
-        out_shape=jax.ShapeDtypeStruct((ways, rows, blocks[0].shape[1]), bf16),
-        in_specs=[pl.BlockSpec(memory_space=pltpu.SMEM)] + [vmem] * len(blocks),
-        out_specs=vmem,
-        compiler_params=pltpu.CompilerParams(vmem_limit_bytes=20 << 20),
-        name="place_rows",
-    )(side, *blocks)
+    )(at, heads, *weights)
+
+
+def total_kernel(*refs):
+    total = refs[0][...].astype(f32)
+    for ref in refs[1:-1]:
+        total += ref[...].astype(f32)
+    refs[-1][...] = total.astype(bf16)
+
+
+def total_of(blocks):
+    return pl.pallas_call(
+        total_kernel,
+        out_shape=jax.ShapeDtypeStruct(blocks[0].shape, bf16),
+        compiler_params=pltpu.CompilerParams(vmem_limit_bytes=20 << 20),
+        name="total",
+    )(*blocks)
 
 
 Y, Z = 4, 8
@@ -334,11 +336,18 @@
     weights = [out_weight] + [along_y(out_weight, step) for step in (1, 2, 3)]
     joined = across_z(join(own, parts, group, Z))
     heads = across_z(combine(joined, group)).reshape(quarter, width)
-    blocks = project(heads, weights)
-    side = (place // Z).astype(jnp.int32).reshape(1)
-    blocks = [blocks[0]] + [along_y(blocks[step], -step) for step in (1, 2, 3)]
-    scored = lax.all_to_all(place_rows(side, blocks, ways), "mp", 0, 0, tiled=True)
-    return jnp.sum(scored.astype(f32), axis=0).astype(bf16)
+    at = jnp.stack([place // Z, lax.axis_index("mp")]).astype(jnp.int32)
+    blocks = []
+    for step, block in enumerate(project(at, heads, weights, ways)):
+        pairs = []
+        for y in range(Y):
+            for z in range(Z):
+                for m in range(ways):
+                    half, column = divmod((m + step) % ways, Y)
+                    target = (column * Z + z) * ways + y * (ways // Y) + half
+                    pairs.append(((y * Z + z) * ways + m, target))
+        blocks.append(lax.ppermute(block, ("seq", "mp"), pairs))
+    return total_of(blocks)
 
 
 def solution(mesh):

time: 155 us -> 171 us (1.10)
  blocking collectives: 15.4 us -> 0 us
  Pallas kernels: 49 us -> 63.4 us
  starting transfers between devices: 49.9 us -> 64 us
  waiting for transfers between devices: 37.2 us -> 39.3 us
    ppermute x0 -> x8, starting transfers between devices: none -> 28.4 us  [on_device(): blocks.append(lax.ppermute(block, ('seq', 'mp'), pairs))]
    all_to_all x1 -> x0, blocking collectives: 15.4 us -> none  [on_device(): lax.all_to_all(place_rows(side, blocks, ways), 'mp', 0, 0, tiled=True)]
    ppermute x12 -> x9, starting transfers between devices: 25 us -> 11.6 us  [along_y(): return lax.ppermute(array, 'seq', pairs)]
    pallas_call x5, Pallas kernels: 44.4 us -> 57.7 us  [attend(): pl.pallas_call(lambda *refs: attend_kernel(group, min(4, group), 512, *re...]
    ppermute x0 -> x8, waiting for transfers between devices: none -> 6.36 us  [on_device(): blocks.append(lax.ppermute(block, ('seq', 'mp'), pairs))]
    ppermute x12 -> x9, waiting for transfers between devices: 23.5 us -> 18.9 us  [along_y(): return lax.ppermute(array, 'seq', pairs)]
  transfers between devices with their start and end apart: 15 -> 20, of which waited for: 7 -> 6; matrix products, arithmetic and copies ran while one was open for 0% -> 0% of each run, Pallas kernels for 30% -> 35%
where the time goes in v3:
time: 171 us; the launch traced here: 170 us
  starting transfers between devices  64 us (37%)
  Pallas kernels  63.4 us (37%)
  waiting for transfers between devices  39.3 us (23%)
  local copies, waits for them, and re-layouts  2.87 us (2%)
    pallas_call x5, Pallas kernels, attend(): pl.pallas_call(lambda *refs: attend_kernel(group, min(4, group), 512, *re...  57.7 us
    ppermute x8, starting transfers between devices, on_device(): blocks.append(lax.ppermute(block, ('seq', 'mp'), pairs))  28.4 us
    all_to_all x3, starting transfers between devices, across_z(): lax.all_to_all(array, 'seq', 0, 0, axis_index_groups=along_z, tiled=True)  24 us
    ppermute x9, waiting for transfers between devices, along_y(): return lax.ppermute(array, 'seq', pairs)  18.9 us
    all_to_all x3, waiting for transfers between devices, across_z(): lax.all_to_all(array, 'seq', 0, 0, axis_index_groups=along_z, tiled=True)  14 us
    ppermute x9, starting transfers between devices, along_y(): return lax.ppermute(array, 'seq', pairs)  11.6 us
    ppermute x8, waiting for transfers between devices, on_device(): blocks.append(lax.ppermute(block, ('seq', 'mp'), pairs))  6.36 us
  transfers between devices with their start and end apart: 20, of which 6 were waited for; matrix products, arithmetic and copies ran while one was open for 0% of the time, Pallas kernels for 35%

profile of v3, /device:TPU:1, one launch (start us, length us, event | category | flops | bytes accessed | tf_op | source)
XLA Modules:
  0.0 170.0 jit_solution(7544783234551846172)
XLA Ops:
  0.0 0.8 copy-done.5
  0.8 0.8 replicate.1
  1.5 0.0 copy-start.6
  1.5 0.0 copy-start.3
  1.5 9.0 %all-to-all-start = ((bf16[8,16,1024]{2,1,0:T(8,128)(2,1)}), bf16[8,16,1024]{2,1,0:T(8,128)(2,1)S(1)}, u32[]{:S(2)}, u32[]{:S(2)}) async-start(bf16[8,16,1024]{2,1,0:T(8,128)(2,1)} %replicate.1), calls=%async_computation | async-start | bytes 524288 | tf_op jit(solution)/shard_map/all_to_all | solution.py:303
  10.7 0.1 dynamic_slice.15
  10.8 1.3 copy-done.1
  12.1 0.8 prepare.1
  12.9 0.1 fusion.1
  13.0 8.0 %all-to-all-done = bf16[8,16,1024]{2,1,0:T(8,128)(2,1)S(1)} async-done(((bf16[8,16,1024]{2,1,0:T(8,128)(2,1)}), bf16[8,16,1024]{2,1,0:T(8,128)(2,1)S(1)}, u32[]{:S(2)}, u32[]{:S(2)}) %all-to-all-start) | async-done | bytes 262176 | tf_op jit(solution)/shard_map/all_to_all | solution.py:303
  20.9 2.7 %collective-permute-start.4 = (bf16[128,1024]{1,0:T(8,128)(2,1)S(1)}, bf16[128,1024]{1,0:T(8,128)(2,1)S(1)}, u32[]{:S(2)}, u32[]{:S(2)}) collective-permute-start(bf16[128,1024]{1,0:T(8,128)(2,1)S(1)} %bitcast.5), channel_id=1, source_target_pairs={{0,192},{8,200},{16,208},{24,216},{32,224},{40,232},{48,240},{56,2... | collective-permute-start | bytes 786440 | tf_op jit(solution)/shard_map/ppermute | solution.py:307
  23.7 1.6 collective-permute-start.2
  25.4 0.7 copy-done.4
  26.0 2.7 %attend.5.refs_0_ = bf16[528,128]{1,0:T(8,128)(2,1)S(1)} custom-call(bf16[128,512]{1,0:T(8,128)(2,1)S(1)} %get-tuple-element.54.refs_0_, bf16[4096,128]{1,0:T(8,128)(2,1)S(1)} %copy-done, bf16[128,4096]{1,0:T(8,128)(2,1)S(1)} %get-tuple-element.36.refs_2_, bf16[16,128]{1,0:T(8,128)(2,1)S(1)} %copy-done.4, bf16[16,128]{1,0:T(8,128)(2,1)S(1)} %copy-done.3, ...), custom_call_target="tpu_custom_call" | custom-call | tf_op jit(solution)/shard_map/attend/pallas_call | solution.py:161
  28.7 17.4 %attend.9 = bf16[1056,128]{1,0:T(8,128)(2,1)S(1)} custom-call(bf16[128,1024]{1,0:T(8,128)(2,1)S(1)} %collective-permute-done.4.refs_0_, bf16[4096,128]{1,0:T(8,128)(2,1)S(1)} %copy-done, bf16[128,4096]{1,0:T(8,128)(2,1)S(1)} %get-tuple-element.36.refs_2_, bf16[16,128]{1,0:T(8,128)(2,1)S(1)} %copy-done.4, bf16[16,128]{1,0:T(8,128)(2,1)S(1)} %copy-done.3, ...), custom_call_target="tpu_custom_call" | custom-call | tf_op jit(solution)/shard_map/attend/pallas_call | solution.py:161
  46.2 1.9 %collective-permute-start.5 = (bf16[1056,128]{1,0:T(8,128)(2,1)S(1)}, bf16[1056,128]{1,0:T(8,128)(2,1)S(1)}, u32[]{:S(2)}, u32[]{:S(2)}) collective-permute-start(bf16[1056,128]{1,0:T(8,128)(2,1)S(1)} %attend.9), channel_id=1, source_target_pairs={{0,64},{8,72},{16,80},{24,88},{32,96},{40,104},{48,112},{56,120},{... | collective-permute-start | bytes 811016 | tf_op jit(solution)/shard_map/ppermute | solution.py:307
  48.0 17.4 %attend.7 = bf16[1056,128]{1,0:T(8,128)(2,1)S(1)} custom-call(bf16[128,1024]{1,0:T(8,128)(2,1)S(1)} %collective-permute-done.refs_0_, bf16[4096,128]{1,0:T(8,128)(2,1)S(1)} %copy-done, bf16[128,4096]{1,0:T(8,128)(2,1)S(1)} %get-tuple-element.36.refs_2_, bf16[16,128]{1,0:T(8,128)(2,1)S(1)} %copy-done.4, bf16[16,128]{1,0:T(8,128)(2,1)S(1)} %copy-done.3, ...), custom_call_target="tpu_custom_call" | custom-call | tf_op jit(solution)/shard_map/attend/pallas_call | solution.py:161
  65.5 1.1 collective-permute-start.1
  66.6 0.0 collective-permute-done.2.refs_0_
  66.6 17.4 %attend.8 = bf16[1056,128]{1,0:T(8,128)(2,1)S(1)} custom-call(bf16[128,1024]{1,0:T(8,128)(2,1)S(1)} %collective-permute-done.2.refs_0_, bf16[4096,128]{1,0:T(8,128)(2,1)S(1)} %copy-done, bf16[128,4096]{1,0:T(8,128)(2,1)S(1)} %get-tuple-element.36.refs_2_, bf16[16,128]{1,0:T(8,128)(2,1)S(1)} %copy-done.4, bf16[16,128]{1,0:T(8,128)(2,1)S(1)} %copy-done.3, ...), custom_call_target="tpu_custom_call" | custom-call | tf_op jit(solution)/shard_map/attend/pallas_call | solution.py:161
  84.0 0.3 collective-permute-start.3
  84.3 2.7 %attend.6.refs_1_ = bf16[528,128]{1,0:T(8,128)(2,1)S(1)} custom-call(bf16[128,512]{1,0:T(8,128)(2,1)S(1)} %get-tuple-element.53.refs_0_, bf16[4096,128]{1,0:T(8,128)(2,1)S(1)} %copy-done, bf16[128,4096]{1,0:T(8,128)(2,1)S(1)} %get-tuple-element.36.refs_2_, bf16[16,128]{1,0:T(8,128)(2,1)S(1)} %copy-done.4, bf16[16,128]{1,0:T(8,128)(2,1)S(1)} %copy-done.3, ...), custom_call_target="tpu_custom_call" | custom-call | tf_op jit(solution)/shard_map/attend/pallas_call | solution.py:161
  87.0 0.0 collective-permute-done.5.refs_4_
  87.1 4.1 %collective-permute-done.3.refs_3_ = bf16[1056,128]{1,0:T(8,128)(2,1)S(1)} collective-permute-done((bf16[1056,128]{1,0:T(8,128)(2,1)S(1)}, bf16[1056,128]{1,0:T(8,128)(2,1)S(1)}, u32[]{:S(2)}, u32[]{:S(2)}) %collective-permute-start.3) | collective-permute-done | bytes 270368 | tf_op jit(solution)/shard_map/ppermute | solution.py:307
  91.1 1.5 join.1
  92.7 11.6 %all-to-all-start.1 = ((bf16[8,144,128]{2,1,0:T(8,128)(2,1)}), bf16[8,144,128]{2,1,0:T(8,128)(2,1)S(1)}, u32[]{:S(2)}, u32[]{:S(2)}) async-start(bf16[8,144,128]{2,1,0:T(8,128)(2,1)} %join.1), calls=%async_computation.1 | async-start | bytes 589824 | tf_op jit(solution)/shard_map/all_to_all | solution.py:303
  104.2 3.0 %collective-permute-start.8 = (bf16[1024,256]{1,0:T(8,128)(2,1)S(1)}, bf16[1024,256]{1,0:T(8,128)(2,1)S(1)}, u32[]{:S(2)}, u32[]{:S(2)}) collective-permute-start(bf16[1024,256]{1,0:T(8,128)(2,1)S(1)} %copy-done.2), channel_id=1, source_target_pairs={{0,192},{8,200},{16,208},{24,216},{32,224},{40,232},{48,240},{56,2... | collective-permute-start | bytes 1572872 | tf_op jit(solution)/shard_map/ppermute | solution.py:307
  107.2 0.1 collective-permute-start.7
  107.4 0.8 collective-permute-start.6
  108.1 6.0 %all-to-all-done.1.refs_0_ = bf16[8,144,128]{2,1,0:T(8,128)(2,1)S(1)} async-done(((bf16[8,144,128]{2,1,0:T(8,128)(2,1)}), bf16[8,144,128]{2,1,0:T(8,128)(2,1)S(1)}, u32[]{:S(2)}, u32[]{:S(2)}) %all-to-all-start.1) | async-done | bytes 294944 | tf_op jit(solution)/shard_map/all_to_all | solution.py:303
  114.2 1.0 combine.1
  115.2 3.4 %all-to-all-start.2 = ((bf16[8,16,1024]{2,1,0:T(8,128)(2,1)}), bf16[8,16,1024]{2,1,0:T(8,128)(2,1)S(1)}, u32[]{:S(2)}, u32[]{:S(2)}) async-start(bf16[8,16,1024]{2,1,0:T(8,128)(2,1)} %combine.1), calls=%async_computation.2 | async-start | bytes 524288 | tf_op jit(solution)/shard_map/all_to_all | solution.py:303
  118.6 0.1 pad_add_fusion.at_ref
  118.7 0.0 collective-permute-done.8.refs_3_
  118.7 0.0 collective-permute-done.7.refs_2_
  118.7 14.8 %collective-permute-done.6.refs_1_ = bf16[1024,256]{1,0:T(8,128)(2,1)S(1)} collective-permute-done((bf16[1024,256]{1,0:T(8,128)(2,1)S(1)}, bf16[1024,256]{1,0:T(8,128)(2,1)S(1)}, u32[]{:S(2)}, u32[]{:S(2)}) %collective-permute-start.6) | collective-permute-done | bytes 524320 | tf_op jit(solution)/shard_map/ppermute | solution.py:307
  133.5 1.0 project.1
  134.5 1.9 %collective-permute-start.9 = (bf16[64,256]{1,0:T(8,128)(2,1)S(1)}, bf16[64,256]{1,0:T(8,128)(2,1)S(1)}, u32[]{:S(2)}, u32[]{:S(2)}) collective-permute-start(bf16[64,256]{1,0:T(8,128)(2,1)S(1)} %get-tuple-element.45), channel_id=1, source_target_pairs={{0,0},{1,64},{2,128},{3,192},{4,1},{5,65},{6,129},{7,193},{8,8},{9... | collective-permute-start | bytes 98312 | tf_op jit(solution)/shard_map/ppermute | solution.py:349
  136.5 8.1 %collective-permute-start.10 = (bf16[64,256]{1,0:T(8,128)(2,1)S(1)}, bf16[64,256]{1,0:T(8,128)(2,1)S(1)}, u32[]{:S(2)}, u32[]{:S(2)}) collective-permute-start(bf16[64,256]{1,0:T(8,128)(2,1)S(1)} %get-tuple-element.46), channel_id=1, source_target_pairs={{0,64},{1,128},{2,192},{3,1},{4,65},{5,129},{6,193},{7,0},{8,72},{... | collective-permute-start | bytes 98312 | tf_op jit(solution)/shard_map/ppermute | solution.py:349
  144.6 1.9 %collective-permute-start.11 = (bf16[64,256]{1,0:T(8,128)(2,1)S(1)}, bf16[64,256]{1,0:T(8,128)(2,1)S(1)}, u32[]{:S(2)}, u32[]{:S(2)}) collective-permute-start(bf16[64,256]{1,0:T(8,128)(2,1)S(1)} %get-tuple-element.47), channel_id=1, source_target_pairs={{0,128},{1,192},{2,1},{3,65},{4,129},{5,193},{6,0},{7,64},{8,136},... | collective-permute-start | bytes 98312 | tf_op jit(solution)/shard_map/ppermute | solution.py:349
  146.5 0.7 collective-permute-start.12
  147.2 2.6 %collective-permute-start.13 = (bf16[64,256]{1,0:T(8,128)(2,1)S(1)}, bf16[64,256]{1,0:T(8,128)(2,1)S(1)}, u32[]{:S(2)}, u32[]{:S(2)}) collective-permute-start(bf16[64,256]{1,0:T(8,128)(2,1)S(1)} %get-tuple-element.49), channel_id=1, source_target_pairs={{0,1},{1,65},{2,129},{3,193},{4,0},{5,64},{6,128},{7,192},{8,9},{9... | collective-permute-start | bytes 98312 | tf_op jit(solution)/shard_map/ppermute | solution.py:349
  149.8 6.8 %collective-permute-start.14 = (bf16[64,256]{1,0:T(8,128)(2,1)S(1)}, bf16[64,256]{1,0:T(8,128)(2,1)S(1)}, u32[]{:S(2)}, u32[]{:S(2)}) collective-permute-start(bf16[64,256]{1,0:T(8,128)(2,1)S(1)} %get-tuple-element.50), channel_id=1, source_target_pairs={{0,65},{1,129},{2,193},{3,0},{4,64},{5,128},{6,192},{7,1},{8,73},{... | collective-permute-start | bytes 98312 | tf_op jit(solution)/shard_map/ppermute | solution.py:349
  156.7 4.4 %collective-permute-start.15 = (bf16[64,256]{1,0:T(8,128)(2,1)S(1)}, bf16[64,256]{1,0:T(8,128)(2,1)S(1)}, u32[]{:S(2)}, u32[]{:S(2)}) collective-permute-start(bf16[64,256]{1,0:T(8,128)(2,1)S(1)} %get-tuple-element.51), channel_id=1, source_target_pairs={{0,129},{1,193},{2,0},{3,64},{4,128},{5,192},{6,1},{7,65},{8,137},... | collective-permute-start | bytes 98312 | tf_op jit(solution)/shard_map/ppermute | solution.py:349
  161.1 1.9 %collective-permute-start.16 = (bf16[64,256]{1,0:T(8,128)(2,1)S(1)}, bf16[64,256]{1,0:T(8,128)(2,1)S(1)}, u32[]{:S(2)}, u32[]{:S(2)}) collective-permute-start(bf16[64,256]{1,0:T(8,128)(2,1)S(1)} %get-tuple-element.52), channel_id=1, source_target_pairs={{0,193},{1,0},{2,64},{3,128},{4,192},{5,1},{6,65},{7,129},{8,201},... | collective-permute-start | bytes 98312 | tf_op jit(solution)/shard_map/ppermute | solution.py:349
  163.0 0.1 collective-permute-done.15.refs_6_
  163.1 6.3 %collective-permute-done.16.refs_7_ = bf16[64,256]{1,0:T(8,128)(2,1)S(1)} collective-permute-done((bf16[64,256]{1,0:T(8,128)(2,1)S(1)}, bf16[64,256]{1,0:T(8,128)(2,1)S(1)}, u32[]{:S(2)}, u32[]{:S(2)}) %collective-permute-start.16) | collective-permute-done | bytes 32800 | tf_op jit(solution)/shard_map/ppermute | solution.py:349
  169.4 0.7 total.1
  (23 shorter events, 0.1 us)
Async XLA Ops:
  0.0 0.8 copy-start.5
  1.5 9.2 %copy-start.6 = (s32[512]{0:T(512)S(1)}, s32[512]{0:T(512)}, u32[]{:S(2)}) copy-start(s32[512]{0:T(512)} %param.12) | copy-start | bytes 6148
  1.5 9.2 %copy-start.3 = (bf16[16,128]{1,0:T(8,128)(2,1)S(1)}, bf16[16,128]{1,0:T(8,128)(2,1)}, u32[]{:S(2)}) copy-start(bf16[16,128]{1,0:T(8,128)(2,1)} %refs_4_.9) | copy-start | bytes 12292
  1.5 19.4 %all-to-all-start = ((bf16[8,16,1024]{2,1,0:T(8,128)(2,1)}), bf16[8,16,1024]{2,1,0:T(8,128)(2,1)S(1)}, u32[]{:S(2)}, u32[]{:S(2)}) async-start(bf16[8,16,1024]{2,1,0:T(8,128)(2,1)} %replicate.1), calls=%async_computation | async-start | bytes 524288 | tf_op jit(solution)/shard_map/all_to_all | solution.py:303
  10.6 14.8 %copy-start = (bf16[4096,128]{1,0:T(8,128)(2,1)S(1)}, bf16[4096,128]{1,0:T(8,128)(2,1)}, u32[]{:S(2)}) copy-start(bf16[4096,128]{1,0:T(8,128)(2,1)} %refs_1_.9) | copy-start | bytes 3145732
  10.8 1.3 copy-start.1
  20.9 7.8 %collective-permute-start.4 = (bf16[128,1024]{1,0:T(8,128)(2,1)S(1)}, bf16[128,1024]{1,0:T(8,128)(2,1)S(1)}, u32[]{:S(2)}, u32[]{:S(2)}) collective-permute-start(bf16[128,1024]{1,0:T(8,128)(2,1)S(1)} %bitcast.5), channel_id=1, source_target_pairs={{0,192},{8,200},{16,208},{24,216},{32,224},{40,232},{48,240},{56,2... | collective-permute-start | bytes 786440 | tf_op jit(solution)/shard_map/ppermute | solution.py:307
  23.7 24.3 %collective-permute-start = (bf16[128,1024]{1,0:T(8,128)(2,1)S(1)}, bf16[128,1024]{1,0:T(8,128)(2,1)S(1)}, u32[]{:S(2)}, u32[]{:S(2)}) collective-permute-start(bf16[128,1024]{1,0:T(8,128)(2,1)S(1)} %bitcast.6), channel_id=1, source_target_pairs={{0,64},{8,72},{16,80},{24,88},{32,96},{40,104},{48,112},{56,120},{... | collective-permute-start | bytes 786440 | tf_op jit(solution)/shard_map/ppermute | solution.py:307
  23.7 42.9 %collective-permute-start.2 = (bf16[128,1024]{1,0:T(8,128)(2,1)S(1)}, bf16[128,1024]{1,0:T(8,128)(2,1)S(1)}, u32[]{:S(2)}, u32[]{:S(2)}) collective-permute-start(bf16[128,1024]{1,0:T(8,128)(2,1)S(1)} %bitcast.7), channel_id=1, source_target_pairs={{0,128},{8,136},{16,144},{24,152},{32,160},{40,168},{48,176},{56,1... | collective-permute-start | bytes 786440 | tf_op jit(solution)/shard_map/ppermute | solution.py:307
  25.3 0.7 copy-start.4
  46.2 40.9 %collective-permute-start.5 = (bf16[1056,128]{1,0:T(8,128)(2,1)S(1)}, bf16[1056,128]{1,0:T(8,128)(2,1)S(1)}, u32[]{:S(2)}, u32[]{:S(2)}) collective-permute-start(bf16[1056,128]{1,0:T(8,128)(2,1)S(1)} %attend.9), channel_id=1, source_target_pairs={{0,64},{8,72},{16,80},{24,88},{32,96},{40,104},{48,112},{56,120},{... | collective-permute-start | bytes 811016 | tf_op jit(solution)/shard_map/ppermute | solution.py:307
  65.5 21.6 %collective-permute-start.1 = (bf16[1056,128]{1,0:T(8,128)(2,1)S(1)}, bf16[1056,128]{1,0:T(8,128)(2,1)S(1)}, u32[]{:S(2)}, u32[]{:S(2)}) collective-permute-start(bf16[1056,128]{1,0:T(8,128)(2,1)S(1)} %attend.7), channel_id=1, source_target_pairs={{0,192},{8,200},{16,208},{24,216},{32,224},{40,232},{48,240},{56,2... | collective-permute-start | bytes 811016 | tf_op jit(solution)/shard_map/ppermute | solution.py:307
  84.0 7.1 %collective-permute-start.3 = (bf16[1056,128]{1,0:T(8,128)(2,1)S(1)}, bf16[1056,128]{1,0:T(8,128)(2,1)S(1)}, u32[]{:S(2)}, u32[]{:S(2)}) collective-permute-start(bf16[1056,128]{1,0:T(8,128)(2,1)S(1)} %attend.8), channel_id=1, source_target_pairs={{0,128},{8,136},{16,144},{24,152},{32,160},{40,168},{48,176},{56,1... | collective-permute-start | bytes 811016 | tf_op jit(solution)/shard_map/ppermute | solution.py:307
  92.7 11.6 %copy-start.2 = (bf16[1024,256]{1,0:T(8,128)(2,1)S(1)}, bf16[1024,256]{1,0:T(8,128)(2,1)}, u32[]{:S(2)}) copy-start(bf16[1024,256]{1,0:T(8,128)(2,1)} %refs_0_) | copy-start | bytes 1572868
  92.7 21.5 %all-to-all-start.1 = ((bf16[8,144,128]{2,1,0:T(8,128)(2,1)}), bf16[8,144,128]{2,1,0:T(8,128)(2,1)S(1)}, u32[]{:S(2)}, u32[]{:S(2)}) async-start(bf16[8,144,128]{2,1,0:T(8,128)(2,1)} %join.1), calls=%async_computation.1 | async-start | bytes 589824 | tf_op jit(solution)/shard_map/all_to_all | solution.py:303
  104.2 14.5 %collective-permute-start.8 = (bf16[1024,256]{1,0:T(8,128)(2,1)S(1)}, bf16[1024,256]{1,0:T(8,128)(2,1)S(1)}, u32[]{:S(2)}, u32[]{:S(2)}) collective-permute-start(bf16[1024,256]{1,0:T(8,128)(2,1)S(1)} %copy-done.2), channel_id=1, source_target_pairs={{0,192},{8,200},{16,208},{24,216},{32,224},{40,232},{48,240},{56,2... | collective-permute-start | bytes 1572872 | tf_op jit(solution)/shard_map/ppermute | solution.py:307
  107.2 11.5 %collective-permute-start.7 = (bf16[1024,256]{1,0:T(8,128)(2,1)S(1)}, bf16[1024,256]{1,0:T(8,128)(2,1)S(1)}, u32[]{:S(2)}, u32[]{:S(2)}) collective-permute-start(bf16[1024,256]{1,0:T(8,128)(2,1)S(1)} %copy-done.2), channel_id=1, source_target_pairs={{0,128},{8,136},{16,144},{24,152},{32,160},{40,168},{48,176},{56,1... | collective-permute-start | bytes 1572872 | tf_op jit(solution)/shard_map/ppermute | solution.py:307
  107.4 26.1 %collective-permute-start.6 = (bf16[1024,256]{1,0:T(8,128)(2,1)S(1)}, bf16[1024,256]{1,0:T(8,128)(2,1)S(1)}, u32[]{:S(2)}, u32[]{:S(2)}) collective-permute-start(bf16[1024,256]{1,0:T(8,128)(2,1)S(1)} %copy-done.2), channel_id=1, source_target_pairs={{0,64},{8,72},{16,80},{24,88},{32,96},{40,104},{48,112},{56,120},{... | collective-permute-start | bytes 1572872 | tf_op jit(solution)/shard_map/ppermute | solution.py:307
  115.2 18.3 %all-to-all-start.2 = ((bf16[8,16,1024]{2,1,0:T(8,128)(2,1)}), bf16[8,16,1024]{2,1,0:T(8,128)(2,1)S(1)}, u32[]{:S(2)}, u32[]{:S(2)}) async-start(bf16[8,16,1024]{2,1,0:T(8,128)(2,1)} %combine.1), calls=%async_computation.2 | async-start | bytes 524288 | tf_op jit(solution)/shard_map/all_to_all | solution.py:303
  134.5 15.3 %collective-permute-start.9 = (bf16[64,256]{1,0:T(8,128)(2,1)S(1)}, bf16[64,256]{1,0:T(8,128)(2,1)S(1)}, u32[]{:S(2)}, u32[]{:S(2)}) collective-permute-start(bf16[64,256]{1,0:T(8,128)(2,1)S(1)} %get-tuple-element.45), channel_id=1, source_target_pairs={{0,0},{1,64},{2,128},{3,192},{4,1},{5,65},{6,129},{7,193},{8,8},{9... | collective-permute-start | bytes 98312 | tf_op jit(solution)/shard_map/ppermute | solution.py:349
  136.5 20.2 %collective-permute-start.10 = (bf16[64,256]{1,0:T(8,128)(2,1)S(1)}, bf16[64,256]{1,0:T(8,128)(2,1)S(1)}, u32[]{:S(2)}, u32[]{:S(2)}) collective-permute-start(bf16[64,256]{1,0:T(8,128)(2,1)S(1)} %get-tuple-element.46), channel_id=1, source_target_pairs={{0,64},{1,128},{2,192},{3,1},{4,65},{5,129},{6,193},{7,0},{8,72},{... | collective-permute-start | bytes 98312 | tf_op jit(solution)/shard_map/ppermute | solution.py:349
  144.6 16.5 %collective-permute-start.11 = (bf16[64,256]{1,0:T(8,128)(2,1)S(1)}, bf16[64,256]{1,0:T(8,128)(2,1)S(1)}, u32[]{:S(2)}, u32[]{:S(2)}) collective-permute-start(bf16[64,256]{1,0:T(8,128)(2,1)S(1)} %get-tuple-element.47), channel_id=1, source_target_pairs={{0,128},{1,192},{2,1},{3,65},{4,129},{5,193},{6,0},{7,64},{8,136},... | collective-permute-start | bytes 98312 | tf_op jit(solution)/shard_map/ppermute | solution.py:349
  146.5 16.5 %collective-permute-start.12 = (bf16[64,256]{1,0:T(8,128)(2,1)S(1)}, bf16[64,256]{1,0:T(8,128)(2,1)S(1)}, u32[]{:S(2)}, u32[]{:S(2)}) collective-permute-start(bf16[64,256]{1,0:T(8,128)(2,1)S(1)} %get-tuple-element.48), channel_id=1, source_target_pairs={{0,192},{1,1},{2,65},{3,129},{4,193},{5,0},{6,64},{7,128},{8,200},... | collective-permute-start | bytes 98312 | tf_op jit(solution)/shard_map/ppermute | solution.py:349
  147.2 15.8 %collective-permute-start.13 = (bf16[64,256]{1,0:T(8,128)(2,1)S(1)}, bf16[64,256]{1,0:T(8,128)(2,1)S(1)}, u32[]{:S(2)}, u32[]{:S(2)}) collective-permute-start(bf16[64,256]{1,0:T(8,128)(2,1)S(1)} %get-tuple-element.49), channel_id=1, source_target_pairs={{0,1},{1,65},{2,129},{3,193},{4,0},{5,64},{6,128},{7,192},{8,9},{9... | collective-permute-start | bytes 98312 | tf_op jit(solution)/shard_map/ppermute | solution.py:349
  149.8 13.2 %collective-permute-start.14 = (bf16[64,256]{1,0:T(8,128)(2,1)S(1)}, bf16[64,256]{1,0:T(8,128)(2,1)S(1)}, u32[]{:S(2)}, u32[]{:S(2)}) collective-permute-start(bf16[64,256]{1,0:T(8,128)(2,1)S(1)} %get-tuple-element.50), channel_id=1, source_target_pairs={{0,65},{1,129},{2,193},{3,0},{4,64},{5,128},{6,192},{7,1},{8,73},{... | collective-permute-start | bytes 98312 | tf_op jit(solution)/shard_map/ppermute | solution.py:349
  156.7 6.5 %collective-permute-start.15 = (bf16[64,256]{1,0:T(8,128)(2,1)S(1)}, bf16[64,256]{1,0:T(8,128)(2,1)S(1)}, u32[]{:S(2)}, u32[]{:S(2)}) collective-permute-start(bf16[64,256]{1,0:T(8,128)(2,1)S(1)} %get-tuple-element.51), channel_id=1, source_target_pairs={{0,129},{1,193},{2,0},{3,64},{4,128},{5,192},{6,1},{7,65},{8,137},... | collective-permute-start | bytes 98312 | tf_op jit(solution)/shard_map/ppermute | solution.py:349
  161.1 8.3 %collective-permute-start.16 = (bf16[64,256]{1,0:T(8,128)(2,1)S(1)}, bf16[64,256]{1,0:T(8,128)(2,1)S(1)}, u32[]{:S(2)}, u32[]{:S(2)}) collective-permute-start(bf16[64,256]{1,0:T(8,128)(2,1)S(1)} %get-tuple-element.52), channel_id=1, source_target_pairs={{0,193},{1,0},{2,64},{3,128},{4,192},{5,1},{6,65},{7,129},{8,201},... | collective-permute-start | bytes 98312 | tf_op jit(solution)/shard_map/ppermute | solution.py:349

commit v4 on v2

--- a/solution.py
+++ b/solution.py
@@ -22,26 +22,31 @@
     return high, middle, rest - middle
 
 
-def prepare_kernel(v_ref, rv_ref, vt_ref, fact_ref):
-    v = v_ref[...]
+def prepare_kernel(v_ref, rk_ref, rv_ref, vt_ref, rk_out_ref, rvt_ref, fact_ref):
+    v, rv = v_ref[...], rv_ref[...]
     vt_ref[...] = v.T
+    rk_out_ref[...] = rk_ref[...]
+    rvt_ref[...] = rv.T
     fact_ref[0, 0] = jnp.maximum(
-        jnp.max(jnp.abs(v.astype(f32))), jnp.max(jnp.abs(rv_ref[...].astype(f32)))
-    )
-
-
-def prepare(values, own_values):
+        jnp.max(jnp.abs(v.astype(f32))), jnp.max(jnp.abs(rv.astype(f32)))
+    )
+
+
+def prepare(values, own_keys, own_values):
     vmem = pl.BlockSpec(memory_space=pltpu.VMEM)
+    own = own_keys.shape[0]
     return pl.pallas_call(
         prepare_kernel,
         out_shape=(
             pltpu.VMEM((HD, values.shape[0]), bf16),
+            pltpu.VMEM((own, HD), bf16),
+            pltpu.VMEM((HD, own), bf16),
             jax.ShapeDtypeStruct((1, 1), f32),
         ),
-        out_specs=(vmem, pl.BlockSpec(memory_space=pltpu.SMEM)),
+        out_specs=(vmem, vmem, vmem, pl.BlockSpec(memory_space=pltpu.SMEM)),
         compiler_params=pltpu.CompilerParams(vmem_limit_bytes=20 << 20),
         name="prepare",
-    )(values, own_values)
+    )(values, own_keys, own_values)
 
 
 def replicate_kernel(x_ref, out_ref, sems):
@@ -58,7 +63,7 @@
     return pl.pallas_call(
         replicate_kernel,
         out_shape=jax.ShapeDtypeStruct((count,) + array.shape, array.dtype),
-        in_specs=[pl.BlockSpec(memory_space=pltpu.VMEM)],
+        in_specs=[pl.BlockSpec(memory_space=pltpu.HBM)],
         out_specs=pl.BlockSpec(memory_space=pl.ANY),
         scratch_shapes=[pltpu.SemaphoreType.DMA((count,))],
         compiler_params=pltpu.CompilerParams(vmem_limit_bytes=20 << 20),
@@ -67,7 +72,7 @@
 
 
 def attend_kernel(
-    group, stack, key_block, q_ref, k_ref, vt_ref, rk_ref, rv_ref, bias_ref, fact_ref, out_ref,
+    lead, group, stack, key_block, q_ref, k_ref, vt_ref, rk_ref, rvt_ref, bias_ref, fact_ref, out_ref,
     logs_ref,
 ):
     tokens = q_ref.shape[0]
@@ -96,12 +101,15 @@
     def fold(weights):
         return jnp.sum(weights.reshape(-1, 8, weights.shape[1]), axis=0)
 
-    own_columns = rv_ref[...].T
     everything, logs = [], []
     bias = jnp.concatenate([bias_ref[...]] * stack, axis=1)
     for first in range(0, group, stack):
         q = jnp.concatenate(
-            [q_ref[:, head * HD : (head + 1) * HD] for head in range(first, first + stack)], axis=0
+            [
+                q_ref[:, head * HD : (head + 1) * HD]
+                for head in range(lead + first, lead + first + stack)
+            ],
+            axis=0,
         )
         total, sums = None, None
         now = scores(k_ref[:key_block, :], q)
@@ -117,7 +125,7 @@
             sums = fold(weights) if sums is None else sums + fold(weights)
             now = following
         weights = jnp.exp2(now)
-        total += product(own_columns, weights)
+        total += product(rvt_ref[...], weights)
         sums = jnp.sum(sums + fold(weights), axis=0, keepdims=True)
         everything.append(sums)
         log = jnp.log2(sums)
@@ -137,14 +145,14 @@
     def _():
         @pl.loop(0, group)
         def _(head):
-            q = q_ref[:, pl.ds(pl.multiple_of(head * HD, HD), HD)]
+            q = q_ref[:, pl.ds(pl.multiple_of((lead + head) * HD, HD), HD)]
             mine = scores(rk_ref[...], q) + bias_ref[...]
             rest = scores(k_ref[...], q)
             top = jnp.maximum(
                 jnp.max(mine, axis=0, keepdims=True), jnp.max(rest, axis=0, keepdims=True)
             )
             mine, rest = jnp.exp2(mine - top), jnp.exp2(rest - top)
-            total = product(own_columns, mine) + product(vt_ref[...], rest)
+            total = product(rvt_ref[...], mine) + product(vt_ref[...], rest)
             sums = jnp.sum(mine, axis=0, keepdims=True) + jnp.sum(rest, axis=0, keepdims=True)
             logs_ref[pl.ds(head, 1), :] = jnp.log2(sums) + top
             out_ref[pl.ds(pl.multiple_of(head * tokens, tokens), tokens), :] = result_of(
@@ -154,19 +162,18 @@
         logs_rows([logs_ref[...]])
 
 
-def attend(queries, keys, columns, own_keys, own_values, bias, fact):
-    tokens, width = queries.shape
-    group = width // HD
+def attend(lead, group, queries, keys, columns, own_keys, own_columns, bias, fact):
+    tokens = queries.shape[0]
     vmem = pl.BlockSpec(memory_space=pltpu.VMEM)
     return pl.pallas_call(
-        lambda *refs: attend_kernel(group, min(4, group), 512, *refs),
+        lambda *refs: attend_kernel(lead, group, min(4, group), 512, *refs),
         out_shape=jax.ShapeDtypeStruct((group * (tokens + DEPTH), HD), bf16),
         in_specs=[vmem] * 6 + [pl.BlockSpec(memory_space=pltpu.SMEM)],
         out_specs=vmem,
         scratch_shapes=[pltpu.VMEM((group, tokens), f32)],
         compiler_params=pltpu.CompilerParams(vmem_limit_bytes=20 << 20),
         name="attend",
-    )(queries, keys, columns, own_keys, own_values, bias, fact)
+    )(queries, keys, columns, own_keys, own_columns, bias, fact)
 
 
 def join_kernel(group, halves, *refs):
@@ -242,49 +249,6 @@
     )(parts)
 
 
-def project_kernel(heads_ref, *refs):
-    sides = len(refs) // 2
-    heads = heads_ref[...]
-    for weight_ref, out_ref in zip(refs[:sides], refs[sides:]):
-        out_ref[...] = jnp.dot(heads, weight_ref[...], preferred_element_type=f32).astype(bf16)
-
-
-def project(heads, weights):
-    vmem = pl.BlockSpec(memory_space=pltpu.VMEM)
-    shape = jax.ShapeDtypeStruct((heads.shape[0], weights[0].shape[1]), bf16)
-    return pl.pallas_call(
-        project_kernel,
-        out_shape=(shape,) * len(weights),
-        out_specs=(vmem,) * len(weights),
-        compiler_params=pltpu.CompilerParams(vmem_limit_bytes=20 << 20),
-        name="project",
-    )(heads, *weights)
-
-
-def place_rows_kernel(side_ref, *refs):
-    block_refs, out_ref = refs[:-1], refs[-1]
-    sides = len(block_refs)
-    rows = out_ref.shape[1]
-    per = out_ref.shape[0] // sides
-    for step, ref in enumerate(block_refs):
-        owner = lax.rem(side_ref[0] + step, sides)
-        for half in range(per):
-            out_ref[owner * per + half] = ref[half * rows : (half + 1) * rows, :]
-
-
-def place_rows(side, blocks, ways):
-    vmem = pl.BlockSpec(memory_space=pltpu.VMEM)
-    rows = len(blocks) * blocks[0].shape[0] // ways
-    return pl.pallas_call(
-        place_rows_kernel,
-        out_shape=jax.ShapeDtypeStruct((ways, rows, blocks[0].shape[1]), bf16),
-        in_specs=[pl.BlockSpec(memory_space=pltpu.SMEM)] + [vmem] * len(blocks),
-        out_specs=vmem,
-        compiler_params=pltpu.CompilerParams(vmem_limit_bytes=20 << 20),
-        name="place_rows",
-    )(side, *blocks)
-
-
 Y, Z = 4, 8
 
 
@@ -306,7 +270,7 @@
 
     mine = across_z(replicate(queries, Z)).reshape(quarter, width)
 
-    columns, fact = prepare(prefix_values, resp_values)
+    columns, own_keys, own_columns, fact = prepare(prefix_values, resp_keys, resp_values)
     first = place * tokens
     own_segments = lax.dynamic_slice_in_dim(segment_ids, first, tokens)
     own_rows = first + jnp.arange(tokens, dtype=jnp.int32)
@@ -319,25 +283,34 @@
         owner = (place // Z + Y - step) % Y
         return lax.dynamic_slice_in_dim(bias, owner * quarter, quarter, 1)
 
-    def part_for(array, block):
-        return attend(array, prefix_keys, columns, resp_keys, resp_values, block, fact)
+    def part_for(array, block, lead=0, count=group):
+        return attend(
+            lead, count, array, prefix_keys, columns, own_keys, own_columns, block, fact
+        )
 
     blocks = [bias_for(step) for step in range(Y)]
-    mine, columns, fact, *blocks = lax.optimization_barrier((mine, columns, fact, *blocks))
+    mine, columns, own_keys, own_columns, fact, *blocks = lax.optimization_barrier(
+        (mine, columns, own_keys, own_columns, fact, *blocks)
+    )
     arrivals = {step: along_y(mine, step) for step in (1, 3, 2)}
-    own = [part_for(mine[:, : width // 2], blocks[0])]
+    own = [part_for(mine, blocks[0], 0, group // 2)]
     *blocks, own[0] = lax.optimization_barrier((*blocks, own[0]))
     parts = [along_y(part_for(arrivals[step], blocks[step]), -step) for step in (1, 2, 3)]
-    own.append(part_for(mine[:, width // 2 :], blocks[0]))
-
-    out_weight, own[1] = lax.optimization_barrier((out_weight, own[1]))
-    weights = [out_weight] + [along_y(out_weight, step) for step in (1, 2, 3)]
+    own.append(part_for(mine, blocks[0], group // 2, group // 2))
+
     joined = across_z(join(own, parts, group, Z))
     heads = across_z(combine(joined, group)).reshape(quarter, width)
-    blocks = project(heads, weights)
-    side = (place // Z).astype(jnp.int32).reshape(1)
-    blocks = [blocks[0]] + [along_y(blocks[step], -step) for step in (1, 2, 3)]
-    scored = lax.all_to_all(place_rows(side, blocks, ways), "mp", 0, 0, tiled=True)
+    pieces = [heads] + [along_y(heads, step) for step in (1, 3, 2)]
+    scored = [
+        jnp.dot(piece, out_weight, preferred_element_type=f32).astype(bf16) for piece in pieces
+    ]
+    order = (0, 1, 3, 2)
+    whole = jnp.zeros((rows, out_weight.shape[1]), bf16)
+    for step, piece in zip(order, scored):
+        owner = (place // Z + Y - step) % Y
+        whole = lax.dynamic_update_slice_in_dim(whole, piece, owner * quarter, 0)
+    scored = whole.reshape(ways, rows // ways, -1)
+    scored = lax.all_to_all(scored, "mp", 0, 0, tiled=True)
     return jnp.sum(scored.astype(f32), axis=0).astype(bf16)
 
 

time: 155 us -> 154 us (level); the launches traced: 155 us -> 153 us
  blocking collectives: 15.4 us -> 47.1 us
  starting transfers between devices: 49.9 us -> 24.3 us
  waiting for transfers between devices: 37.2 us -> 15.1 us
  Pallas kernels: 49 us -> 60.2 us
    all_to_all x1 -> x3, blocking collectives: 15.4 us -> 47.1 us  [the longest x2 29.6 us: across_z(): lax.all_to_all(array, 'seq', 0, 0, axis_index_groups=along_z, tiled=True)]
    all_to_all x3 -> x1, starting transfers between devices: 25 us -> 9.03 us  [across_z(): lax.all_to_all(array, 'seq', 0, 0, axis_index_groups=along_z, tiled=True)]
    ppermute x12 -> x9, waiting for transfers between devices: 23.5 us -> 8.96 us  [along_y(): return lax.ppermute(array, 'seq', pairs)]
    pallas_call x7 -> x5, Pallas kernels: 44.9 us -> 57.5 us  [attend(): pl.pallas_call(lambda *refs: attend_kernel(lead, group, min(4, group), 51...]
    ppermute x12 -> x9, starting transfers between devices: 25 us -> 15.3 us  [along_y(): return lax.ppermute(array, 'seq', pairs)]
    all_to_all x3 -> x1, waiting for transfers between devices: 13.7 us -> 6.13 us  [across_z(): lax.all_to_all(array, 'seq', 0, 0, axis_index_groups=along_z, tiled=True)]
  transfers between devices with their start and end apart: 15 -> 10, of which waited for: 7 -> 6; matrix products, arithmetic and copies ran while one was open for 0% -> 1% of each run, Pallas kernels for 30% -> 38%
where the time goes in v4:
time: 154 us; the launch traced here: 153 us
  Pallas kernels  60.2 us (39%)
  blocking collectives  47.1 us (31%)
  starting transfers between devices  24.3 us (16%)
  waiting for transfers between devices  15.1 us (10%)
  local copies, waits for them, and re-layouts  4.26 us (3%)
    pallas_call x5, Pallas kernels, attend(): pl.pallas_call(lambda *refs: attend_kernel(lead, group, min(4, group), 51...  57.5 us
    all_to_all x2, blocking collectives, across_z(): lax.all_to_all(array, 'seq', 0, 0, axis_index_groups=along_z, tiled=True)  29.6 us
    all_to_all x1, blocking collectives, on_device(): scored = lax.all_to_all(scored, 'mp', 0, 0, tiled=True)  17.4 us
    ppermute x9, starting transfers between devices, along_y(): return lax.ppermute(array, 'seq', pairs)  15.3 us
    all_to_all x1, starting transfers between devices, across_z(): lax.all_to_all(array, 'seq', 0, 0, axis_index_groups=along_z, tiled=True)  9.03 us
    ppermute x9, waiting for transfers between devices, along_y(): return lax.ppermute(array, 'seq', pairs)  8.96 us
    all_to_all x1, waiting for transfers between devices, across_z(): lax.all_to_all(array, 'seq', 0, 0, axis_index_groups=along_z, tiled=True)  6.13 us
    unnamed x14, local copies, waits for them, and re-layouts  3.48 us
  transfers between devices with their start and end apart: 10, of which 6 were waited for; matrix products, arithmetic and copies ran while one was open for 1% of the time, Pallas kernels for 38%

profile of v4, /device:TPU:1, one launch (start us, length us, event | category | flops | bytes accessed | tf_op | source)
XLA Modules:
  0.0 152.7 jit_solution(2293573027855680149)
XLA Ops:
  0.0 0.0 copy-start
  0.0 0.0 copy-start.1
  0.0 0.9 copy-done.3
  0.9 0.8 replicate.1
  1.7 9.0 %all-to-all-start = ((bf16[8,16,1024]{2,1,0:T(8,128)(2,1)}), bf16[8,16,1024]{2,1,0:T(8,128)(2,1)S(1)}, u32[]{:S(2)}, u32[]{:S(2)}) async-start(bf16[8,16,1024]{2,1,0:T(8,128)(2,1)} %replicate.1), calls=%async_computation | async-start | bytes 524288 | tf_op jit(solution)/shard_map/all_to_all | solution.py:265
  10.7 0.8 dynamic_slice.15
  11.4 1.2 copy-done.2
  12.7 0.7 copy-done.4
  13.3 0.7 copy-done.5
  14.0 0.8 prepare.1
  14.8 0.0 copy-done.6
  14.8 0.1 fusion.5
  14.9 6.1 %all-to-all-done = bf16[8,16,1024]{2,1,0:T(8,128)(2,1)S(1)} async-done(((bf16[8,16,1024]{2,1,0:T(8,128)(2,1)}), bf16[8,16,1024]{2,1,0:T(8,128)(2,1)S(1)}, u32[]{:S(2)}, u32[]{:S(2)}) %all-to-all-start) | async-done | bytes 262176 | tf_op jit(solution)/shard_map/all_to_all | solution.py:265
  21.1 2.7 %collective-permute-start.4 = (bf16[128,1024]{1,0:T(8,128)(2,1)S(1)}, bf16[128,1024]{1,0:T(8,128)(2,1)S(1)}, u32[]{:S(2)}, u32[]{:S(2)}) collective-permute-start(bf16[128,1024]{1,0:T(8,128)(2,1)S(1)} %bitcast.11), channel_id=1, source_target_pairs={{0,192},{8,200},{16,208},{24,216},{32,224},{40,232},{48,240},{56,2... | collective-permute-start | bytes 786440 | tf_op jit(solution)/shard_map/ppermute | solution.py:269
  23.8 0.3 collective-permute-start.2
  24.1 0.7 collective-permute-start
  24.8 0.0 copy-done.1
  24.8 2.7 %attend.5.refs_0_ = bf16[528,128]{1,0:T(8,128)(2,1)S(1)} custom-call(bf16[128,1024]{1,0:T(8,128)(2,1)S(1)} %bitcast.14, bf16[4096,128]{1,0:T(8,128)(2,1)S(1)} %copy-done.1, bf16[128,4096]{1,0:T(8,128)(2,1)S(1)} %get-tuple-element.32.refs_2_, bf16[16,128]{1,0:T(8,128)(2,1)S(1)} %get-tuple-element.33.refs_3_, bf16[128,16]{1,0:T(8,128)(2,1)S(1)} %get-tuple-element.34.refs_4_, ...), custom_call_target="tpu_custom_call" | custom-call | tf_op jit(solution)/shard_map/attend/pallas_call | solution.py:168
  27.5 2.3 %collective-permute-done.4.refs_0_ = bf16[128,1024]{1,0:T(8,128)(2,1)S(1)} collective-permute-done((bf16[128,1024]{1,0:T(8,128)(2,1)S(1)}, bf16[128,1024]{1,0:T(8,128)(2,1)S(1)}, u32[]{:S(2)}, u32[]{:S(2)}) %collective-permute-start.4) | collective-permute-done | bytes 262176 | tf_op jit(solution)/shard_map/ppermute | solution.py:269
  29.8 17.4 %attend.9 = bf16[1056,128]{1,0:T(8,128)(2,1)S(1)} custom-call(bf16[128,1024]{1,0:T(8,128)(2,1)S(1)} %collective-permute-done.4.refs_0_, bf16[4096,128]{1,0:T(8,128)(2,1)S(1)} %copy-done.1, bf16[128,4096]{1,0:T(8,128)(2,1)S(1)} %get-tuple-element.32.refs_2_, bf16[16,128]{1,0:T(8,128)(2,1)S(1)} %get-tuple-element.33.refs_3_, ...), custom_call_target="tpu_custom_call" | custom-call | tf_op jit(solution)/shard_map/attend/pallas_call | solution.py:168
  47.2 6.0 %collective-permute-start.5 = (bf16[1056,128]{1,0:T(8,128)(2,1)S(1)}, bf16[1056,128]{1,0:T(8,128)(2,1)S(1)}, u32[]{:S(2)}, u32[]{:S(2)}) collective-permute-start(bf16[1056,128]{1,0:T(8,128)(2,1)S(1)} %attend.9), channel_id=1, source_target_pairs={{0,64},{8,72},{16,80},{24,88},{32,96},{40,104},{48,112},{56,120},{... | collective-permute-start | bytes 811016 | tf_op jit(solution)/shard_map/ppermute | solution.py:269
  53.2 0.0 collective-permute-done.2.refs_0_
  53.2 17.4 %attend.8 = bf16[1056,128]{1,0:T(8,128)(2,1)S(1)} custom-call(bf16[128,1024]{1,0:T(8,128)(2,1)S(1)} %collective-permute-done.2.refs_0_, bf16[4096,128]{1,0:T(8,128)(2,1)S(1)} %copy-done.1, bf16[128,4096]{1,0:T(8,128)(2,1)S(1)} %get-tuple-element.32.refs_2_, bf16[16,128]{1,0:T(8,128)(2,1)S(1)} %get-tuple-element.33.refs_3_, ...), custom_call_target="tpu_custom_call" | custom-call | tf_op jit(solution)/shard_map/attend/pallas_call | solution.py:168
  70.6 0.1 collective-permute-start.3
  70.7 0.0 collective-permute-done.refs_0_
  70.7 17.4 %attend.7 = bf16[1056,128]{1,0:T(8,128)(2,1)S(1)} custom-call(bf16[128,1024]{1,0:T(8,128)(2,1)S(1)} %collective-permute-done.refs_0_, bf16[4096,128]{1,0:T(8,128)(2,1)S(1)} %copy-done.1, bf16[128,4096]{1,0:T(8,128)(2,1)S(1)} %get-tuple-element.32.refs_2_, bf16[16,128]{1,0:T(8,128)(2,1)S(1)} %get-tuple-element.33.refs_3_, ...), custom_call_target="tpu_custom_call" | custom-call | tf_op jit(solution)/shard_map/attend/pallas_call | solution.py:168
  88.1 2.7 %collective-permute-start.1 = (bf16[1056,128]{1,0:T(8,128)(2,1)S(1)}, bf16[1056,128]{1,0:T(8,128)(2,1)S(1)}, u32[]{:S(2)}, u32[]{:S(2)}) collective-permute-start(bf16[1056,128]{1,0:T(8,128)(2,1)S(1)} %attend.7), channel_id=1, source_target_pairs={{0,192},{8,200},{16,208},{24,216},{32,224},{40,232},{48,240},{56,2... | collective-permute-start | bytes 811016 | tf_op jit(solution)/shard_map/ppermute | solution.py:269
  90.8 2.7 %attend.6.refs_1_ = bf16[528,128]{1,0:T(8,128)(2,1)S(1)} custom-call(bf16[128,1024]{1,0:T(8,128)(2,1)S(1)} %bitcast.15, bf16[4096,128]{1,0:T(8,128)(2,1)S(1)} %copy-done.1, bf16[128,4096]{1,0:T(8,128)(2,1)S(1)} %get-tuple-element.32.refs_2_, bf16[16,128]{1,0:T(8,128)(2,1)S(1)} %get-tuple-element.33.refs_3_, bf16[128,16]{1,0:T(8,128)(2,1)S(1)} %get-tuple-element.34.refs_4_, ...), custom_call_target="tpu_custom_call" | custom-call | tf_op jit(solution)/shard_map/attend/pallas_call | solution.py:168
  93.5 0.0 collective-permute-done.5.refs_4_
  93.5 0.0 collective-permute-done.3.refs_3_
  93.5 0.7 collective-permute-done.1.refs_2_
  94.2 0.8 join.1
  95.0 17.9 %all_to_all.20.refs_0_ = bf16[8,144,128]{2,1,0:T(8,128)(2,1)S(1)} all-to-all(bf16[8,144,128]{2,1,0:T(8,128)(2,1)S(1)} %join.1), channel_id=1, replica_groups={{0,8,16,24,32,40,48,56},{64,72,80,88,96,104,112,120},{128,136,144,152,1..., dimensions={0} | all-to-all | bytes 589824 | tf_op jit(solution)/shard_map/all_to_all | solution.py:265
  112.9 0.3 combine.1
  113.3 11.7 %all_to_all.21 = bf16[8,16,1024]{2,1,0:T(8,128)(2,1)S(1)} all-to-all(bf16[8,16,1024]{2,1,0:T(8,128)(2,1)S(1)} %combine.1), channel_id=1, replica_groups={{0,8,16,24,32,40,48,56},{64,72,80,88,96,104,112,120},{128,136,144,152,1..., dimensions={0} | all-to-all | bytes 524288 | tf_op jit(solution)/shard_map/all_to_all | solution.py:265
  125.0 0.0 collective-permute-start.6
  125.0 2.7 %collective-permute-start.7 = (bf16[128,1024]{1,0:T(8,128)(2,1)S(1)}, bf16[128,1024]{1,0:T(8,128)(2,1)S(1)}, u32[]{:S(2)}, u32[]{:S(2)}) collective-permute-start(bf16[128,1024]{1,0:T(8,128)(2,1)S(1)} %bitcast.17), channel_id=1, source_target_pairs={{0,192},{8,200},{16,208},{24,216},{32,224},{40,232},{48,240},{56,2... | collective-permute-start | bytes 786440 | tf_op jit(solution)/shard_map/ppermute | solution.py:269
  127.7 0.0 collective-permute-start.8
  127.7 0.0 copy-done
  127.7 0.2 fusion.3
  128.0 3.5 %collective-permute-done.6 = bf16[128,1024]{1,0:T(8,128)(2,1)S(1)} collective-permute-done((bf16[128,1024]{1,0:T(8,128)(2,1)S(1)}, bf16[128,1024]{1,0:T(8,128)(2,1)S(1)}, u32[]{:S(2)}, u32[]{:S(2)}) %collective-permute-start.6) | collective-permute-done | bytes 262176 | tf_op jit(solution)/shard_map/ppermute | solution.py:269
  131.4 0.2 fusion.2
  131.7 2.1 %collective-permute-done.7 = bf16[128,1024]{1,0:T(8,128)(2,1)S(1)} collective-permute-done((bf16[128,1024]{1,0:T(8,128)(2,1)S(1)}, bf16[128,1024]{1,0:T(8,128)(2,1)S(1)}, u32[]{:S(2)}, u32[]{:S(2)}) %collective-permute-start.7) | collective-permute-done | bytes 262176 | tf_op jit(solution)/shard_map/ppermute | solution.py:269
  133.8 0.2 fusion.1
  134.0 0.4 collective-permute-done.8
  134.4 0.2 fusion
  134.7 17.4 %all_to_all.22 = bf16[8,64,256]{2,1,0:T(8,128)(2,1)S(1)} all-to-all(bf16[8,64,256]{2,1,0:T(8,128)(2,1)S(1)} %bitcast.20), channel_id=1, replica_groups=mesh['seq'=32,'mp'=8] {'mp'}, dimensions={0} | all-to-all | bytes 524288 | tf_op jit(solution)/shard_map/all_to_all | solution.py:313
  152.1 0.7 reduce_sum.12
  (8 shorter events, 0.0 us)
Async XLA Ops:
  0.0 127.7 %copy-start = (bf16[1024,256]{1,0:T(8,128)(2,1)S(1)}, bf16[1024,256]{1,0:T(8,128)(2,1)}, u32[]{:S(2)}) copy-start(bf16[1024,256]{1,0:T(8,128)(2,1)} %param.13) | copy-start | bytes 1572868
  0.0 24.8 %copy-start.1 = (bf16[4096,128]{1,0:T(8,128)(2,1)S(1)}, bf16[4096,128]{1,0:T(8,128)(2,1)}, u32[]{:S(2)}) copy-start(bf16[4096,128]{1,0:T(8,128)(2,1)} %refs_1_.9) | copy-start | bytes 3145732
  0.0 0.9 copy-start.3
  1.7 19.4 %all-to-all-start = ((bf16[8,16,1024]{2,1,0:T(8,128)(2,1)}), bf16[8,16,1024]{2,1,0:T(8,128)(2,1)S(1)}, u32[]{:S(2)}, u32[]{:S(2)}) async-start(bf16[8,16,1024]{2,1,0:T(8,128)(2,1)} %replicate.1), calls=%async_computation | async-start | bytes 524288 | tf_op jit(solution)/shard_map/all_to_all | solution.py:265
  11.4 1.2 copy-start.2
  12.7 0.7 copy-start.4
  13.3 0.7 copy-start.5
  14.0 0.8 copy-start.6
  21.1 8.8 %collective-permute-start.4 = (bf16[128,1024]{1,0:T(8,128)(2,1)S(1)}, bf16[128,1024]{1,0:T(8,128)(2,1)S(1)}, u32[]{:S(2)}, u32[]{:S(2)}) collective-permute-start(bf16[128,1024]{1,0:T(8,128)(2,1)S(1)} %bitcast.11), channel_id=1, source_target_pairs={{0,192},{8,200},{16,208},{24,216},{32,224},{40,232},{48,240},{56,2... | collective-permute-start | bytes 786440 | tf_op jit(solution)/shard_map/ppermute | solution.py:269
  23.8 29.4 %collective-permute-start.2 = (bf16[128,1024]{1,0:T(8,128)(2,1)S(1)}, bf16[128,1024]{1,0:T(8,128)(2,1)S(1)}, u32[]{:S(2)}, u32[]{:S(2)}) collective-permute-start(bf16[128,1024]{1,0:T(8,128)(2,1)S(1)} %bitcast.12), channel_id=1, source_target_pairs={{0,128},{8,136},{16,144},{24,152},{32,160},{40,168},{48,176},{56,1... | collective-permute-start | bytes 786440 | tf_op jit(solution)/shard_map/ppermute | solution.py:269
  24.1 46.6 %collective-permute-start = (bf16[128,1024]{1,0:T(8,128)(2,1)S(1)}, bf16[128,1024]{1,0:T(8,128)(2,1)S(1)}, u32[]{:S(2)}, u32[]{:S(2)}) collective-permute-start(bf16[128,1024]{1,0:T(8,128)(2,1)S(1)} %bitcast.13), channel_id=1, source_target_pairs={{0,64},{8,72},{16,80},{24,88},{32,96},{40,104},{48,112},{56,120},{... | collective-permute-start | bytes 786440 | tf_op jit(solution)/shard_map/ppermute | solution.py:269
  47.2 46.3 %collective-permute-start.5 = (bf16[1056,128]{1,0:T(8,128)(2,1)S(1)}, bf16[1056,128]{1,0:T(8,128)(2,1)S(1)}, u32[]{:S(2)}, u32[]{:S(2)}) collective-permute-start(bf16[1056,128]{1,0:T(8,128)(2,1)S(1)} %attend.9), channel_id=1, source_target_pairs={{0,64},{8,72},{16,80},{24,88},{32,96},{40,104},{48,112},{56,120},{... | collective-permute-start | bytes 811016 | tf_op jit(solution)/shard_map/ppermute | solution.py:269
  70.6 22.9 %collective-permute-start.3 = (bf16[1056,128]{1,0:T(8,128)(2,1)S(1)}, bf16[1056,128]{1,0:T(8,128)(2,1)S(1)}, u32[]{:S(2)}, u32[]{:S(2)}) collective-permute-start(bf16[1056,128]{1,0:T(8,128)(2,1)S(1)} %attend.8), channel_id=1, source_target_pairs={{0,128},{8,136},{16,144},{24,152},{32,160},{40,168},{48,176},{56,1... | collective-permute-start | bytes 811016 | tf_op jit(solution)/shard_map/ppermute | solution.py:269
  88.1 6.1 %collective-permute-start.1 = (bf16[1056,128]{1,0:T(8,128)(2,1)S(1)}, bf16[1056,128]{1,0:T(8,128)(2,1)S(1)}, u32[]{:S(2)}, u32[]{:S(2)}) collective-permute-start(bf16[1056,128]{1,0:T(8,128)(2,1)S(1)} %attend.7), channel_id=1, source_target_pairs={{0,192},{8,200},{16,208},{24,216},{32,224},{40,232},{48,240},{56,2... | collective-permute-start | bytes 811016 | tf_op jit(solution)/shard_map/ppermute | solution.py:269
  125.0 6.4 %collective-permute-start.6 = (bf16[128,1024]{1,0:T(8,128)(2,1)S(1)}, bf16[128,1024]{1,0:T(8,128)(2,1)S(1)}, u32[]{:S(2)}, u32[]{:S(2)}) collective-permute-start(bf16[128,1024]{1,0:T(8,128)(2,1)S(1)} %bitcast.16), channel_id=1, source_target_pairs={{0,64},{8,72},{16,80},{24,88},{32,96},{40,104},{48,112},{56,120},{... | collective-permute-start | bytes 786440 | tf_op jit(solution)/shard_map/ppermute | solution.py:269
  125.0 8.8 %collective-permute-start.7 = (bf16[128,1024]{1,0:T(8,128)(2,1)S(1)}, bf16[128,1024]{1,0:T(8,128)(2,1)S(1)}, u32[]{:S(2)}, u32[]{:S(2)}) collective-permute-start(bf16[128,1024]{1,0:T(8,128)(2,1)S(1)} %bitcast.17), channel_id=1, source_target_pairs={{0,192},{8,200},{16,208},{24,216},{32,224},{40,232},{48,240},{56,2... | collective-permute-start | bytes 786440 | tf_op jit(solution)/shard_map/ppermute | solution.py:269
  127.7 6.7 %collective-permute-start.8 = (bf16[128,1024]{1,0:T(8,128)(2,1)S(1)}, bf16[128,1024]{1,0:T(8,128)(2,1)S(1)}, u32[]{:S(2)}, u32[]{:S(2)}) collective-permute-start(bf16[128,1024]{1,0:T(8,128)(2,1)S(1)} %bitcast.18), channel_id=1, source_target_pairs={{0,128},{8,136},{16,144},{24,152},{32,160},{40,168},{48,176},{56,1... | collective-permute-start | bytes 786440 | tf_op jit(solution)/shard_map/ppermute | solution.py:269

commit v5 on v4

--- a/solution.py
+++ b/solution.py
@@ -292,9 +292,10 @@
     mine, columns, own_keys, own_columns, fact, *blocks = lax.optimization_barrier(
         (mine, columns, own_keys, own_columns, fact, *blocks)
     )
-    arrivals = {step: along_y(mine, step) for step in (1, 3, 2)}
+    arrivals = {step: along_y(mine, step) for step in (1, 3)}
     own = [part_for(mine, blocks[0], 0, group // 2)]
-    *blocks, own[0] = lax.optimization_barrier((*blocks, own[0]))
+    *blocks, later, own[0] = lax.optimization_barrier((*blocks, mine, own[0]))
+    arrivals[2] = along_y(later, 2)
     parts = [along_y(part_for(arrivals[step], blocks[step]), -step) for step in (1, 2, 3)]
     own.append(part_for(mine, blocks[0], group // 2, group // 2))
 

time: 154 us -> 154 us (level)
  waiting for transfers between devices: 15.1 us -> 13.3 us
  starting transfers between devices: 24.3 us -> 26 us
    ppermute x9, waiting for transfers between devices: 8.96 us -> 7.2 us  [along_y(): return lax.ppermute(array, 'seq', pairs)]
    ppermute x9, starting transfers between devices: 15.3 us -> 17 us  [along_y(): return lax.ppermute(array, 'seq', pairs)]
  transfers between devices with their start and end apart: 10 -> 10, of which waited for: 6 -> 5; matrix products, arithmetic and copies ran while one was open for 1% -> 1% of each run, Pallas kernels for 38% -> 38%
where the time goes in v5:
time: 154 us; the launch traced here: 153 us
  Pallas kernels  60.2 us (39%)
  blocking collectives  47.2 us (31%)
  starting transfers between devices  26 us (17%)
  waiting for transfers between devices  13.3 us (9%)
  local copies, waits for them, and re-layouts  4.26 us (3%)
    pallas_call x5, Pallas kernels, attend(): pl.pallas_call(lambda *refs: attend_kernel(lead, group, min(4, group), 51...  57.5 us
    all_to_all x2, blocking collectives, across_z(): lax.all_to_all(array, 'seq', 0, 0, axis_index_groups=along_z, tiled=True)  30.3 us
    ppermute x9, starting transfers between devices, along_y(): return lax.ppermute(array, 'seq', pairs)  17 us
    all_to_all x1, blocking collectives, on_device(): scored = lax.all_to_all(scored, 'mp', 0, 0, tiled=True)  16.8 us
    all_to_all x1, starting transfers between devices, across_z(): lax.all_to_all(array, 'seq', 0, 0, axis_index_groups=along_z, tiled=True)  9.03 us
    ppermute x9, waiting for transfers between devices, along_y(): return lax.ppermute(array, 'seq', pairs)  7.2 us
    all_to_all x1, waiting for transfers between devices, across_z(): lax.all_to_all(array, 'seq', 0, 0, axis_index_groups=along_z, tiled=True)  6.13 us
    unnamed x14, local copies, waits for them, and re-layouts  3.48 us
  transfers between devices with their start and end apart: 10, of which 5 were waited for; matrix products, arithmetic and copies ran while one was open for 1% of the time, Pallas kernels for 38%

profile of v5, /device:TPU:1, one launch (start us, length us, event | category | flops | bytes accessed | tf_op | source)
XLA Modules:
  0.0 152.8 jit_solution(13193928559656864127)
XLA Ops:
  0.0 0.0 copy-start
  0.0 0.0 copy-start.1
  0.0 0.9 copy-done.3
  0.9 0.8 replicate.1
  1.7 9.0 %all-to-all-start = ((bf16[8,16,1024]{2,1,0:T(8,128)(2,1)}), bf16[8,16,1024]{2,1,0:T(8,128)(2,1)S(1)}, u32[]{:S(2)}, u32[]{:S(2)}) async-start(bf16[8,16,1024]{2,1,0:T(8,128)(2,1)} %replicate.1), calls=%async_computation | async-start | bytes 524288 | tf_op jit(solution)/shard_map/all_to_all | solution.py:265
  10.7 0.8 dynamic_slice.15
  11.4 1.2 copy-done.2
  12.7 0.7 copy-done.4
  13.3 0.7 copy-done.5
  14.0 0.8 prepare.1
  14.8 0.0 copy-done.6
  14.8 0.1 fusion.5
  14.9 6.1 %all-to-all-done = bf16[8,16,1024]{2,1,0:T(8,128)(2,1)S(1)} async-done(((bf16[8,16,1024]{2,1,0:T(8,128)(2,1)}), bf16[8,16,1024]{2,1,0:T(8,128)(2,1)S(1)}, u32[]{:S(2)}, u32[]{:S(2)}) %all-to-all-start) | async-done | bytes 262176 | tf_op jit(solution)/shard_map/all_to_all | solution.py:265
  21.1 2.7 %collective-permute-start.4 = (bf16[128,1024]{1,0:T(8,128)(2,1)S(1)}, bf16[128,1024]{1,0:T(8,128)(2,1)S(1)}, u32[]{:S(2)}, u32[]{:S(2)}) collective-permute-start(bf16[128,1024]{1,0:T(8,128)(2,1)S(1)} %bitcast.11), channel_id=1, source_target_pairs={{0,192},{8,200},{16,208},{24,216},{32,224},{40,232},{48,240},{56,2... | collective-permute-start | bytes 786440 | tf_op jit(solution)/shard_map/ppermute | solution.py:269
  23.8 0.0 copy-done.1
  23.8 2.7 %attend.5.refs_0_ = bf16[528,128]{1,0:T(8,128)(2,1)S(1)} custom-call(bf16[128,1024]{1,0:T(8,128)(2,1)S(1)} %bitcast.12, bf16[4096,128]{1,0:T(8,128)(2,1)S(1)} %copy-done.1, bf16[128,4096]{1,0:T(8,128)(2,1)S(1)} %get-tuple-element.33.refs_2_, bf16[16,128]{1,0:T(8,128)(2,1)S(1)} %get-tuple-element.34.refs_3_, bf16[128,16]{1,0:T(8,128)(2,1)S(1)} %get-tuple-element.35.refs_4_, ...), custom_call_target="tpu_custom_call" | custom-call | tf_op jit(solution)/shard_map/attend/pallas_call | solution.py:168
  26.5 6.9 %collective-permute-start.2 = (bf16[128,1024]{1,0:T(8,128)(2,1)S(1)}, bf16[128,1024]{1,0:T(8,128)(2,1)S(1)}, u32[]{:S(2)}, u32[]{:S(2)}) collective-permute-start(bf16[128,1024]{1,0:T(8,128)(2,1)S(1)} %bitcast.13), channel_id=1, source_target_pairs={{0,128},{8,136},{16,144},{24,152},{32,160},{40,168},{48,176},{56,1... | collective-permute-start | bytes 786440 | tf_op jit(solution)/shard_map/ppermute | solution.py:269
  33.3 0.7 collective-permute-start
  34.0 0.0 collective-permute-done.4.refs_0_
  34.0 17.4 %attend.9 = bf16[1056,128]{1,0:T(8,128)(2,1)S(1)} custom-call(bf16[128,1024]{1,0:T(8,128)(2,1)S(1)} %collective-permute-done.4.refs_0_, bf16[4096,128]{1,0:T(8,128)(2,1)S(1)} %copy-done.1, bf16[128,4096]{1,0:T(8,128)(2,1)S(1)} %get-tuple-element.33.refs_2_, bf16[16,128]{1,0:T(8,128)(2,1)S(1)} %get-tuple-element.34.refs_3_, ...), custom_call_target="tpu_custom_call" | custom-call | tf_op jit(solution)/shard_map/attend/pallas_call | solution.py:168
  51.4 0.3 collective-permute-start.5
  51.7 0.0 collective-permute-done.2.refs_0_
  51.7 17.4 %attend.8 = bf16[1056,128]{1,0:T(8,128)(2,1)S(1)} custom-call(bf16[128,1024]{1,0:T(8,128)(2,1)S(1)} %collective-permute-done.2.refs_0_, bf16[4096,128]{1,0:T(8,128)(2,1)S(1)} %copy-done.1, bf16[128,4096]{1,0:T(8,128)(2,1)S(1)} %get-tuple-element.33.refs_2_, bf16[16,128]{1,0:T(8,128)(2,1)S(1)} %get-tuple-element.34.refs_3_, ...), custom_call_target="tpu_custom_call" | custom-call | tf_op jit(solution)/shard_map/attend/pallas_call | solution.py:168
  69.1 0.1 collective-permute-start.3
  69.2 0.0 collective-permute-done.refs_0_
  69.2 17.4 %attend.7 = bf16[1056,128]{1,0:T(8,128)(2,1)S(1)} custom-call(bf16[128,1024]{1,0:T(8,128)(2,1)S(1)} %collective-permute-done.refs_0_, bf16[4096,128]{1,0:T(8,128)(2,1)S(1)} %copy-done.1, bf16[128,4096]{1,0:T(8,128)(2,1)S(1)} %get-tuple-element.33.refs_2_, bf16[16,128]{1,0:T(8,128)(2,1)S(1)} %get-tuple-element.34.refs_3_, ...), custom_call_target="tpu_custom_call" | custom-call | tf_op jit(solution)/shard_map/attend/pallas_call | solution.py:168
  86.6 3.6 %collective-permute-start.1 = (bf16[1056,128]{1,0:T(8,128)(2,1)S(1)}, bf16[1056,128]{1,0:T(8,128)(2,1)S(1)}, u32[]{:S(2)}, u32[]{:S(2)}) collective-permute-start(bf16[1056,128]{1,0:T(8,128)(2,1)S(1)} %attend.7), channel_id=1, source_target_pairs={{0,192},{8,200},{16,208},{24,216},{32,224},{40,232},{48,240},{56,2... | collective-permute-start | bytes 811016 | tf_op jit(solution)/shard_map/ppermute | solution.py:269
  90.2 2.7 %attend.6.refs_1_ = bf16[528,128]{1,0:T(8,128)(2,1)S(1)} custom-call(bf16[128,1024]{1,0:T(8,128)(2,1)S(1)} %bitcast.15, bf16[4096,128]{1,0:T(8,128)(2,1)S(1)} %copy-done.1, bf16[128,4096]{1,0:T(8,128)(2,1)S(1)} %get-tuple-element.33.refs_2_, bf16[16,128]{1,0:T(8,128)(2,1)S(1)} %get-tuple-element.34.refs_3_, bf16[128,16]{1,0:T(8,128)(2,1)S(1)} %get-tuple-element.35.refs_4_, ...), custom_call_target="tpu_custom_call" | custom-call | tf_op jit(solution)/shard_map/attend/pallas_call | solution.py:168
  92.9 0.0 collective-permute-done.5.refs_4_
  92.9 0.0 collective-permute-done.3.refs_3_
  92.9 0.7 collective-permute-done.1.refs_2_
  93.6 0.8 join.1
  94.4 18.6 %all_to_all.20.refs_0_ = bf16[8,144,128]{2,1,0:T(8,128)(2,1)S(1)} all-to-all(bf16[8,144,128]{2,1,0:T(8,128)(2,1)S(1)} %join.1), channel_id=1, replica_groups={{0,8,16,24,32,40,48,56},{64,72,80,88,96,104,112,120},{128,136,144,152,1..., dimensions={0} | all-to-all | bytes 589824 | tf_op jit(solution)/shard_map/all_to_all | solution.py:265
  113.0 0.3 combine.1
  113.3 11.8 %all_to_all.21 = bf16[8,16,1024]{2,1,0:T(8,128)(2,1)S(1)} all-to-all(bf16[8,16,1024]{2,1,0:T(8,128)(2,1)S(1)} %combine.1), channel_id=1, replica_groups={{0,8,16,24,32,40,48,56},{64,72,80,88,96,104,112,120},{128,136,144,152,1..., dimensions={0} | all-to-all | bytes 524288 | tf_op jit(solution)/shard_map/all_to_all | solution.py:265
  125.1 0.0 collective-permute-start.6
  125.1 2.7 %collective-permute-start.7 = (bf16[128,1024]{1,0:T(8,128)(2,1)S(1)}, bf16[128,1024]{1,0:T(8,128)(2,1)S(1)}, u32[]{:S(2)}, u32[]{:S(2)}) collective-permute-start(bf16[128,1024]{1,0:T(8,128)(2,1)S(1)} %bitcast.17), channel_id=1, source_target_pairs={{0,192},{8,200},{16,208},{24,216},{32,224},{40,232},{48,240},{56,2... | collective-permute-start | bytes 786440 | tf_op jit(solution)/shard_map/ppermute | solution.py:269
  127.8 0.0 collective-permute-start.8
  127.9 0.0 copy-done
  127.9 0.2 fusion.3
  128.1 3.4 %collective-permute-done.6 = bf16[128,1024]{1,0:T(8,128)(2,1)S(1)} collective-permute-done((bf16[128,1024]{1,0:T(8,128)(2,1)S(1)}, bf16[128,1024]{1,0:T(8,128)(2,1)S(1)}, u32[]{:S(2)}, u32[]{:S(2)}) %collective-permute-start.6) | collective-permute-done | bytes 262176 | tf_op jit(solution)/shard_map/ppermute | solution.py:269
  131.5 0.2 fusion.2
  131.8 2.1 %collective-permute-done.7 = bf16[128,1024]{1,0:T(8,128)(2,1)S(1)} collective-permute-done((bf16[128,1024]{1,0:T(8,128)(2,1)S(1)}, bf16[128,1024]{1,0:T(8,128)(2,1)S(1)}, u32[]{:S(2)}, u32[]{:S(2)}) %collective-permute-start.7) | collective-permute-done | bytes 262176 | tf_op jit(solution)/shard_map/ppermute | solution.py:269
  133.9 0.2 fusion.1
  134.2 0.9 collective-permute-done.8
  135.1 0.2 fusion
  135.3 16.8 %all_to_all.22 = bf16[8,64,256]{2,1,0:T(8,128)(2,1)S(1)} all-to-all(bf16[8,64,256]{2,1,0:T(8,128)(2,1)S(1)} %bitcast.20), channel_id=1, replica_groups=mesh['seq'=32,'mp'=8] {'mp'}, dimensions={0} | all-to-all | bytes 524288 | tf_op jit(solution)/shard_map/all_to_all | solution.py:314
  152.1 0.7 reduce_sum.12
  (8 shorter events, 0.0 us)
Async XLA Ops:
  0.0 127.9 %copy-start = (bf16[1024,256]{1,0:T(8,128)(2,1)S(1)}, bf16[1024,256]{1,0:T(8,128)(2,1)}, u32[]{:S(2)}) copy-start(bf16[1024,256]{1,0:T(8,128)(2,1)} %param.13) | copy-start | bytes 1572868
  0.0 23.8 %copy-start.1 = (bf16[4096,128]{1,0:T(8,128)(2,1)S(1)}, bf16[4096,128]{1,0:T(8,128)(2,1)}, u32[]{:S(2)}) copy-start(bf16[4096,128]{1,0:T(8,128)(2,1)} %refs_1_.9) | copy-start | bytes 3145732
  0.0 0.9 copy-start.3
  1.7 19.4 %all-to-all-start = ((bf16[8,16,1024]{2,1,0:T(8,128)(2,1)}), bf16[8,16,1024]{2,1,0:T(8,128)(2,1)S(1)}, u32[]{:S(2)}, u32[]{:S(2)}) async-start(bf16[8,16,1024]{2,1,0:T(8,128)(2,1)} %replicate.1), calls=%async_computation | async-start | bytes 524288 | tf_op jit(solution)/shard_map/all_to_all | solution.py:265
  11.4 1.2 copy-start.2
  12.7 0.7 copy-start.4
  13.3 0.7 copy-start.5
  14.0 0.8 copy-start.6
  21.1 13.0 %collective-permute-start.4 = (bf16[128,1024]{1,0:T(8,128)(2,1)S(1)}, bf16[128,1024]{1,0:T(8,128)(2,1)S(1)}, u32[]{:S(2)}, u32[]{:S(2)}) collective-permute-start(bf16[128,1024]{1,0:T(8,128)(2,1)S(1)} %bitcast.11), channel_id=1, source_target_pairs={{0,192},{8,200},{16,208},{24,216},{32,224},{40,232},{48,240},{56,2... | collective-permute-start | bytes 786440 | tf_op jit(solution)/shard_map/ppermute | solution.py:269
  26.5 25.2 %collective-permute-start.2 = (bf16[128,1024]{1,0:T(8,128)(2,1)S(1)}, bf16[128,1024]{1,0:T(8,128)(2,1)S(1)}, u32[]{:S(2)}, u32[]{:S(2)}) collective-permute-start(bf16[128,1024]{1,0:T(8,128)(2,1)S(1)} %bitcast.13), channel_id=1, source_target_pairs={{0,128},{8,136},{16,144},{24,152},{32,160},{40,168},{48,176},{56,1... | collective-permute-start | bytes 786440 | tf_op jit(solution)/shard_map/ppermute | solution.py:269
  33.3 35.9 %collective-permute-start = (bf16[128,1024]{1,0:T(8,128)(2,1)S(1)}, bf16[128,1024]{1,0:T(8,128)(2,1)S(1)}, u32[]{:S(2)}, u32[]{:S(2)}) collective-permute-start(bf16[128,1024]{1,0:T(8,128)(2,1)S(1)} %bitcast.14), channel_id=1, source_target_pairs={{0,64},{8,72},{16,80},{24,88},{32,96},{40,104},{48,112},{56,120},{... | collective-permute-start | bytes 786440 | tf_op jit(solution)/shard_map/ppermute | solution.py:269
  51.4 41.5 %collective-permute-start.5 = (bf16[1056,128]{1,0:T(8,128)(2,1)S(1)}, bf16[1056,128]{1,0:T(8,128)(2,1)S(1)}, u32[]{:S(2)}, u32[]{:S(2)}) collective-permute-start(bf16[1056,128]{1,0:T(8,128)(2,1)S(1)} %attend.9), channel_id=1, source_target_pairs={{0,64},{8,72},{16,80},{24,88},{32,96},{40,104},{48,112},{56,120},{... | collective-permute-start | bytes 811016 | tf_op jit(solution)/shard_map/ppermute | solution.py:269
  69.1 23.8 %collective-permute-start.3 = (bf16[1056,128]{1,0:T(8,128)(2,1)S(1)}, bf16[1056,128]{1,0:T(8,128)(2,1)S(1)}, u32[]{:S(2)}, u32[]{:S(2)}) collective-permute-start(bf16[1056,128]{1,0:T(8,128)(2,1)S(1)} %attend.8), channel_id=1, source_target_pairs={{0,128},{8,136},{16,144},{24,152},{32,160},{40,168},{48,176},{56,1... | collective-permute-start | bytes 811016 | tf_op jit(solution)/shard_map/ppermute | solution.py:269
  86.6 7.0 %collective-permute-start.1 = (bf16[1056,128]{1,0:T(8,128)(2,1)S(1)}, bf16[1056,128]{1,0:T(8,128)(2,1)S(1)}, u32[]{:S(2)}, u32[]{:S(2)}) collective-permute-start(bf16[1056,128]{1,0:T(8,128)(2,1)S(1)} %attend.7), channel_id=1, source_target_pairs={{0,192},{8,200},{16,208},{24,216},{32,224},{40,232},{48,240},{56,2... | collective-permute-start | bytes 811016 | tf_op jit(solution)/shard_map/ppermute | solution.py:269
  125.1 6.4 %collective-permute-start.6 = (bf16[128,1024]{1,0:T(8,128)(2,1)S(1)}, bf16[128,1024]{1,0:T(8,128)(2,1)S(1)}, u32[]{:S(2)}, u32[]{:S(2)}) collective-permute-start(bf16[128,1024]{1,0:T(8,128)(2,1)S(1)} %bitcast.16), channel_id=1, source_target_pairs={{0,64},{8,72},{16,80},{24,88},{32,96},{40,104},{48,112},{56,120},{... | collective-permute-start | bytes 786440 | tf_op jit(solution)/shard_map/ppermute | solution.py:269
  125.1 8.8 %collective-permute-start.7 = (bf16[128,1024]{1,0:T(8,128)(2,1)S(1)}, bf16[128,1024]{1,0:T(8,128)(2,1)S(1)}, u32[]{:S(2)}, u32[]{:S(2)}) collective-permute-start(bf16[128,1024]{1,0:T(8,128)(2,1)S(1)} %bitcast.17), channel_id=1, source_target_pairs={{0,192},{8,200},{16,208},{24,216},{32,224},{40,232},{48,240},{56,2... | collective-permute-start | bytes 786440 | tf_op jit(solution)/shard_map/ppermute | solution.py:269
  127.8 7.3 %collective-permute-start.8 = (bf16[128,1024]{1,0:T(8,128)(2,1)S(1)}, bf16[128,1024]{1,0:T(8,128)(2,1)S(1)}, u32[]{:S(2)}, u32[]{:S(2)}) collective-permute-start(bf16[128,1024]{1,0:T(8,128)(2,1)S(1)} %bitcast.18), channel_id=1, source_target_pairs={{0,128},{8,136},{16,144},{24,152},{32,160},{40,168},{48,176},{56,1... | collective-permute-start | bytes 786440 | tf_op jit(solution)/shard_map/ppermute | solution.py:269

commit v6 on v5

--- a/solution.py
+++ b/solution.py
@@ -301,11 +301,11 @@
 
     joined = across_z(join(own, parts, group, Z))
     heads = across_z(combine(joined, group)).reshape(quarter, width)
-    pieces = [heads] + [along_y(heads, step) for step in (1, 3, 2)]
+    pieces = [heads] + [along_y(heads, step) for step in (2, 1, 3)]
     scored = [
         jnp.dot(piece, out_weight, preferred_element_type=f32).astype(bf16) for piece in pieces
     ]
-    order = (0, 1, 3, 2)
+    order = (0, 2, 1, 3)
     whole = jnp.zeros((rows, out_weight.shape[1]), bf16)
     for step, piece in zip(order, scored):
         owner = (place // Z + Y - step) % Y

time: 154 us -> 154 us (level)
  Pallas kernels: 60.2 us -> 47.3 us
  starting transfers between devices: 26 us -> 38.6 us
    pallas_call x5, Pallas kernels: 57.5 us -> 44.7 us  [attend(): pl.pallas_call(lambda *refs: attend_kernel(lead, group, min(4, group), 51...]
    ppermute x9, starting transfers between devices: 17 us -> 29.5 us  [along_y(): return lax.ppermute(array, 'seq', pairs)]
  transfers between devices with their start and end apart: 10 -> 10, of which waited for: 5 -> 4; matrix products, arithmetic and copies ran while one was open for 1% -> 1% of each run, Pallas kernels for 38% -> 30%
where the time goes in v6:
time: 154 us; the launch traced here: 153 us
  blocking collectives  48.4 us (31%)
  Pallas kernels  47.3 us (31%)
  starting transfers between devices  38.6 us (25%)
  waiting for transfers between devices  12.9 us (8%)
  local copies, waits for them, and re-layouts  4.26 us (3%)
    pallas_call x5, Pallas kernels, attend(): pl.pallas_call(lambda *refs: attend_kernel(lead, group, min(4, group), 51...  44.7 us
    all_to_all x2, blocking collectives, across_z(): lax.all_to_all(array, 'seq', 0, 0, axis_index_groups=along_z, tiled=True)  30.9 us
    ppermute x9, starting transfers between devices, along_y(): return lax.ppermute(array, 'seq', pairs)  29.5 us
    all_to_all x1, blocking collectives, on_device(): scored = lax.all_to_all(scored, 'mp', 0, 0, tiled=True)  17.5 us
    all_to_all x1, starting transfers between devices, across_z(): lax.all_to_all(array, 'seq', 0, 0, axis_index_groups=along_z, tiled=True)  9.03 us
    ppermute x9, waiting for transfers between devices, along_y(): return lax.ppermute(array, 'seq', pairs)  6.74 us
    all_to_all x1, waiting for transfers between devices, across_z(): lax.all_to_all(array, 'seq', 0, 0, axis_index_groups=along_z, tiled=True)  6.13 us
    unnamed x14, local copies, waits for them, and re-layouts  3.48 us
  transfers between devices with their start and end apart: 10, of which 4 were waited for; matrix products, arithmetic and copies ran while one was open for 1% of the time, Pallas kernels for 30%

profile of v6, /device:TPU:1, one launch (start us, length us, event | category | flops | bytes accessed | tf_op | source)
XLA Modules:
  0.0 153.3 jit_solution(14375053207649038433)
XLA Ops:
  0.0 0.0 copy-start
  0.0 0.0 copy-start.1
  0.0 0.9 copy-done.3
  0.9 0.8 replicate.1
  1.7 9.0 %all-to-all-start = ((bf16[8,16,1024]{2,1,0:T(8,128)(2,1)}), bf16[8,16,1024]{2,1,0:T(8,128)(2,1)S(1)}, u32[]{:S(2)}, u32[]{:S(2)}) async-start(bf16[8,16,1024]{2,1,0:T(8,128)(2,1)} %replicate.1), calls=%async_computation | async-start | bytes 524288 | tf_op jit(solution)/shard_map/all_to_all | solution.py:265
  10.7 0.8 dynamic_slice.15
  11.4 1.2 copy-done.2
  12.7 0.7 copy-done.4
  13.3 0.7 copy-done.5
  14.0 0.8 prepare.1
  14.8 0.0 copy-done.6
  14.8 0.1 fusion.5
  14.9 6.1 %all-to-all-done = bf16[8,16,1024]{2,1,0:T(8,128)(2,1)S(1)} async-done(((bf16[8,16,1024]{2,1,0:T(8,128)(2,1)}), bf16[8,16,1024]{2,1,0:T(8,128)(2,1)S(1)}, u32[]{:S(2)}, u32[]{:S(2)}) %all-to-all-start) | async-done | bytes 262176 | tf_op jit(solution)/shard_map/all_to_all | solution.py:265
  21.1 2.7 %collective-permute-start.4 = (bf16[128,1024]{1,0:T(8,128)(2,1)S(1)}, bf16[128,1024]{1,0:T(8,128)(2,1)S(1)}, u32[]{:S(2)}, u32[]{:S(2)}) collective-permute-start(bf16[128,1024]{1,0:T(8,128)(2,1)S(1)} %bitcast.11), channel_id=1, source_target_pairs={{0,192},{8,200},{16,208},{24,216},{32,224},{40,232},{48,240},{56,2... | collective-permute-start | bytes 786440 | tf_op jit(solution)/shard_map/ppermute | solution.py:269
  23.8 0.0 copy-done.1
  23.8 2.7 %attend.5.refs_0_ = bf16[528,128]{1,0:T(8,128)(2,1)S(1)} custom-call(bf16[128,1024]{1,0:T(8,128)(2,1)S(1)} %bitcast.12, bf16[4096,128]{1,0:T(8,128)(2,1)S(1)} %copy-done.1, bf16[128,4096]{1,0:T(8,128)(2,1)S(1)} %get-tuple-element.33.refs_2_, bf16[16,128]{1,0:T(8,128)(2,1)S(1)} %get-tuple-element.34.refs_3_, bf16[128,16]{1,0:T(8,128)(2,1)S(1)} %get-tuple-element.35.refs_4_, ...), custom_call_target="tpu_custom_call" | custom-call | tf_op jit(solution)/shard_map/attend/pallas_call | solution.py:168
  26.5 6.9 %collective-permute-start.2 = (bf16[128,1024]{1,0:T(8,128)(2,1)S(1)}, bf16[128,1024]{1,0:T(8,128)(2,1)S(1)}, u32[]{:S(2)}, u32[]{:S(2)}) collective-permute-start(bf16[128,1024]{1,0:T(8,128)(2,1)S(1)} %bitcast.13), channel_id=1, source_target_pairs={{0,128},{8,136},{16,144},{24,152},{32,160},{40,168},{48,176},{56,1... | collective-permute-start | bytes 786440 | tf_op jit(solution)/shard_map/ppermute | solution.py:269
  33.3 0.7 collective-permute-start
  34.0 0.0 collective-permute-done.4.refs_0_
  34.0 4.5 %attend.9 = bf16[1056,128]{1,0:T(8,128)(2,1)S(1)} custom-call(bf16[128,1024]{1,0:T(8,128)(2,1)S(1)} %collective-permute-done.4.refs_0_, bf16[4096,128]{1,0:T(8,128)(2,1)S(1)} %copy-done.1, bf16[128,4096]{1,0:T(8,128)(2,1)S(1)} %get-tuple-element.33.refs_2_, bf16[16,128]{1,0:T(8,128)(2,1)S(1)} %get-tuple-element.34.refs_3_, ...), custom_call_target="tpu_custom_call" | custom-call | tf_op jit(solution)/shard_map/attend/pallas_call | solution.py:168
  38.6 13.1 %collective-permute-start.5 = (bf16[1056,128]{1,0:T(8,128)(2,1)S(1)}, bf16[1056,128]{1,0:T(8,128)(2,1)S(1)}, u32[]{:S(2)}, u32[]{:S(2)}) collective-permute-start(bf16[1056,128]{1,0:T(8,128)(2,1)S(1)} %attend.9), channel_id=1, source_target_pairs={{0,64},{8,72},{16,80},{24,88},{32,96},{40,104},{48,112},{56,120},{... | collective-permute-start | bytes 811016 | tf_op jit(solution)/shard_map/ppermute | solution.py:269
  51.7 0.0 collective-permute-done.2.refs_0_
  51.7 17.4 %attend.8 = bf16[1056,128]{1,0:T(8,128)(2,1)S(1)} custom-call(bf16[128,1024]{1,0:T(8,128)(2,1)S(1)} %collective-permute-done.2.refs_0_, bf16[4096,128]{1,0:T(8,128)(2,1)S(1)} %copy-done.1, bf16[128,4096]{1,0:T(8,128)(2,1)S(1)} %get-tuple-element.33.refs_2_, bf16[16,128]{1,0:T(8,128)(2,1)S(1)} %get-tuple-element.34.refs_3_, ...), custom_call_target="tpu_custom_call" | custom-call | tf_op jit(solution)/shard_map/attend/pallas_call | solution.py:168
  69.1 0.1 collective-permute-start.3
  69.2 0.0 collective-permute-done.refs_0_
  69.2 17.4 %attend.7 = bf16[1056,128]{1,0:T(8,128)(2,1)S(1)} custom-call(bf16[128,1024]{1,0:T(8,128)(2,1)S(1)} %collective-permute-done.refs_0_, bf16[4096,128]{1,0:T(8,128)(2,1)S(1)} %copy-done.1, bf16[128,4096]{1,0:T(8,128)(2,1)S(1)} %get-tuple-element.33.refs_2_, bf16[16,128]{1,0:T(8,128)(2,1)S(1)} %get-tuple-element.34.refs_3_, ...), custom_call_target="tpu_custom_call" | custom-call | tf_op jit(solution)/shard_map/attend/pallas_call | solution.py:168
  86.6 3.0 %collective-permute-start.1 = (bf16[1056,128]{1,0:T(8,128)(2,1)S(1)}, bf16[1056,128]{1,0:T(8,128)(2,1)S(1)}, u32[]{:S(2)}, u32[]{:S(2)}) collective-permute-start(bf16[1056,128]{1,0:T(8,128)(2,1)S(1)} %attend.7), channel_id=1, source_target_pairs={{0,192},{8,200},{16,208},{24,216},{32,224},{40,232},{48,240},{56,2... | collective-permute-start | bytes 811016 | tf_op jit(solution)/shard_map/ppermute | solution.py:269
  89.6 2.7 %attend.6.refs_1_ = bf16[528,128]{1,0:T(8,128)(2,1)S(1)} custom-call(bf16[128,1024]{1,0:T(8,128)(2,1)S(1)} %bitcast.15, bf16[4096,128]{1,0:T(8,128)(2,1)S(1)} %copy-done.1, bf16[128,4096]{1,0:T(8,128)(2,1)S(1)} %get-tuple-element.33.refs_2_, bf16[16,128]{1,0:T(8,128)(2,1)S(1)} %get-tuple-element.34.refs_3_, bf16[128,16]{1,0:T(8,128)(2,1)S(1)} %get-tuple-element.35.refs_4_, ...), custom_call_target="tpu_custom_call" | custom-call | tf_op jit(solution)/shard_map/attend/pallas_call | solution.py:168
  92.3 0.0 collective-permute-done.5.refs_4_
  92.3 0.0 collective-permute-done.3.refs_3_
  92.3 0.7 collective-permute-done.1.refs_2_
  93.0 0.8 join.1
  93.8 19.2 %all_to_all.20.refs_0_ = bf16[8,144,128]{2,1,0:T(8,128)(2,1)S(1)} all-to-all(bf16[8,144,128]{2,1,0:T(8,128)(2,1)S(1)} %join.1), channel_id=1, replica_groups={{0,8,16,24,32,40,48,56},{64,72,80,88,96,104,112,120},{128,136,144,152,1..., dimensions={0} | all-to-all | bytes 589824 | tf_op jit(solution)/shard_map/all_to_all | solution.py:265
  113.0 0.3 combine.1
  113.3 11.7 %all_to_all.21 = bf16[8,16,1024]{2,1,0:T(8,128)(2,1)S(1)} all-to-all(bf16[8,16,1024]{2,1,0:T(8,128)(2,1)S(1)} %combine.1), channel_id=1, replica_groups={{0,8,16,24,32,40,48,56},{64,72,80,88,96,104,112,120},{128,136,144,152,1..., dimensions={0} | all-to-all | bytes 524288 | tf_op jit(solution)/shard_map/all_to_all | solution.py:265
  125.1 0.3 collective-permute-start.6
  125.4 0.4 collective-permute-start.7
  125.8 2.2 %collective-permute-start.8 = (bf16[128,1024]{1,0:T(8,128)(2,1)S(1)}, bf16[128,1024]{1,0:T(8,128)(2,1)S(1)}, u32[]{:S(2)}, u32[]{:S(2)}) collective-permute-start(bf16[128,1024]{1,0:T(8,128)(2,1)S(1)} %bitcast.18), channel_id=1, source_target_pairs={{0,192},{8,200},{16,208},{24,216},{32,224},{40,232},{48,240},{56,2... | collective-permute-start | bytes 786440 | tf_op jit(solution)/shard_map/ppermute | solution.py:269
  128.1 0.0 copy-done
  128.1 0.2 fusion.3
  128.3 3.6 %collective-permute-done.6 = bf16[128,1024]{1,0:T(8,128)(2,1)S(1)} collective-permute-done((bf16[128,1024]{1,0:T(8,128)(2,1)S(1)}, bf16[128,1024]{1,0:T(8,128)(2,1)S(1)}, u32[]{:S(2)}, u32[]{:S(2)}) %collective-permute-start.6) | collective-permute-done | bytes 262176 | tf_op jit(solution)/shard_map/ppermute | solution.py:269
  131.9 0.2 fusion.2
  132.2 2.5 %collective-permute-done.7 = bf16[128,1024]{1,0:T(8,128)(2,1)S(1)} collective-permute-done((bf16[128,1024]{1,0:T(8,128)(2,1)S(1)}, bf16[128,1024]{1,0:T(8,128)(2,1)S(1)}, u32[]{:S(2)}, u32[]{:S(2)}) %collective-permute-start.7) | collective-permute-done | bytes 262176 | tf_op jit(solution)/shard_map/ppermute | solution.py:269
  134.6 0.2 fusion.1
  134.9 0.0 collective-permute-done.8
  134.9 0.2 fusion
  135.1 17.5 %all_to_all.22 = bf16[8,64,256]{2,1,0:T(8,128)(2,1)S(1)} all-to-all(bf16[8,64,256]{2,1,0:T(8,128)(2,1)S(1)} %bitcast.20), channel_id=1, replica_groups=mesh['seq'=32,'mp'=8] {'mp'}, dimensions={0} | all-to-all | bytes 524288 | tf_op jit(solution)/shard_map/all_to_all | solution.py:314
  152.6 0.7 reduce_sum.12
  (8 shorter events, 0.0 us)
Async XLA Ops:
  0.0 128.1 %copy-start = (bf16[1024,256]{1,0:T(8,128)(2,1)S(1)}, bf16[1024,256]{1,0:T(8,128)(2,1)}, u32[]{:S(2)}) copy-start(bf16[1024,256]{1,0:T(8,128)(2,1)} %param.13) | copy-start | bytes 1572868
  0.0 23.8 %copy-start.1 = (bf16[4096,128]{1,0:T(8,128)(2,1)S(1)}, bf16[4096,128]{1,0:T(8,128)(2,1)}, u32[]{:S(2)}) copy-start(bf16[4096,128]{1,0:T(8,128)(2,1)} %refs_1_.9) | copy-start | bytes 3145732
  0.0 0.9 copy-start.3
  1.7 19.4 %all-to-all-start = ((bf16[8,16,1024]{2,1,0:T(8,128)(2,1)}), bf16[8,16,1024]{2,1,0:T(8,128)(2,1)S(1)}, u32[]{:S(2)}, u32[]{:S(2)}) async-start(bf16[8,16,1024]{2,1,0:T(8,128)(2,1)} %replicate.1), calls=%async_computation | async-start | bytes 524288 | tf_op jit(solution)/shard_map/all_to_all | solution.py:265
  11.4 1.2 copy-start.2
  12.7 0.7 copy-start.4
  13.3 0.7 copy-start.5
  14.0 0.8 copy-start.6
  21.1 13.0 %collective-permute-start.4 = (bf16[128,1024]{1,0:T(8,128)(2,1)S(1)}, bf16[128,1024]{1,0:T(8,128)(2,1)S(1)}, u32[]{:S(2)}, u32[]{:S(2)}) collective-permute-start(bf16[128,1024]{1,0:T(8,128)(2,1)S(1)} %bitcast.11), channel_id=1, source_target_pairs={{0,192},{8,200},{16,208},{24,216},{32,224},{40,232},{48,240},{56,2... | collective-permute-start | bytes 786440 | tf_op jit(solution)/shard_map/ppermute | solution.py:269
  26.5 25.2 %collective-permute-start.2 = (bf16[128,1024]{1,0:T(8,128)(2,1)S(1)}, bf16[128,1024]{1,0:T(8,128)(2,1)S(1)}, u32[]{:S(2)}, u32[]{:S(2)}) collective-permute-start(bf16[128,1024]{1,0:T(8,128)(2,1)S(1)} %bitcast.13), channel_id=1, source_target_pairs={{0,128},{8,136},{16,144},{24,152},{32,160},{40,168},{48,176},{56,1... | collective-permute-start | bytes 786440 | tf_op jit(solution)/shard_map/ppermute | solution.py:269
  33.3 35.8 %collective-permute-start = (bf16[128,1024]{1,0:T(8,128)(2,1)S(1)}, bf16[128,1024]{1,0:T(8,128)(2,1)S(1)}, u32[]{:S(2)}, u32[]{:S(2)}) collective-permute-start(bf16[128,1024]{1,0:T(8,128)(2,1)S(1)} %bitcast.14), channel_id=1, source_target_pairs={{0,64},{8,72},{16,80},{24,88},{32,96},{40,104},{48,112},{56,120},{... | collective-permute-start | bytes 786440 | tf_op jit(solution)/shard_map/ppermute | solution.py:269
  38.6 53.8 %collective-permute-start.5 = (bf16[1056,128]{1,0:T(8,128)(2,1)S(1)}, bf16[1056,128]{1,0:T(8,128)(2,1)S(1)}, u32[]{:S(2)}, u32[]{:S(2)}) collective-permute-start(bf16[1056,128]{1,0:T(8,128)(2,1)S(1)} %attend.9), channel_id=1, source_target_pairs={{0,64},{8,72},{16,80},{24,88},{32,96},{40,104},{48,112},{56,120},{... | collective-permute-start | bytes 811016 | tf_op jit(solution)/shard_map/ppermute | solution.py:269
  69.1 23.2 %collective-permute-start.3 = (bf16[1056,128]{1,0:T(8,128)(2,1)S(1)}, bf16[1056,128]{1,0:T(8,128)(2,1)S(1)}, u32[]{:S(2)}, u32[]{:S(2)}) collective-permute-start(bf16[1056,128]{1,0:T(8,128)(2,1)S(1)} %attend.8), channel_id=1, source_target_pairs={{0,128},{8,136},{16,144},{24,152},{32,160},{40,168},{48,176},{56,1... | collective-permute-start | bytes 811016 | tf_op jit(solution)/shard_map/ppermute | solution.py:269
  86.6 6.4 %collective-permute-start.1 = (bf16[1056,128]{1,0:T(8,128)(2,1)S(1)}, bf16[1056,128]{1,0:T(8,128)(2,1)S(1)}, u32[]{:S(2)}, u32[]{:S(2)}) collective-permute-start(bf16[1056,128]{1,0:T(8,128)(2,1)S(1)} %attend.7), channel_id=1, source_target_pairs={{0,192},{8,200},{16,208},{24,216},{32,224},{40,232},{48,240},{56,2... | collective-permute-start | bytes 811016 | tf_op jit(solution)/shard_map/ppermute | solution.py:269
  125.1 6.8 %collective-permute-start.6 = (bf16[128,1024]{1,0:T(8,128)(2,1)S(1)}, bf16[128,1024]{1,0:T(8,128)(2,1)S(1)}, u32[]{:S(2)}, u32[]{:S(2)}) collective-permute-start(bf16[128,1024]{1,0:T(8,128)(2,1)S(1)} %bitcast.16), channel_id=1, source_target_pairs={{0,128},{8,136},{16,144},{24,152},{32,160},{40,168},{48,176},{56,1... | collective-permute-start | bytes 786440 | tf_op jit(solution)/shard_map/ppermute | solution.py:269
  125.4 9.2 %collective-permute-start.7 = (bf16[128,1024]{1,0:T(8,128)(2,1)S(1)}, bf16[128,1024]{1,0:T(8,128)(2,1)S(1)}, u32[]{:S(2)}, u32[]{:S(2)}) collective-permute-start(bf16[128,1024]{1,0:T(8,128)(2,1)S(1)} %bitcast.17), channel_id=1, source_target_pairs={{0,64},{8,72},{16,80},{24,88},{32,96},{40,104},{48,112},{56,120},{... | collective-permute-start | bytes 786440 | tf_op jit(solution)/shard_map/ppermute | solution.py:269
  125.8 9.0 %collective-permute-start.8 = (bf16[128,1024]{1,0:T(8,128)(2,1)S(1)}, bf16[128,1024]{1,0:T(8,128)(2,1)S(1)}, u32[]{:S(2)}, u32[]{:S(2)}) collective-permute-start(bf16[128,1024]{1,0:T(8,128)(2,1)S(1)} %bitcast.18), channel_id=1, source_target_pairs={{0,192},{8,200},{16,208},{24,216},{32,224},{40,232},{48,240},{56,2... | collective-permute-start | bytes 786440 | tf_op jit(solution)/shard_map/ppermute | solution.py:269
